TPU v7x, 32 devices: a whole 2x2x4 slice. The times are simulated.
32 devices in a mesh: groups: 2 (over y), ctx: 4 (over z), exp: 2 (over x), tp: 2 (over core).
Axes of the slice: x: 2, y: 2, z: 4, core: 2. Of those that a mesh axis runs over, the one named last changes fastest.
Arguments:
- resid: bfloat16 [512, 4096], P(('groups', 'ctx')), parts along dimension 0, may hold values from -40 to 40
- conv_out: bfloat16 [512, 4096], P(('groups', 'ctx'), ('exp', 'tp')), parts along dimension 0, may hold values from -6 to 6
- gate_z: bfloat16 [512, 4096], P(('groups', 'ctx'), ('exp', 'tp')), parts along dimension 0, may hold values from -6 to 6
- dt_raw: float32 [512, 4096], P(('groups', 'ctx'), ('exp', 'tp')), parts along dimension 0, may hold values from -14 to 2
- b_proj: float32 [512, 16], P(('groups', 'ctx')), parts along dimension 0, may hold values from -6 to 6
- c_proj: float32 [512, 16], P(('groups', 'ctx')), parts along dimension 0, may hold values from -6 to 6
- a_log: float32 [16, 4096], P(None, ('exp', 'tp')), may hold values from -0.7 to 0.7
- d_skip: float32 [4096], P(('exp', 'tp')), may hold values from 0.5 to 1.5
- out_weight: bfloat16 [4096, 4096], P(('exp', 'tp'), 'ctx'), may hold values from -0.09375 to 0.09375
- norm_gain: float32 [4096], replicated, may hold values from 0.1 to 1.9
- route_ids: int32 [512, 2], P(('groups', 'ctx')), parts along dimension 0, may hold values from 0 to 3, as said below
- route_weight: float32 [512, 2], P(('groups', 'ctx')), parts along dimension 0, may hold values from 0.2 to 1
- w_gate: bfloat16 [4096, 32768], P('tp', ('ctx', 'exp')), may hold values from -0.09375 to 0.09375
- w_up: bfloat16 [4096, 32768], P('tp', ('ctx', 'exp')), may hold values from -0.09375 to 0.09375
- w_down: bfloat16 [32768, 4096], P(('ctx', 'exp'), 'tp'), may hold values from -0.0625 to 0.0625
Outputs:
- layer_out: bfloat16 [512, 4096], P(('groups', 'ctx'), ('tp', 'exp')), parts along dimension 0
There are 2 independent parts, one for each index of `groups`. A program takes and returns all parts, laid end to end along the dimension named above; an argument that names none is the same for every part. Nothing has to cross between parts.
Inputs may be any that keep to these rules, and one draw needn't show every extreme that they name: `route_ids`: each row names two different experts. Among the 64 rows of one block (rows b * 64 to (b + 1) * 64 - 1), no expert is named by more than 40 rows, and one expert, the same in every block of a part, is named by exactly 40 rows of every block.
All inputs are finite; a program needn't handle non-finite values.
Results may differ from a plain program's by a relative error of at most 0.01.
Values may be sent and summed in bfloat16 or wider, within the bound.
No kernel may reach another device: no remote copies, remote signals or barrier semaphores. Data moves between devices by JAX's collectives and lax.ppermute only.
A program may use at most 128 MiB of HBM per device.

v0:
```python
import jax
import jax.numpy as jnp
from jax import lax
from jax.sharding import PartitionSpec as P

EXPERTS = 4
CAP = 40


def shifted(x, axis, by):
    peers = lax.axis_size(axis)
    pairs = [(i, i + by) for i in range(peers) if 0 <= i + by < peers]
    return lax.ppermute(x, axis, pairs)


def body(
    resid,
    conv_out,
    gate_z,
    dt_raw,
    b_proj,
    c_proj,
    a_log,
    d_skip,
    out_weight,
    norm_gain,
    route_ids,
    route_weight,
    w_gate,
    w_up,
    w_down,
):
    tokens = resid.shape[0]
    model_width = resid.shape[1]
    ctx_count = lax.axis_size("ctx")
    exp_count = lax.axis_size("exp")
    tp_count = lax.axis_size("tp")
    half_width = model_width // tp_count
    piece_width = half_width // exp_count
    tp_index = lax.axis_index("tp")
    exp_index = lax.axis_index("exp")
    stride_amount = jax.nn.softplus(dt_raw)
    rate = -jnp.exp(a_log)
    inputs = conv_out.astype(jnp.float32)

    def advance(carry_state, column):
        step_now, b_now, c_now, in_now = column
        carry_state = (
            jnp.exp(step_now[None, :] * rate) * carry_state
            + step_now[None, :] * b_now[:, None] * in_now[None, :]
        )
        return (carry_state, jnp.sum(c_now[:, None] * carry_state, axis=0))

    last_state, scanned_local = lax.scan(
        advance,
        jnp.zeros(rate.shape, jnp.float32),
        (stride_amount, b_proj, c_proj, inputs),
        unroll=8,
    )
    cum_step = jnp.cumsum(stride_amount, axis=0)
    last_decay = jnp.exp(cum_step[-1][None, :] * rate)

    def relay_turn(turn_index, carry_state):
        return shifted(last_decay * carry_state + last_state, "ctx", 1)

    entering = lax.fori_loop(0, ctx_count - 1, relay_turn, jnp.zeros_like(last_state))
    carried = jnp.exp(cum_step[:, None, :] * rate[None, :, :])
    scanned = scanned_local + jnp.sum(c_proj[:, :, None] * carried * entering[None, :, :], axis=1)
    gated_out = (
        (scanned + d_skip[None, :] * inputs) * jax.nn.silu(gate_z.astype(jnp.float32))
    ).astype(jnp.bfloat16)
    partial_value = jnp.dot(
        gated_out,
        lax.all_gather(out_weight, "ctx", axis=1, tiled=True),
        preferred_element_type=jnp.float32,
    )
    mamba_out = lax.psum(partial_value, ("exp", "tp"))
    stream = (resid.astype(jnp.float32) + mamba_out).astype(jnp.bfloat16)
    stream_wide = stream.astype(jnp.float32)
    square_mean = jnp.mean(stream_wide * stream_wide, axis=1, keepdims=True)
    normed = (stream_wide * lax.rsqrt(square_mean + 1e-06) * norm_gain[None, :]).astype(
        jnp.bfloat16
    )
    half_feats = lax.dynamic_slice_in_dim(normed, tp_index * half_width, half_width, 1)
    slot_total = EXPERTS * CAP
    flat_ids = route_ids.reshape(-1)
    pair_count = flat_ids.shape[0]
    onehot = (flat_ids[:, None] == jnp.arange(EXPERTS, dtype=jnp.int32)[None, :]).astype(
        jnp.float32
    )
    pair_index = jnp.arange(pair_count, dtype=jnp.int32)
    earlier_mask = (pair_index[:, None] > pair_index[None, :]).astype(jnp.float32)
    before = jnp.dot(earlier_mask, onehot, precision=lax.Precision.HIGHEST)
    position = jnp.sum(before * onehot, axis=1).astype(jnp.int32)
    target = (flat_ids * CAP + position).reshape(tokens, 2)
    matches = jnp.arange(slot_total, dtype=jnp.int32)[None, :, None] == target[:, None, :]
    placement = jnp.any(matches, axis=2).astype(jnp.bfloat16)
    combine_weights = jnp.sum(jnp.where(matches, route_weight[:, None, :], 0.0), axis=2)
    members = ctx_count // EXPERTS
    outgoing = lax.dot_general(
        placement, half_feats, (((0,), (0,)), ((), ())), preferred_element_type=jnp.float32
    )
    outgoing = jnp.repeat(
        outgoing.astype(jnp.bfloat16).reshape(EXPERTS, CAP, half_width), members, axis=0
    )
    arrived = lax.all_to_all(outgoing, "ctx", split_axis=0, concat_axis=0, tiled=True)
    sources = arrived.shape[0]
    item_count = arrived.shape[1]
    flat_rows = arrived.reshape(sources * item_count, half_width)
    gate_value = jnp.dot(flat_rows, w_gate, preferred_element_type=jnp.float32)
    up_value = jnp.dot(flat_rows, w_up, preferred_element_type=jnp.float32)
    gate_value, up_value = (
        lax.psum(gate_value.astype(jnp.bfloat16), "tp").astype(jnp.float32),
        lax.psum(up_value.astype(jnp.bfloat16), "tp").astype(jnp.float32),
    )
    hidden = (jax.nn.silu(gate_value) * up_value).astype(jnp.bfloat16)
    answer = jnp.dot(hidden, w_down, preferred_element_type=jnp.float32).astype(jnp.bfloat16)
    answer = answer.reshape(sources, item_count, half_width)
    returned = lax.all_to_all(answer, "ctx", split_axis=0, concat_axis=0, tiled=True)
    reply_width = returned.shape[2]
    merged = jnp.sum(
        returned.astype(jnp.float32).reshape(EXPERTS, members, CAP, reply_width), axis=1
    )
    merged = merged.reshape(slot_total, reply_width)
    moe_rows = jnp.dot(combine_weights, merged, precision=lax.Precision.HIGHEST)
    moe_piece = lax.psum_scatter(
        moe_rows.astype(jnp.bfloat16), "exp", scatter_dimension=1, tiled=True
    ).astype(jnp.float32)
    own_stream = lax.dynamic_slice_in_dim(
        stream_wide, tp_index * half_width + exp_index * piece_width, piece_width, 1
    )
    return (own_stream + moe_piece).astype(jnp.bfloat16)


def solution(mesh):
    in_specs = (
        P(("groups", "ctx"), None),
        P(("groups", "ctx"), ("exp", "tp")),
        P(("groups", "ctx"), ("exp", "tp")),
        P(("groups", "ctx"), ("exp", "tp")),
        P(("groups", "ctx"), None),
        P(("groups", "ctx"), None),
        P(None, ("exp", "tp")),
        P(("exp", "tp")),
        P(("exp", "tp"), "ctx"),
        P(),
        P(("groups", "ctx"), None),
        P(("groups", "ctx"), None),
        P("tp", ("ctx", "exp")),
        P("tp", ("ctx", "exp")),
        P(("ctx", "exp"), "tp"),
    )
    out_specs = P(("groups", "ctx"), ("tp", "exp"))
    return jax.shard_map(body, mesh=mesh, in_specs=in_specs, out_specs=out_specs, check_vma=False)
```

profile of v0, /device:TPU:0, one launch (start us, length us, event | category | flops | bytes accessed | tf_op | source)
XLA Modules:
  0.0 321.7 jit_solution(10836095283426707197)
XLA Ops:
  6.6 0.7 all-gather.2.cloned.1.call-update
  7.3 1.1 fusion.30
  8.4 0.2 reduce_window_sum.11
  8.9 5.6 %while.24 = (s32[]{:T(128)}, f32[16,1024]{1,0:T(8,128)S(1)}, f32[8,8,1024]{2,1,0:T(8,128)S(1)}, f32[8,8,1024]{2,1,0:T(8,128)S(1)}, f32[16,1024]{1,0:T(8,128)S(1)...) while((s32[]{:T(128)}, f32[16,1024]{1,0:T(8,128)S(1)}, ...), condition=%wide.region_9.10_spmd.clone, body=%wide.region_0.9_spmd.clone.sunk | while | flops 1269770 | bytes 1316388 | solution.py:54
  9.1 0.2 multiply_reduce_fusion.13
  9.4 0.2 multiply_reduce_fusion.14
  9.8 0.2 multiply_reduce_fusion.13
  10.1 0.2 multiply_reduce_fusion.14
  10.5 0.2 multiply_reduce_fusion.13
  10.8 0.2 multiply_reduce_fusion.14
  11.2 0.2 multiply_reduce_fusion.13
  11.5 0.2 multiply_reduce_fusion.14
  11.9 0.2 multiply_reduce_fusion.13
  12.2 0.2 multiply_reduce_fusion.14
  12.6 0.2 multiply_reduce_fusion.13
  12.9 0.2 multiply_reduce_fusion.14
  13.3 0.2 multiply_reduce_fusion.13
  13.4 0.1 multiply_reduce_fusion.15
  13.6 0.2 multiply_reduce_fusion.14
  14.0 0.2 multiply_reduce_fusion.13
  14.3 0.2 multiply_reduce_fusion.14
  14.6 22.7 %while.23 = (s32[]{:T(128)}, f32[16,1024]{1,0:T(8,128)S(1)}, f32[16,1024]{1,0:T(8,128)S(1)}, f32[16,1024]{1,0:T(8,128)S(1)}, s32[]{:T(128)}) while((s32[]{:T(128)}, f32[16,1024]{1,0:T(8,128)S(1)}, f32[16,1024]{1,0:T(8,128)S(1)}, f32[16,1024]{1,0:T(8,128)S(1)}, s32[]{:T(128)}) %tuple.101), condition=%wide.region_12.13_spmd, body=%wide.region_11.12_spmd.sunk | while | flops 32770 | bytes 524389 | solution.py:66
  14.6 4.9 %collective-permute-start = (f32[16,1024]{1,0:T(8,128)S(1)}, f32[16,1024]{1,0:T(8,128)S(1)}, u32[]{:S(2)}, u32[]{:S(2)}) collective-permute-start(f32[16,1024]{1,0:T(8,128)S(1)} %multiply_add_fusion.14), channel_id=1, source_target_pairs={{0,4},{4,8},{8,12},{1,5},{5,9},{9,13},{2,6},{6,10},{10,14},{3,7},{... | collective-permute-start | bytes 196616 | tf_op jit(solution)/shard_map/while/body/eval_jaxpr/ppermute | solution.py:13
  19.5 1.9 collective-permute-done
  21.4 4.3 %collective-permute-start = (f32[16,1024]{1,0:T(8,128)S(1)}, f32[16,1024]{1,0:T(8,128)S(1)}, u32[]{:S(2)}, u32[]{:S(2)}) collective-permute-start(f32[16,1024]{1,0:T(8,128)S(1)} %multiply_add_fusion.14), channel_id=1, source_target_pairs={{0,4},{4,8},{8,12},{1,5},{5,9},{9,13},{2,6},{6,10},{10,14},{3,7},{... | collective-permute-start | bytes 196616 | tf_op jit(solution)/shard_map/while/body/eval_jaxpr/ppermute | solution.py:13
  25.7 3.1 collective-permute-done
  28.9 5.1 %collective-permute-start = (f32[16,1024]{1,0:T(8,128)S(1)}, f32[16,1024]{1,0:T(8,128)S(1)}, u32[]{:S(2)}, u32[]{:S(2)}) collective-permute-start(f32[16,1024]{1,0:T(8,128)S(1)} %multiply_add_fusion.14), channel_id=1, source_target_pairs={{0,4},{4,8},{8,12},{1,5},{5,9},{9,13},{2,6},{6,10},{10,14},{3,7},{... | collective-permute-start | bytes 196616 | tf_op jit(solution)/shard_map/while/body/eval_jaxpr/ppermute | solution.py:13
  33.9 3.3 %collective-permute-done = f32[16,1024]{1,0:T(8,128)S(1)} collective-permute-done((f32[16,1024]{1,0:T(8,128)S(1)}, f32[16,1024]{1,0:T(8,128)S(1)}, u32[]{:S(2)}, u32[]{:S(2)}) %collective-permute-start) | collective-permute-done | bytes 65568 | tf_op jit(solution)/shard_map/while/body/eval_jaxpr/ppermute | solution.py:13
  37.2 1.5 multiply_reduce_fusion.8
  38.7 122.6 %all-gather.2.cloned.1.call-done = bf16[1024,4096]{1,0:T(8,128)(2,1)} async-done(((bf16[1024,1024]{1,0:T(8,128)(2,1)}), bf16[1024,4096]{1,0:T(8,128)(2,1)}) %all-gather.2.cloned.1.call-update) | async-done | bytes 8388624 | tf_op jit(solution)/shard_map/all_gather | solution.py:74
  161.3 6.1 %fusion.21 = f32[64,4096]{1,0:T(8,128)} fusion(bf16[1024,4096]{1,0:T(8,128)(2,1)} %all-gather.2.cloned.1.call-done, bf16[64,1024]{1,0:T(8,128)(2,1)S(1)} %copy-done, bf16[64,1024]{1,0:T(8,128)(2,1)S(1)} %copy-done.2, f32[64,1024]{1,0:T(8,128)S(1)} %multiply_reduce_fusion.8, f32[8,8,1024]{2,1,0:T(8,128)S(1)} %get-tuple-element.70, f32[1024]{0:T(1024)S(1)} %copy-done.3), kind=kOutput, calls=%fused_computation.90 | convolution fusion | flops 537591808 | bytes 10227712 | tf_op jit(solution)/shard_map/dot_general | solution.py:72
  167.6 0.1 eq.29
  167.8 0.1 fusion.8
  167.9 0.1 convert_element_type.70
  168.2 0.1 fusion.23
  168.3 36.2 %all-reduce.4.cloned.1.call-done = f32[64,4096]{1,0:T(8,128)} async-done(((f32[64,4096]{1,0:T(8,128)}), f32[64,4096]{1,0:T(8,128)}) %all-reduce.4.cloned.1.call-update) | async-done | bytes 1048592 | tf_op jit(solution)/shard_map/psum | solution.py:77
  204.5 1.5 multiply_reduce_fusion.9
  206.0 0.4 convolution_convert_fusion.3
  206.4 21.2 %all_to_all.10 = bf16[4,40,2048]{2,1,0:T(8,128)(2,1)S(1)} all-to-all(bf16[4,40,2048]{2,1,0:T(8,128)(2,1)S(1)} %bitcast.138), channel_id=1, replica_groups=mesh['groups'=2,'ctx'=4,'exp'=2,'tp'=2] {'ctx'}, dimensions={0} | all-to-all | bytes 1310720 | tf_op jit(solution)/shard_map/all_to_all | solution.py:106
  227.6 9.8 %convolution_convert_fusion = bf16[160,4096]{1,0:T(8,128)(2,1)} fusion(bf16[160,2048]{1,0:T(8,128)(2,1)S(1)} %bitcast.155, bf16[2048,4096]{1,0:T(8,128)(2,1)} %param.32), kind=kOutput, calls=%fused_computation.53 | convolution fusion | flops 2685009920 | bytes 18743296 | tf_op jit(solution)/shard_map/dot_general | solution.py:111
  237.4 9.8 %convolution_convert_fusion.1 = bf16[160,4096]{1,0:T(8,128)(2,1)} fusion(bf16[160,2048]{1,0:T(8,128)(2,1)S(1)} %bitcast.156, bf16[2048,4096]{1,0:T(8,128)(2,1)} %param.31), kind=kOutput, calls=%fused_computation.54 | convolution fusion | flops 2685009920 | bytes 18743296 | tf_op jit(solution)/shard_map/dot_general | solution.py:110
  247.2 21.2 %all-reduce.6.cloned.1.call-done = (bf16[160,4096]{1,0:T(8,128)(2,1)}, bf16[160,4096]{1,0:T(8,128)(2,1)}) async-done(((bf16[160,4096]{1,0:T(8,128)(2,1)}, bf16[160,4096]{1,0:T(8,128)(2,1)}), (bf16[160,4096]{1,0:T(8,128)(2,1)}, bf16[160,4096]{1,0:T(8,128)(2,1)})) %all-reduce.6.cloned.1.call-update) | async-done | bytes 2621456 | tf_op jit(solution)/shard_map/psum | solution.py:114
  268.4 10.6 %convolution_convert_fusion.2 = bf16[160,2048]{1,0:T(8,128)(2,1)} fusion(bf16[4096,2048]{1,0:T(8,128)(2,1)} %param.33, bf16[160,4096]{1,0:T(8,128)(2,1)} %get-tuple-element.131, bf16[160,4096]{1,0:T(8,128)(2,1)} %get-tuple-element.132), kind=kOutput, calls=%fused_computation.63 | convolution fusion | flops 2689925120 | bytes 20054016 | tf_op jit(solution)/shard_map/dot_general | solution.py:117
  279.0 4.9 %all-to-all-start.1 = ((bf16[4,40,2048]{2,1,0:T(8,128)(2,1)}), bf16[4,40,2048]{2,1,0:T(8,128)(2,1)S(1)}, u32[]{:S(2)}, u32[]{:S(2)}) async-start(bf16[4,40,2048]{2,1,0:T(8,128)(2,1)} %bitcast.8), calls=%async_computation.1 | async-start | bytes 1310720 | tf_op jit(solution)/shard_map/all_to_all | solution.py:119
  284.0 17.6 %all-to-all-done.1 = bf16[4,40,2048]{2,1,0:T(8,128)(2,1)S(1)} async-done(((bf16[4,40,2048]{2,1,0:T(8,128)(2,1)}), bf16[4,40,2048]{2,1,0:T(8,128)(2,1)S(1)}, u32[]{:S(2)}, u32[]{:S(2)}) %all-to-all-start.1) | async-done | bytes 655392 | tf_op jit(solution)/shard_map/all_to_all | solution.py:119
  301.6 1.1 convolution_convert_fusion.4
  302.8 10.9 %reduce-scatter.2.cloned.1.call-done = bf16[64,1024]{1,0:T(8,128)(2,1)} async-done(((bf16[64,2048]{1,0:T(8,128)(2,1)}), bf16[64,1024]{1,0:T(8,128)(2,1)}) %reduce-scatter.2.cloned.1.call-update) | async-done | bytes 131088 | tf_op jit(solution)/shard_map/reduce_scatter | solution.py:126
  313.6 1.6 add_convert_fusion.1
  (107 shorter events, 2.9 us)
Async XLA Ops:
  6.5 2.2 copy-start.5
  6.5 2.2 copy-start.6
  6.5 2.3 copy-start.4
  6.5 2.4 copy-start
  6.5 154.8 %all-gather.2.cloned.1.call-start = ((), (), s32[]{:S(2)}) async-start(), calls=%async_computation.3 | async-start | bytes 10485760 | tf_op jit(solution)/shard_map/all_gather | solution.py:74
  7.3 197.2 %all-reduce.4.cloned.1.call-start = ((), (), s32[]{:S(2)}) async-start(), calls=%async_computation.4 | async-start | bytes 2097152 | tf_op jit(solution)/shard_map/psum | solution.py:77
  14.5 146.8 %copy-start.2 = (bf16[64,1024]{1,0:T(8,128)(2,1)S(1)}, bf16[64,1024]{1,0:T(8,128)(2,1)}, u32[]{:S(2)}) copy-start(bf16[64,1024]{1,0:T(8,128)(2,1)} %param.21) | copy-start | bytes 393220
  14.5 146.8 %copy-start.3 = (f32[1024]{0:T(1024)S(1)}, f32[1024]{0:T(1024)}, u32[]{:S(2)}) copy-start(f32[1024]{0:T(1024)} %param.26) | copy-start | bytes 12292
  14.6 6.8 %collective-permute-start = (f32[16,1024]{1,0:T(8,128)S(1)}, f32[16,1024]{1,0:T(8,128)S(1)}, u32[]{:S(2)}, u32[]{:S(2)}) collective-permute-start(f32[16,1024]{1,0:T(8,128)S(1)} %multiply_add_fusion.14), channel_id=1, source_target_pairs={{0,4},{4,8},{8,12},{1,5},{5,9},{9,13},{2,6},{6,10},{10,14},{3,7},{... | collective-permute-start | bytes 196616 | tf_op jit(solution)/shard_map/while/body/eval_jaxpr/ppermute | solution.py:13
  21.4 7.4 %collective-permute-start = (f32[16,1024]{1,0:T(8,128)S(1)}, f32[16,1024]{1,0:T(8,128)S(1)}, u32[]{:S(2)}, u32[]{:S(2)}) collective-permute-start(f32[16,1024]{1,0:T(8,128)S(1)} %multiply_add_fusion.14), channel_id=1, source_target_pairs={{0,4},{4,8},{8,12},{1,5},{5,9},{9,13},{2,6},{6,10},{10,14},{3,7},{... | collective-permute-start | bytes 196616 | tf_op jit(solution)/shard_map/while/body/eval_jaxpr/ppermute | solution.py:13
  28.9 8.4 %collective-permute-start = (f32[16,1024]{1,0:T(8,128)S(1)}, f32[16,1024]{1,0:T(8,128)S(1)}, u32[]{:S(2)}, u32[]{:S(2)}) collective-permute-start(f32[16,1024]{1,0:T(8,128)S(1)} %multiply_add_fusion.14), channel_id=1, source_target_pairs={{0,4},{4,8},{8,12},{1,5},{5,9},{9,13},{2,6},{6,10},{10,14},{3,7},{... | collective-permute-start | bytes 196616 | tf_op jit(solution)/shard_map/while/body/eval_jaxpr/ppermute | solution.py:13
  161.3 6.2 %copy-start.7 = (s32[64,2]{0,1:T(2,128)S(1)}, s32[64,2]{0,1:T(2,128)}, u32[]{:S(2)}) copy-start(s32[64,2]{0,1:T(2,128)} %param.29) | copy-start | bytes 1540
  161.3 43.2 %copy-start.1 = (bf16[64,4096]{1,0:T(8,128)(2,1)S(1)}, bf16[64,4096]{1,0:T(8,128)(2,1)}, u32[]{:S(2)}) copy-start(bf16[64,4096]{1,0:T(8,128)(2,1)} %param.19) | copy-start | bytes 1572868
  167.5 100.9 %all-reduce.6.cloned.1.call-start = ((), (), s32[]{:S(2)}) async-start(), calls=%async_computation.6 | async-start | bytes 5242880 | tf_op jit(solution)/shard_map/psum | solution.py:114
  168.2 37.8 %dynamic-slice-start = ((f32[4096]{0:T(1024)}, s32[]{:T(128)}), f32[2048]{0:T(1024)S(1)}, s32[]{:S(2)}) async-start(f32[4096]{0:T(1024)} %param.28, s32[]{:T(128)} %select_n.17), calls=%async_computation.7 | async-start | bytes 16896 | tf_op jit(solution)/shard_map/dynamic_slice | solution.py:84
  268.4 15.5 %copy-start.8 = (f32[64,2]{0,1:T(2,128)S(1)}, f32[64,2]{0,1:T(2,128)}, u32[]{:S(2)}) copy-start(f32[64,2]{0,1:T(2,128)} %param.30) | copy-start | bytes 1540
  279.0 22.6 %all-to-all-start.1 = ((bf16[4,40,2048]{2,1,0:T(8,128)(2,1)}), bf16[4,40,2048]{2,1,0:T(8,128)(2,1)S(1)}, u32[]{:S(2)}, u32[]{:S(2)}) async-start(bf16[4,40,2048]{2,1,0:T(8,128)(2,1)} %bitcast.8), calls=%async_computation.1 | async-start | bytes 1310720 | tf_op jit(solution)/shard_map/all_to_all | solution.py:119
  283.9 29.7 %reduce-scatter.2.cloned.1.call-start = ((), (), s32[]{:S(2)}) async-start(), calls=%async_computation.5 | async-start | bytes 393216 | tf_op jit(solution)/shard_map/reduce_scatter | solution.py:126
Sparse Core Ops, SparseCore 0:
  8.9 152.3 all-gather.1
  167.6 36.8 all-reduce.3
  247.3 21.0 all-reduce.5
  302.9 10.6 reduce-scatter.1
where the time goes:
time: 322 us
  waiting for transfers between devices  218 us (68%)
  matrix products  37.9 us (12%)
  blocking collectives  21.2 us (7%)
  starting transfers between devices  19.2 us (6%)
  between operations  13.3 us (4%)
  other arithmetic  9.74 us (3%)
    all_gather x1, waiting for transfers between devices, body(): lax.all_gather(out_weight, 'ctx', axis=1, tiled=True)  123 us
    psum x1, waiting for transfers between devices, body(): mamba_out = lax.psum(partial_value, ('exp', 'tp'))  36.2 us
    all_to_all x1, blocking collectives, body(): lax.all_to_all(outgoing, 'ctx', split_axis=0, concat_axis=0, tiled=True)  21.2 us
    psum x1, waiting for transfers between devices, body(): lax.psum(up_value.astype(jnp.bfloat16), 'tp').astype(jnp.float32)  21.2 us
    all_to_all x1, waiting for transfers between devices, body(): lax.all_to_all(answer, 'ctx', split_axis=0, concat_axis=0, tiled=True)  17.6 us
    ppermute x3, starting transfers between devices, shifted(): return lax.ppermute(x, axis, pairs)  14.3 us
    reduce_scatter x1, waiting for transfers between devices, body(): lax.psum_scatter(moe_rows.astype(jnp.bfloat16), 'exp', scatter_dimension=...  10.9 us
    dot_general x1, matrix products, body(): jnp.dot(hidden, w_down, preferred_element_type=jnp.float32)  10.6 us
  transfers between devices with their start and end apart: 8, of which 8 were waited for; matrix products, arithmetic and copies ran while one was open for 3% of the time, Pallas kernels for 0%

commit v1 on v0

--- a/solution.py
+++ b/solution.py
@@ -1,6 +1,8 @@
 import jax
 import jax.numpy as jnp
 from jax import lax
+from jax.experimental import pallas as pl
+from jax.experimental.pallas import tpu as pltpu
 from jax.sharding import PartitionSpec as P
 
 EXPERTS = 4
@@ -132,6 +134,454 @@
     return (own_stream + moe_piece).astype(jnp.bfloat16)
 
 
+LOG2E = 1.4426950408889634
+AXES = ("ctx", "exp", "tp")
+f32 = jnp.float32
+bf16 = jnp.bfloat16
+
+
+def lanes_to_rows(store_ref, value):
+    rows, width = value.shape
+    count = width // 128
+    for k in range(count):
+        store_ref[pl.ds(k, rows, stride=count), :] = value[:, k * 128 : (k + 1) * 128]
+
+
+def scan_kernel(
+    b_ref, c_ref, dt_ref, conv_ref, z_ref, alog_ref, skip_ref,
+    base_ref, cum_ref, silu_ref, rate_ref, pack_ref, step_s, in_s, z_s, alog_s,
+):
+    tokens, width = dt_ref.shape
+    states = alog_ref.shape[0]
+    g = width // 128
+    lanes_to_rows(step_s, jax.nn.softplus(dt_ref[...]))
+    lanes_to_rows(in_s, conv_ref[...].astype(f32))
+    lanes_to_rows(z_s, z_ref[...].astype(f32))
+    lanes_to_rows(alog_s, alog_ref[...])
+    rate_ref[...] = -jnp.exp(alog_s[...]) * LOG2E
+    skip = skip_ref[...]
+
+    def advance(t, carry):
+        state, cum = carry
+        rows = pl.ds(pl.multiple_of(t * g, g), g)
+        step = step_s[rows, :]
+        inp = in_s[rows, :]
+        drive = step * inp
+        out = skip * inp
+        after = []
+        for n in range(states):
+            now = jnp.exp2(step * rate_ref[n * g : (n + 1) * g, :]) * state[n] + b_ref[t, n] * drive
+            out = out + c_ref[t, n] * now
+            after.append(now)
+        cum = cum + step
+        base_ref[rows, :] = out
+        cum_ref[rows, :] = cum
+        return (tuple(after), cum)
+
+    zero = jnp.zeros((g, 128), f32)
+    state, cum = lax.fori_loop(0, tokens, advance, ((zero,) * states, zero), unroll=2)
+    z = z_s[...]
+    silu_ref[...] = z / (1.0 + jnp.exp(-z))
+    pack_ref[...] = jnp.concatenate(list(state) + [cum, zero], axis=0).astype(bf16)
+
+
+def correct_kernel(c_ref, one_ref, two_ref, three_ref, base_ref, cum_ref, silu_ref, rate_ref, out_ref, gated_s):
+    tokens, width = out_ref.shape
+    g = width // 128
+    states = rate_ref.shape[0] // g
+    top = states * g
+
+    def halves(ref):
+        both = ref[...].astype(f32)
+        return both[:top].reshape(states, g, 128), both[top : top + g]
+
+    rate = rate_ref[...].reshape(states, g, 128)
+    s1, c1 = halves(one_ref)
+    s2, c2 = halves(two_ref)
+    s3, _ = halves(three_ref)
+    entering = s1 + jnp.exp2(c1[None] * rate) * (s2 + jnp.exp2(c2[None] * rate) * s3)
+
+    def one(t, _):
+        rows = pl.ds(pl.multiple_of(t * g, g), g)
+        cum = cum_ref[rows, :]
+        out = base_ref[rows, :]
+        for n in range(states):
+            out = out + c_ref[t, n] * (jnp.exp2(cum * rate_ref[n * g : (n + 1) * g, :]) * entering[n])
+        gated_s[rows, :] = out * silu_ref[rows, :]
+        return 0
+
+    lax.fori_loop(0, tokens, one, 0, unroll=2)
+    for k in range(g):
+        out_ref[:, k * 128 : (k + 1) * 128] = gated_s[pl.ds(k, tokens, stride=g), :].astype(bf16)
+
+
+def place_pair(scratch, odd, first, second):
+    rows = first.shape[0]
+    scratch[pl.ds(pl.multiple_of(odd * rows, rows), rows), :] = first
+    scratch[pl.ds(pl.multiple_of((1 - odd) * rows, rows), rows), :] = second
+
+
+def project_kernel(first_ref, second_ref, own_w_ref, peer_w_ref, out_ref, rows_s):
+    @pl.when(pl.program_id(0) == 0)
+    def _():
+        place_pair(rows_s, lax.axis_index("ctx") % 2, first_ref[...], second_ref[...])
+
+    half = own_w_ref.shape[0]
+    out_ref[...] = (
+        jnp.dot(rows_s[:, :half], own_w_ref[...], preferred_element_type=f32)
+        + jnp.dot(rows_s[:, half:], peer_w_ref[...], preferred_element_type=f32)
+    ).astype(bf16)
+
+
+def select_kernel(
+    own_ref, peer_ref, first_ref, second_ref, gain_ref, choose_ref,
+    stream_first_ref, stream_second_ref, d0_ref, d1_ref, d2_ref, d3_ref, rows_s,
+):
+    odd = lax.axis_index("ctx") % 2
+    block = stream_first_ref.shape[0]
+    width = own_ref.shape[1]
+    place_pair(rows_s, odd, first_ref[...], second_ref[...])
+    stream = (
+        rows_s[:, :width].astype(f32) + (own_ref[...].astype(f32) + peer_ref[...].astype(f32))
+    ).astype(bf16)
+    rows_s[:, :width] = stream
+    stream_first_ref[...] = rows_s[pl.ds(pl.multiple_of(odd * block, block), block), :width]
+    stream_second_ref[...] = rows_s[pl.ds(pl.multiple_of((1 - odd) * block, block), block), :width]
+    wide = stream.astype(f32)
+    squares = jnp.sum(wide * wide, axis=1, keepdims=True)
+    high = squares.astype(bf16)
+    low = (squares - high.astype(f32)).astype(bf16)
+    lane = lax.broadcasted_iota(jnp.int32, (2 * block, 128), 1)
+    stats = jnp.where(lane == 0, high.astype(f32), jnp.where(lane == 1, low.astype(f32), 0.0)).astype(bf16)
+    feats = (wide * gain_ref[...]).astype(bf16)
+    count = d0_ref.shape[0]
+    for p, ref in enumerate((d0_ref, d1_ref, d2_ref, d3_ref)):
+        pick = choose_ref[p * count : (p + 1) * count, :]
+        ref[:, :width] = jnp.dot(pick, feats, preferred_element_type=f32).astype(bf16)
+        ref[:, width:] = jnp.dot(pick, stats, preferred_element_type=f32).astype(bf16)
+
+
+def gate_up_kernel(
+    a0_ref, a1_ref, a2_ref, a3_ref, b0_ref, b1_ref, b2_ref, b3_ref, wg_ref, wu_ref,
+    gate_ref, up_ref, squares_ref, feats_s,
+):
+    @pl.when(pl.program_id(0) == 0)
+    def _():
+        expert = lax.axis_index("ctx")
+        tp = lax.axis_index("tp")
+        here = expert // 2 == tp
+        count = a0_ref.shape[0]
+        width = a0_ref.shape[1] - 128
+
+        def put(group, near_ref, far_ref):
+            rows = pl.ds(pl.multiple_of((tp ^ group) * count, count), count)
+            for side, ref in ((expert % 2, near_ref), (1 - expert % 2, far_ref)):
+                feats_s[rows, pl.ds(pl.multiple_of(side * width, width), width)] = ref[:, :width]
+            squares_ref[rows, :] = near_ref[:, width:].astype(f32) + far_ref[:, width:].astype(f32)
+
+        @pl.when(here)
+        def _():
+            put(0, a0_ref, a1_ref)
+            put(1, b0_ref, b1_ref)
+
+        @pl.when(jnp.logical_not(here))
+        def _():
+            put(0, a2_ref, a3_ref)
+            put(1, b2_ref, b3_ref)
+
+    feats = feats_s[...]
+    gate_ref[...] = jnp.dot(feats, wg_ref[...], preferred_element_type=f32).astype(bf16)
+    up_ref[...] = jnp.dot(feats, wu_ref[...], preferred_element_type=f32).astype(bf16)
+
+
+def hidden_of(gate0, gate1, up0, up1, sq0, sq1, features):
+    squares = sq0[...] + sq1[...]
+    scale = lax.rsqrt((squares[:, 0:1] + squares[:, 1:2]) * (1.0 / features) + 1e-06)
+    gate = (gate0[...].astype(f32) + gate1[...].astype(f32)) * scale
+    up = (up0[...].astype(f32) + up1[...].astype(f32)) * scale
+    return (gate / (1.0 + jnp.exp(-gate)) * up).astype(bf16)
+
+
+def down_first_kernel(features, gate0, gate1, up0, up1, sq0, sq1, w_ref, out_ref, hidden_s):
+    @pl.when(pl.program_id(0) == 0)
+    def _():
+        hidden_s[...] = hidden_of(gate0, gate1, up0, up1, sq0, sq1, features)
+
+    out_ref[...] = jnp.dot(hidden_s[...], w_ref[...], preferred_element_type=f32)
+
+
+def down_second_kernel(features, gate0, gate1, up0, up1, sq0, sq1, w_ref, acc_ref, out_ref, hidden_s):
+    @pl.when(pl.program_id(0) == 0)
+    def _():
+        hidden_s[...] = hidden_of(gate0, gate1, up0, up1, sq0, sq1, features)
+
+    out_ref[...] = (acc_ref[...] + jnp.dot(hidden_s[...], w_ref[...], preferred_element_type=f32)).astype(bf16)
+
+
+def reply_kernel(own_ref, peer_ref, r0_ref, r1_ref, r2_ref, r3_ref, sum_s):
+    expert = lax.axis_index("ctx")
+    sum_s[...] = own_ref[...].astype(f32) + peer_ref[...].astype(f32)
+    count = r0_ref.shape[0]
+    for p, ref in enumerate((r0_ref, r1_ref, r2_ref, r3_ref)):
+        ref[...] = sum_s[pl.ds(pl.multiple_of((expert ^ p) * count, 8), count), :].astype(bf16)
+
+
+def finish_kernel(stream_ref, high_ref, low_ref, r0_ref, r1_ref, r2_ref, r3_ref, out_ref):
+    total = stream_ref[...].astype(f32)
+    for p, ref in enumerate((r0_ref, r1_ref, r2_ref, r3_ref)):
+        rows = ref[...]
+        total = total + jnp.dot(high_ref[p], rows, preferred_element_type=f32)
+        total = total + jnp.dot(low_ref[p], rows, preferred_element_type=f32)
+    out_ref[...] = total.astype(bf16)
+
+
+VMEM_LIMIT = 40 * 1024 * 1024
+
+
+def params(**kw):
+    return pltpu.CompilerParams(vmem_limit_bytes=VMEM_LIMIT, **kw)
+
+
+VM = pl.BlockSpec(memory_space=pltpu.VMEM)
+SM = pl.BlockSpec(memory_space=pltpu.SMEM)
+
+
+def call(kernel, out, ins, scratch=(), args=()):
+    return pl.pallas_call(
+        kernel, out_shape=out, in_specs=ins, out_specs=jax.tree.map(lambda _: VM, out), scratch_shapes=list(scratch),
+        compiler_params=params(),
+    )(*args)
+
+
+def shape(rows, cols, kind):
+    return jax.ShapeDtypeStruct((rows, cols), kind)
+
+
+def fast_body(
+    resid, conv_out, gate_z, dt_raw, b_proj, c_proj, a_log, d_skip, out_weight, norm_gain,
+    route_ids, route_weight, w_gate, w_up, w_down,
+):
+    tokens, model_width = resid.shape
+    ctx_count, exp_count, tp_count = (lax.axis_size(a) for a in AXES)
+    ctx, exp, tp = (lax.axis_index(a) for a in AXES)
+    channels = conv_out.shape[1]
+    states = a_log.shape[0]
+    block_cols = out_weight.shape[1]
+    half_width = model_width // tp_count
+    piece_width = half_width // exp_count
+    g = channels // 128
+
+    def number(c, x, t):
+        return (c * exp_count + x) * tp_count + t
+
+    def owner(c):
+        return c // (ctx_count // tp_count)
+
+    chips = [(c, x) for c in range(ctx_count) for x in range(exp_count)]
+
+    def permute(x, pairs):
+        return lax.ppermute(x, AXES, pairs)
+
+    def to_owner(x, p):
+        return permute(x, [(number(c ^ p, e, owner(c)), number(c, e, owner(c))) for c, e in chips])
+
+    def from_owner(x, p):
+        return permute(x, [(number(c, e, owner(c)), number(c ^ p, e, owner(c))) for c, e in chips])
+
+    def swap_tp(x):
+        return lax.ppermute(x, "tp", [(i, tp_count - 1 - i) for i in range(tp_count)])
+
+    with jax.named_scope("scan"):
+        flat = shape(tokens * g, 128, f32)
+        rates = shape(states * g, 128, f32)
+        packed = shape((states + 2) * g, 128, bf16)
+        base, cum, silu_z, rate, pack = call(
+            scan_kernel, (flat, flat, flat, rates, packed), [SM, SM] + [VM] * 5,
+            [pltpu.VMEM((tokens * g, 128), f32)] * 3 + [pltpu.VMEM((states * g, 128), f32)],
+            (b_proj, c_proj, dt_raw, conv_out, gate_z, a_log, d_skip.reshape(g, 128)),
+        )
+    with jax.named_scope("relay"):
+        entered = [
+            permute(
+                pack,
+                [(number(c, x, t), number(c + s, x, t)) for c, x in chips for t in range(tp_count) if c + s < ctx_count],
+            )
+            for s in range(1, ctx_count)
+        ]
+    with jax.named_scope("routing"):
+        flat_ids = route_ids.reshape(-1)
+        pairs = flat_ids.shape[0]
+        onehot = (flat_ids[:, None] == jnp.arange(EXPERTS, dtype=jnp.int32)[None, :]).astype(f32)
+        index = jnp.arange(pairs, dtype=jnp.int32)
+        earlier = (index[:, None] > index[None, :]).astype(f32)
+        before = jnp.dot(earlier, onehot, preferred_element_type=f32)
+        position = jnp.sum(before * onehot, axis=1).astype(jnp.int32)
+        target = (flat_ids * CAP + position).reshape(tokens, 2)
+        slots = jnp.arange(EXPERTS * CAP, dtype=jnp.int32)
+        hits = slots[None, :, None] == target[:, None, :]
+        weights = jnp.sum(jnp.where(hits, route_weight[:, None, :], 0.0), axis=2).reshape(tokens, EXPERTS, CAP)
+        weights = jnp.stack(
+            [lax.dynamic_index_in_dim(weights, ctx ^ p, 1, keepdims=False) for p in range(EXPERTS)]
+        )
+        weights_high = weights.astype(bf16)
+        weights_low = (weights - weights_high.astype(f32)).astype(bf16)
+        target_lanes = jnp.pad(target.astype(bf16), ((0, 0), (0, 126)))
+    with jax.named_scope("residual"):
+        cols = [
+            jnp.concatenate([lax.dynamic_slice_in_dim(resid, (ctx ^ p) * block_cols, block_cols, 1), target_lanes], axis=1)
+            for p in range(ctx_count)
+        ]
+        cols = [cols[0]] + [to_owner(cols[p], p) for p in range(1, ctx_count)]
+        gain = lax.dynamic_slice_in_dim(norm_gain, ctx * block_cols, block_cols, 0)[None, :]
+        peer_weight = swap_tp(out_weight)
+    with jax.named_scope("choices"):
+        odd = ctx % 2
+        choose = []
+        for first, second in ((cols[0], cols[1]), (cols[2], cols[3])):
+            ids = [v[:, block_cols : block_cols + 2].astype(f32).T for v in (first, second)]
+            ids = jnp.stack([jnp.where(odd == 0, ids[0], ids[1]), jnp.where(odd == 0, ids[1], ids[0])])
+            want = (
+                (ctx ^ jnp.arange(EXPERTS, dtype=jnp.int32))[:, None] * CAP + jnp.arange(CAP, dtype=jnp.int32)[None, :]
+            ).astype(f32)
+            hit = jnp.any(want[:, None, :, None, None] == ids.transpose(0, 2, 1)[None, :, None, :, :], axis=4)
+            both = hit[:, :, :, None, :] & (jnp.arange(2)[:, None] == jnp.arange(2)[None, :])[None, :, None, :, None]
+            choose.append(both.reshape(EXPERTS * 2 * CAP, 2 * tokens).astype(bf16))
+    with jax.named_scope("correct"):
+        gated = call(
+            correct_kernel, shape(tokens, channels, bf16), [SM] + [VM] * 7, [pltpu.VMEM((tokens * g, 128), f32)],
+            (c_proj, *entered, base, cum, silu_z, rate),
+        )
+    with jax.named_scope("gather_gated"):
+        gated = jnp.concatenate([gated, swap_tp(gated)], axis=1)
+        blocks = [gated] + [to_owner(gated, p) for p in range(1, ctx_count)]
+
+    def project(first, second):
+        n_block = 256 if block_cols % 256 == 0 else block_cols
+        rows = 2 * tokens
+        depth = out_weight.shape[0]
+        whole = pl.BlockSpec((tokens, 2 * depth), lambda n: (0, 0))
+        part = pl.BlockSpec((depth, n_block), lambda n: (0, n))
+        return pl.pallas_call(
+            project_kernel,
+            out_shape=shape(rows, block_cols, bf16),
+            grid=(block_cols // n_block,),
+            in_specs=[whole, whole, part, part],
+            out_specs=pl.BlockSpec((rows, n_block), lambda n: (0, n)),
+            scratch_shapes=[pltpu.VMEM((rows, 2 * depth), bf16)],
+            compiler_params=params(),
+        )(first, second, out_weight, peer_weight)
+
+    stream_blocks = []
+    sent = []
+    for group in range(2):
+        with jax.named_scope("project"):
+            own = project(blocks[2 * group], blocks[2 * group + 1])
+        with jax.named_scope("sum_exp"):
+            peer = permute(own, [(number(c, x, owner(c)), number(c, 1 - x, owner(c))) for c, x in chips])
+        with jax.named_scope("select"):
+            block = shape(tokens, block_cols, bf16)
+            routed = shape(2 * CAP, block_cols + 128, bf16)
+            first, second, *out = call(
+                select_kernel, (block, block) + (routed,) * 4, [VM] * 6,
+                [pltpu.VMEM((2 * tokens, block_cols + 128), bf16)],
+                (own, peer, cols[2 * group], cols[2 * group + 1], gain, choose[group]),
+            )
+            stream_blocks += [first, second]
+        with jax.named_scope("dispatch"):
+            sent.append([out[0]] + [from_owner(out[p], p) for p in range(1, ctx_count)])
+    with jax.named_scope("stream_home"):
+        own_stream = stream_blocks[0]
+        home = [
+            permute(
+                stream_blocks[p],
+                [(number(c, c % exp_count, owner(c)), number(c ^ p, c % exp_count, owner(c))) for c in range(ctx_count)],
+            )
+            for p in range(1, ctx_count)
+        ]
+        apart = ctx ^ (tp * exp_count + exp)
+        for p in range(1, ctx_count):
+            own_stream = jnp.where(apart == p, home[p - 1], own_stream)
+
+    slots_total = EXPERTS * CAP
+    hidden_width = w_gate.shape[1]
+    part_width = hidden_width // 2
+
+    def gate_up(part):
+        n_block = 256
+        steps = part_width // n_block
+        begin = part * steps
+        routed = pl.BlockSpec((2 * CAP, block_cols + 128), lambda n: (0, 0))
+        weight = pl.BlockSpec((half_width, n_block), lambda n: (0, begin + n))
+        out = pl.BlockSpec((slots_total, n_block), lambda n: (0, n))
+        return pl.pallas_call(
+            gate_up_kernel,
+            out_shape=(
+                shape(slots_total, part_width, bf16), shape(slots_total, part_width, bf16), shape(slots_total, 128, f32),
+            ),
+            grid=(steps,),
+            in_specs=[routed] * 8 + [weight, weight],
+            out_specs=(out, out, pl.BlockSpec((slots_total, 128), lambda n: (0, 0))),
+            scratch_shapes=[pltpu.VMEM((slots_total, half_width), bf16)],
+            compiler_params=params(),
+        )(*sent[0], *sent[1], w_gate, w_up)
+
+    with jax.named_scope("gate_up"):
+        parts = []
+        for part in range(2):
+            gate, up, squares = gate_up(part)
+            if part == 0:
+                squares_own, squares_peer = squares, swap_tp(squares)
+            parts.append((gate, swap_tp(gate), up, swap_tp(up), squares_own, squares_peer))
+
+    def down(part, kernel, kind, base_block, count, acc=None):
+        n_block = 256
+        whole = pl.BlockSpec((slots_total, part_width), lambda n, s: (0, 0))
+        small = pl.BlockSpec((slots_total, 128), lambda n, s: (0, 0))
+        ins = [whole] * 4 + [small] * 2 + [pl.BlockSpec((part_width, n_block), lambda n, s: (part, s[0] + n))]
+        args = [*parts[part], w_down]
+        if acc is not None:
+            ins.append(pl.BlockSpec((slots_total, n_block), lambda n, s: (0, s[0] + n)))
+            args.append(acc)
+
+        def body_kernel(start_ref, *refs):
+            kernel(model_width, *refs)
+
+        return pl.pallas_call(
+            body_kernel,
+            out_shape=shape(slots_total, count * n_block, kind),
+            grid_spec=pltpu.PrefetchScalarGridSpec(
+                num_scalar_prefetch=1,
+                grid=(count,),
+                in_specs=ins,
+                out_specs=pl.BlockSpec((slots_total, n_block), lambda n, s: (0, n)),
+                scratch_shapes=[pltpu.VMEM((slots_total, part_width), bf16)],
+            ),
+            compiler_params=params(),
+        )(base_block, *args)
+
+    with jax.named_scope("down"):
+        blocks_per_piece = piece_width // 256
+        zero = jnp.zeros((1,), jnp.int32)
+        acc = down(0, down_first_kernel, f32, zero, half_width // 256)
+        theirs = down(1, down_second_kernel, bf16, zero + (1 - exp) * blocks_per_piece, blocks_per_piece, acc)
+        mine = down(1, down_second_kernel, bf16, zero + exp * blocks_per_piece, blocks_per_piece, acc)
+    with jax.named_scope("reply"):
+        peer = lax.ppermute(theirs, "exp", [(0, 1), (1, 0)])
+        reply = shape(CAP, piece_width, bf16)
+        replies = call(
+            reply_kernel, (reply,) * 4, [VM] * 2, [pltpu.VMEM((slots_total, piece_width), f32)], (mine, peer)
+        )
+        replies = [replies[0]] + [
+            permute(replies[p], [(number(c, x, t), number(c ^ p, x, t)) for c, x in chips for t in range(tp_count)])
+            for p in range(1, ctx_count)
+        ]
+    with jax.named_scope("finish"):
+        return call(
+            finish_kernel, shape(tokens, piece_width, bf16), [VM] * 7, (),
+            (own_stream, weights_high, weights_low, *replies),
+        )
+
+
 def solution(mesh):
     in_specs = (
         P(("groups", "ctx"), None),
@@ -151,4 +601,7 @@
         P(("ctx", "exp"), "tp"),
     )
     out_specs = P(("groups", "ctx"), ("tp", "exp"))
-    return jax.shard_map(body, mesh=mesh, in_specs=in_specs, out_specs=out_specs, check_vma=False)
+    sizes = dict(mesh.shape)
+    small = (sizes["ctx"], sizes["exp"], sizes["tp"]) == (EXPERTS, 2, 2)
+    chosen = fast_body if small else body
+    return jax.shard_map(chosen, mesh=mesh, in_specs=in_specs, out_specs=out_specs, check_vma=False)

time: 322 us -> 171 us (0.53)
  waiting for transfers between devices: 218 us -> 23.3 us
  Pallas kernels: 0 us -> 54 us
  starting transfers between devices: 19.2 us -> 58.6 us
  matrix products: 37.9 us -> 0.15 us
  local copies, waits for them, and re-layouts: 2.05 us -> 25.6 us
  blocking collectives: 21.2 us -> 0 us
  between operations: 13.3 us -> 0.6 us
    all_gather x1 -> x0, waiting for transfers between devices: 123 us -> none  [body(): lax.all_gather(out_weight, 'ctx', axis=1, tiled=True)]
    psum x2 -> x0, waiting for transfers between devices: 57.4 us -> none  [the longest x1 36.2 us: body(): mamba_out = lax.psum(partial_value, ('exp', 'tp'))]
    pallas_call x0 -> x13, Pallas kernels: none -> 54 us  [the longest x2 20.7 us: gate_up(): pl.pallas_call(gate_up_kernel, out_shape=(shape(slots_total, part_width,...]
    ppermute x3 -> x31, starting transfers between devices: 14.3 us -> 58.6 us  [the longest x23 52.1 us: permute(): return lax.ppermute(x, AXES, pairs)]
    dot_general x7 -> x1, matrix products: 37.9 us -> 0.15 us  [fast_body(): before = jnp.dot(earlier, onehot, preferred_element_type=f32)]
    all_to_all x1 -> x0, blocking collectives: 21.2 us -> none  [body(): lax.all_to_all(outgoing, 'ctx', split_axis=0, concat_axis=0, tiled=True)]
    all_to_all x1 -> x0, waiting for transfers between devices: 17.6 us -> none  [body(): lax.all_to_all(answer, 'ctx', split_axis=0, concat_axis=0, tiled=True)]
    unnamed x21 -> x45, local copies, waits for them, and re-layouts: 0.3 us -> 16.4 us
  transfers between devices with their start and end apart: 8 -> 31, of which waited for: 8 -> 9; matrix products, arithmetic and copies ran while one was open for 3% -> 10% of each run, Pallas kernels for 0% -> 19%
where the time goes in v1:
time: 171 us; the launch traced here: 169 us
  starting transfers between devices  58.6 us (34%)
  Pallas kernels  54 us (32%)
  local copies, waits for them, and re-layouts  25.6 us (15%)
  waiting for transfers between devices  23.3 us (14%)
  other arithmetic  7.05 us (4%)
    ppermute x23, starting transfers between devices, permute(): return lax.ppermute(x, AXES, pairs)  52.1 us
    ppermute x23, waiting for transfers between devices, permute(): return lax.ppermute(x, AXES, pairs)  21.1 us
    pallas_call x2, Pallas kernels, gate_up(): pl.pallas_call(gate_up_kernel, out_shape=(shape(slots_total, part_width,...  20.7 us
    pallas_call x3, Pallas kernels, down(): pl.pallas_call(body_kernel, out_shape=shape(slots_total, count * n_block,...  20.2 us
    unnamed x45, local copies, waits for them, and re-layouts  16.4 us
    pallas_call x6, Pallas kernels, call(): pl.pallas_call(kernel, out_shape=out, in_specs=ins, out_specs=jax.tree.ma...  9.22 us
    dynamic_slice x5, local copies, waits for them, and re-layouts, fast_body(): lax.dynamic_index_in_dim(weights, ctx ^ p, 1, keepdims=False)  5.67 us
    ppermute x7, starting transfers between devices, swap_tp(): lax.ppermute(x, 'tp', [(i, tp_count - 1 - i) for i in range(tp_count)])  5.03 us
  transfers between devices with their start and end apart: 31, of which 9 were waited for; matrix products, arithmetic and copies ran while one was open for 10% of the time, Pallas kernels for 19%

profile of v1, /device:TPU:0, one launch (start us, length us, event | category | flops | bytes accessed | tf_op | source)
XLA Modules:
  0.0 169.2 jit_solution(6269656285378220668)
XLA Ops:
  5.8 3.5 %scan.1 = (f32[512,128]{1,0:T(8,128)S(1)}, f32[512,128]{1,0:T(8,128)S(1)}, f32[512,128]{1,0:T(8,128)S(1)}, f32[128,128]{1,0:T(8,128)S(1)}, bf16[144,128]{1,0:T(8,128)(2,1)S(1)}) custom-call(f32[64,16]{1,0:T(8,128)S(1)} %copy.62.b_ref, f32[64,16]{1,0:T(8,128)S(1)} %copy.64.c_ref, f32[64,1024]{1,0:T(8,128)S(1)} %copy-done.2, bf16[64,1024]{1,0:T(8,128)(2,1)S(1)} %copy-done.9, ...), custom_call_target="tpu_custom_call" | custom-call | tf_op jit(solution)/shard_map/scan/pallas_call | solution.py:350
  9.4 7.0 %collective-permute-start.2 = (bf16[144,128]{1,0:T(8,128)(2,1)S(1)}, bf16[144,128]{1,0:T(8,128)(2,1)S(1)}, u32[]{:S(2)}, u32[]{:S(2)}) collective-permute-start(bf16[144,128]{1,0:T(8,128)(2,1)S(1)} %get-tuple-element.31), channel_id=1, source_target_pairs={{0,12},{1,13},{2,14},{3,15},{16,28},{17,29},{18,30},{19,31}} | collective-permute-start | bytes 110600 | tf_op jit(solution)/shard_map/relay/ppermute | solution.py:383
  16.4 1.3 collective-permute-start.1
  17.7 2.5 %collective-permute-start = (bf16[144,128]{1,0:T(8,128)(2,1)S(1)}, bf16[144,128]{1,0:T(8,128)(2,1)S(1)}, u32[]{:S(2)}, u32[]{:S(2)}) collective-permute-start(bf16[144,128]{1,0:T(8,128)(2,1)S(1)} %get-tuple-element.31), channel_id=1, source_target_pairs={{0,4},{1,5},{2,6},{3,7},{4,8},{5,9},{6,10},{7,11},{8,12},{9,13},{1... | collective-permute-start | bytes 110600 | tf_op jit(solution)/shard_map/relay/ppermute | solution.py:383
  22.3 1.1 constant_dynamic-slice_fusion.5
  24.8 1.9 %collective-permute-start.14 = (bf16[64,1152]{1,0:T(8,128)(2,1)}, bf16[64,1152]{1,0:T(8,128)(2,1)S(1)}, u32[]{:S(2)}, u32[]{:S(2)}) collective-permute-start(bf16[64,1152]{1,0:T(8,128)(2,1)} %get-tuple-element.76), channel_id=1, source_target_pairs={{4,0},{6,2},{0,4},{2,6},{13,9},{15,11},{9,13},{11,15},{20,16},{22,... | collective-permute-start | bytes 442376 | tf_op jit(solution)/shard_map/residual/ppermute | solution.py:383
  27.9 1.3 dynamic_slice.30
  29.2 1.3 collective-permute-start.8
  30.5 1.3 collective-permute-start.9
  31.8 2.3 %correct.1 = bf16[64,1024]{1,0:T(8,128)(2,1)S(1)} custom-call(f32[64,16]{1,0:T(8,128)S(1)} %copy.64.c_ref, bf16[144,128]{1,0:T(8,128)(2,1)S(1)} %collective-permute-done.one_ref, bf16[144,128]{1,0:T(8,128)(2,1)S(1)} %collective-permute-done.1.two_ref, bf16[144,128]{1,0:T(8,128)(2,1)S(1)} %collective-permute-done.2.three_ref, ...), custom_call_target="tpu_custom_call" | custom-call | tf_op jit(solution)/shard_map/correct/pallas_call | solution.py:350
  34.2 1.4 collective-permute-start.3
  36.6 2.9 %collective-permute-start.12 = (bf16[64,2048]{1,0:T(8,128)(2,1)S(1)}, bf16[64,2048]{1,0:T(8,128)(2,1)S(1)}, u32[]{:S(2)}, u32[]{:S(2)}) collective-permute-start(bf16[64,2048]{1,0:T(8,128)(2,1)S(1)} %pad_maximum_fusion.first_ref), channel_id=1, source_target_pairs={{4,0},{6,2},{0,4},{2,6},{13,9},{15,11},{9,13},{11,15},{20,16},{22,... | collective-permute-start | bytes 786440 | tf_op jit(solution)/shard_map/gather_gated/ppermute | solution.py:383
  39.5 1.3 collective-permute-start.5
  40.9 1.3 collective-permute-start.4
  43.8 5.9 %collective-permute-done.5.second_ref = bf16[64,2048]{1,0:T(8,128)(2,1)S(1)} collective-permute-done((bf16[64,2048]{1,0:T(8,128)(2,1)S(1)}, bf16[64,2048]{1,0:T(8,128)(2,1)S(1)}, u32[]{:S(2)}, u32[]{:S(2)}) %collective-permute-start.5) | collective-permute-done | bytes 262176 | tf_op jit(solution)/shard_map/gather_gated/ppermute | solution.py:383
  49.7 7.0 %collective-permute-done.4.first_ref = bf16[64,2048]{1,0:T(8,128)(2,1)S(1)} collective-permute-done((bf16[64,2048]{1,0:T(8,128)(2,1)S(1)}, bf16[64,2048]{1,0:T(8,128)(2,1)S(1)}, u32[]{:S(2)}, u32[]{:S(2)}) %collective-permute-start.4) | collective-permute-done | bytes 262176 | tf_op jit(solution)/shard_map/gather_gated/ppermute | solution.py:383
  56.7 1.6 copy-done
  58.3 2.0 %project.2.own_ref = bf16[128,1024]{1,0:T(8,128)(2,1)S(1)} custom-call(bf16[64,2048]{1,0:T(8,128)(2,1)S(1)} %collective-permute-done.4.first_ref, bf16[64,2048]{1,0:T(8,128)(2,1)S(1)} %collective-permute-done.5.second_ref, bf16[1024,1024]{1,0:T(8,128)(2,1)S(1)} %copy-done, bf16[1024,1024]{1,0:T(8,128)(2,1)S(1)} %collective-permute-done.6.peer_w_ref), custom_call_target="tpu_custom_call" | custom-call | tf_op jit(solution)/shard_map/project/pallas_call | solution.py:464
  60.2 3.4 %collective-permute-start.7 = (bf16[128,1024]{1,0:T(8,128)(2,1)S(1)}, bf16[128,1024]{1,0:T(8,128)(2,1)S(1)}, u32[]{:S(2)}, u32[]{:S(2)}) collective-permute-start(bf16[128,1024]{1,0:T(8,128)(2,1)S(1)} %project.2.own_ref), channel_id=1, source_target_pairs={{0,2},{2,0},{4,6},{6,4},{9,11},{11,9},{13,15},{15,13},{16,18},{18,... | collective-permute-start | bytes 786440 | tf_op jit(solution)/shard_map/sum_exp/ppermute | solution.py:383
  64.5 1.6 copy-done.1
  66.1 2.0 %project.3.own_ref = bf16[128,1024]{1,0:T(8,128)(2,1)S(1)} custom-call(bf16[64,2048]{1,0:T(8,128)(2,1)S(1)} %pad_maximum_fusion.first_ref, bf16[64,2048]{1,0:T(8,128)(2,1)S(1)} %collective-permute-done.12.second_ref, bf16[1024,1024]{1,0:T(8,128)(2,1)S(1)} %copy-done.1, bf16[1024,1024]{1,0:T(8,128)(2,1)S(1)} %collective-permute-done.6.peer_w_ref), custom_call_target="tpu_custom_call" | custom-call | tf_op jit(solution)/shard_map/project/pallas_call | solution.py:464
  68.1 2.4 %collective-permute-start.13 = (bf16[128,1024]{1,0:T(8,128)(2,1)S(1)}, bf16[128,1024]{1,0:T(8,128)(2,1)S(1)}, u32[]{:S(2)}, u32[]{:S(2)}) collective-permute-start(bf16[128,1024]{1,0:T(8,128)(2,1)S(1)} %project.3.own_ref), channel_id=1, source_target_pairs={{0,2},{2,0},{4,6},{6,4},{9,11},{11,9},{13,15},{15,13},{16,18},{18,... | collective-permute-start | bytes 786440 | tf_op jit(solution)/shard_map/sum_exp/ppermute | solution.py:383
  76.1 1.9 %collective-permute-start.19 = (bf16[80,1152]{1,0:T(8,128)(2,1)S(1)}, bf16[80,1152]{1,0:T(8,128)(2,1)S(1)}, u32[]{:S(2)}, u32[]{:S(2)}) collective-permute-start(bf16[80,1152]{1,0:T(8,128)(2,1)S(1)} %get-tuple-element.45), channel_id=1, source_target_pairs={{0,4},{2,6},{4,0},{6,2},{9,13},{11,15},{13,9},{15,11},{16,20},{18,... | collective-permute-start | bytes 552968 | tf_op jit(solution)/shard_map/dispatch/ppermute | solution.py:383
  78.2 1.3 collective-permute-start.20
  79.5 1.3 collective-permute-start.21
  82.9 3.9 %collective-permute-start.16 = (bf16[80,1152]{1,0:T(8,128)(2,1)S(1)}, bf16[80,1152]{1,0:T(8,128)(2,1)S(1)}, u32[]{:S(2)}, u32[]{:S(2)}) collective-permute-start(bf16[80,1152]{1,0:T(8,128)(2,1)S(1)} %get-tuple-element.41), channel_id=1, source_target_pairs={{0,4},{2,6},{4,0},{6,2},{9,13},{11,15},{13,9},{15,11},{16,20},{18,... | collective-permute-start | bytes 552968 | tf_op jit(solution)/shard_map/dispatch/ppermute | solution.py:383
  86.9 1.3 collective-permute-start.17
  88.2 1.3 collective-permute-start.18
  89.5 1.1 collective-permute-done.16.a1_ref
  90.6 1.3 collective-permute-done.17.a2_ref
  91.9 2.0 %collective-permute-done.18.a3_ref = bf16[80,1152]{1,0:T(8,128)(2,1)S(1)} collective-permute-done((bf16[80,1152]{1,0:T(8,128)(2,1)S(1)}, bf16[80,1152]{1,0:T(8,128)(2,1)S(1)}, u32[]{:S(2)}, u32[]{:S(2)}) %collective-permute-start.18) | collective-permute-done | bytes 184352 | tf_op jit(solution)/shard_map/dispatch/ppermute | solution.py:383
  93.9 10.4 %gate_up.3 = (bf16[160,2048]{1,0:T(8,128)(2,1)}, bf16[160,2048]{1,0:T(8,128)(2,1)}, f32[160,128]{1,0:T(8,128)S(1)}) custom-call(bf16[80,1152]{1,0:T(8,128)(2,1)S(1)} %get-tuple-element.40.a0_ref, bf16[80,1152]{1,0:T(8,128)(2,1)S(1)} %collective-permute-done.16.a1_ref, bf16[80,1152]{1,0:T(8,128)(2,1)S(1)} %collective-permute-done.17.a2_ref, ...), custom_call_target="tpu_custom_call" | custom-call | tf_op jit(solution)/shard_map/gate_up/pallas_call | solution.py:516
  104.3 2.5 %collective-permute-start.25 = (bf16[160,2048]{1,0:T(8,128)(2,1)}, bf16[160,2048]{1,0:T(8,128)(2,1)}, u32[]{:S(2)}, u32[]{:S(2)}) collective-permute-start(bf16[160,2048]{1,0:T(8,128)(2,1)} %get-tuple-element.51.refs_0_), channel_id=1, source_target_pairs={{0,1},{1,0},{2,3},{3,2},{4,5},{5,4},{6,7},{7,6},{8,9},{9,8},{10,11... | collective-permute-start | bytes 1966088 | tf_op jit(solution)/shard_map/gate_up/ppermute | solution.py:392
  106.9 10.2 %gate_up.2 = (bf16[160,2048]{1,0:T(8,128)(2,1)S(1)}, bf16[160,2048]{1,0:T(8,128)(2,1)S(1)}, f32[160,128]{1,0:T(8,128)}) custom-call(bf16[80,1152]{1,0:T(8,128)(2,1)S(1)} %get-tuple-element.40.a0_ref, bf16[80,1152]{1,0:T(8,128)(2,1)S(1)} %collective-permute-done.16.a1_ref, bf16[80,1152]{1,0:T(8,128)(2,1)S(1)} %collective-permute-done.17.a2_ref, ...), custom_call_target="tpu_custom_call" | custom-call | tf_op jit(solution)/shard_map/gate_up/pallas_call | solution.py:516
  118.4 1.2 collective-permute-done.24.refs_5_
  119.6 9.0 %down.3.refs_7_ = f32[160,2048]{1,0:T(8,128)S(1)} custom-call(s32[1]{0:T(128)} %constant.55.clone.1.start_ref, bf16[160,2048]{1,0:T(8,128)(2,1)} %get-tuple-element.51.refs_0_, bf16[160,2048]{1,0:T(8,128)(2,1)} %collective-permute-done.25.refs_1_, bf16[160,2048]{1,0:T(8,128)(2,1)} %get-tuple-element.52.refs_2_, ...), custom_call_target="tpu_custom_call" | custom-call | tf_op jit(solution)/shard_map/down/pallas_call | solution.py:549
  128.6 6.0 %down.5 = bf16[160,1024]{1,0:T(8,128)(2,1)} custom-call(s32[1]{0:T(128)} %bitcast.18.start_ref, bf16[160,2048]{1,0:T(8,128)(2,1)S(1)} %get-tuple-element.48.refs_0_, bf16[160,2048]{1,0:T(8,128)(2,1)S(1)} %collective-permute-done.22.refs_1_, bf16[160,2048]{1,0:T(8,128)(2,1)S(1)} %get-tuple-element.49.refs_2_, ...), custom_call_target="tpu_custom_call" | custom-call | tf_op jit(solution)/shard_map/down/pallas_call | solution.py:549
  134.6 1.5 collective-permute-start.27
  137.5 1.4 copy.76
  138.9 1.4 copy.75
  140.3 1.4 copy.74
  141.8 5.8 %collective-permute-start.10 = (bf16[64,1024]{1,0:T(8,128)(2,1)}, bf16[64,1024]{1,0:T(8,128)(2,1)}, u32[]{:S(2)}, u32[]{:S(2)}) collective-permute-start(bf16[64,1024]{1,0:T(8,128)(2,1)} %copy-done.17), channel_id=1, source_target_pairs={{0,12},{6,10},{9,5},{15,3},{16,28},{22,26},{25,21},{31,19}} | collective-permute-start | bytes 393224 | tf_op jit(solution)/shard_map/stream_home/ppermute | solution.py:383
  147.5 2.4 %collective-permute-start.11 = (bf16[64,1024]{1,0:T(8,128)(2,1)}, bf16[64,1024]{1,0:T(8,128)(2,1)}, u32[]{:S(2)}, u32[]{:S(2)}) collective-permute-start(bf16[64,1024]{1,0:T(8,128)(2,1)} %copy-done.16), channel_id=1, source_target_pairs={{0,8},{6,14},{9,1},{15,7},{16,24},{22,30},{25,17},{31,23}} | collective-permute-start | bytes 393224 | tf_op jit(solution)/shard_map/stream_home/ppermute | solution.py:383
  149.9 1.9 %collective-permute-start.15 = (bf16[64,1024]{1,0:T(8,128)(2,1)}, bf16[64,1024]{1,0:T(8,128)(2,1)}, u32[]{:S(2)}, u32[]{:S(2)}) collective-permute-start(bf16[64,1024]{1,0:T(8,128)(2,1)} %copy-done.18), channel_id=1, source_target_pairs={{0,4},{6,2},{9,13},{15,11},{16,20},{22,18},{25,29},{31,27}} | collective-permute-start | bytes 393224 | tf_op jit(solution)/shard_map/stream_home/ppermute | solution.py:383
  153.5 5.1 %down.4.own_ref = bf16[160,1024]{1,0:T(8,128)(2,1)S(1)} custom-call(s32[1]{0:T(128)} %bitcast.17.start_ref, bf16[160,2048]{1,0:T(8,128)(2,1)S(1)} %get-tuple-element.48.refs_0_, bf16[160,2048]{1,0:T(8,128)(2,1)S(1)} %collective-permute-done.22.refs_1_, bf16[160,2048]{1,0:T(8,128)(2,1)S(1)} %get-tuple-element.49.refs_2_, ...), custom_call_target="tpu_custom_call" | custom-call | tf_op jit(solution)/shard_map/down/pallas_call | solution.py:549
  158.7 1.1 reply.1
  160.0 4.3 %collective-permute-start.30 = (bf16[40,1024]{1,0:T(8,128)(2,1)S(1)}, bf16[40,1024]{1,0:T(8,128)(2,1)S(1)}, u32[]{:S(2)}, u32[]{:S(2)}) collective-permute-start(bf16[40,1024]{1,0:T(8,128)(2,1)S(1)} %get-tuple-element.56), channel_id=1, source_target_pairs={{0,12},{1,13},{2,14},{3,15},{4,8},{5,9},{6,10},{7,11},{8,4},{9,5},... | collective-permute-start | bytes 245768 | tf_op jit(solution)/shard_map/reply/ppermute | solution.py:383
  165.3 2.8 %collective-permute-done.29.r2_ref = bf16[40,1024]{1,0:T(8,128)(2,1)S(1)} collective-permute-done((bf16[40,1024]{1,0:T(8,128)(2,1)S(1)}, bf16[40,1024]{1,0:T(8,128)(2,1)S(1)}, u32[]{:S(2)}, u32[]{:S(2)}) %collective-permute-start.29) | collective-permute-done | bytes 81952 | tf_op jit(solution)/shard_map/reply/ppermute | solution.py:383
  (108 shorter events, 28.4 us)
Async XLA Ops:
  1.6 1.0 copy-start.2
  2.5 0.9 copy-start.9
  3.4 0.9 copy-start.10
  4.3 0.8 copy-start.13
  5.2 0.7 copy-start.15
  9.4 19.8 %collective-permute-start.2 = (bf16[144,128]{1,0:T(8,128)(2,1)S(1)}, bf16[144,128]{1,0:T(8,128)(2,1)S(1)}, u32[]{:S(2)}, u32[]{:S(2)}) collective-permute-start(bf16[144,128]{1,0:T(8,128)(2,1)S(1)} %get-tuple-element.31), channel_id=1, source_target_pairs={{0,12},{1,13},{2,14},{3,15},{16,28},{17,29},{18,30},{19,31}} | collective-permute-start | bytes 110600 | tf_op jit(solution)/shard_map/relay/ppermute | solution.py:383
  16.4 14.2 %collective-permute-start.1 = (bf16[144,128]{1,0:T(8,128)(2,1)S(1)}, bf16[144,128]{1,0:T(8,128)(2,1)S(1)}, u32[]{:S(2)}, u32[]{:S(2)}) collective-permute-start(bf16[144,128]{1,0:T(8,128)(2,1)S(1)} %get-tuple-element.31), channel_id=1, source_target_pairs={{0,8},{1,9},{2,10},{3,11},{4,12},{5,13},{6,14},{7,15},{16,24},{17,... | collective-permute-start | bytes 110600 | tf_op jit(solution)/shard_map/relay/ppermute | solution.py:383
  17.7 14.2 %collective-permute-start = (bf16[144,128]{1,0:T(8,128)(2,1)S(1)}, bf16[144,128]{1,0:T(8,128)(2,1)S(1)}, u32[]{:S(2)}, u32[]{:S(2)}) collective-permute-start(bf16[144,128]{1,0:T(8,128)(2,1)S(1)} %get-tuple-element.31), channel_id=1, source_target_pairs={{0,4},{1,5},{2,6},{3,7},{4,8},{5,9},{6,10},{7,11},{8,12},{9,13},{1... | collective-permute-start | bytes 110600 | tf_op jit(solution)/shard_map/relay/ppermute | solution.py:383
  20.1 36.5 %collective-permute-start.6 = (bf16[1024,1024]{1,0:T(8,128)(2,1)}, bf16[1024,1024]{1,0:T(8,128)(2,1)S(1)}, u32[]{:S(2)}, u32[]{:S(2)}) collective-permute-start(bf16[1024,1024]{1,0:T(8,128)(2,1)} %own_w_ref.3), channel_id=1, source_target_pairs={{0,1},{1,0},{2,3},{3,2},{4,5},{5,4},{6,7},{7,6},{8,9},{9,8},{10,11... | collective-permute-start | bytes 6291464 | tf_op jit(solution)/shard_map/residual/ppermute | solution.py:392
  24.8 10.8 %collective-permute-start.14 = (bf16[64,1152]{1,0:T(8,128)(2,1)}, bf16[64,1152]{1,0:T(8,128)(2,1)S(1)}, u32[]{:S(2)}, u32[]{:S(2)}) collective-permute-start(bf16[64,1152]{1,0:T(8,128)(2,1)} %get-tuple-element.76), channel_id=1, source_target_pairs={{4,0},{6,2},{0,4},{2,6},{13,9},{15,11},{9,13},{11,15},{20,16},{22,... | collective-permute-start | bytes 442376 | tf_op jit(solution)/shard_map/residual/ppermute | solution.py:383
  29.2 11.6 %collective-permute-start.8 = (bf16[64,1152]{1,0:T(8,128)(2,1)}, bf16[64,1152]{1,0:T(8,128)(2,1)S(1)}, u32[]{:S(2)}, u32[]{:S(2)}) collective-permute-start(bf16[64,1152]{1,0:T(8,128)(2,1)} %get-tuple-element.74), channel_id=1, source_target_pairs={{8,0},{10,2},{12,4},{14,6},{1,9},{3,11},{5,13},{7,15},{24,16},{26,... | collective-permute-start | bytes 442376 | tf_op jit(solution)/shard_map/residual/ppermute | solution.py:383
  30.5 11.6 %collective-permute-start.9 = (bf16[64,1152]{1,0:T(8,128)(2,1)}, bf16[64,1152]{1,0:T(8,128)(2,1)S(1)}, u32[]{:S(2)}, u32[]{:S(2)}) collective-permute-start(bf16[64,1152]{1,0:T(8,128)(2,1)} %get-tuple-element.75), channel_id=1, source_target_pairs={{12,0},{14,2},{8,4},{10,6},{5,9},{7,11},{1,13},{3,15},{28,16},{30,... | collective-permute-start | bytes 442376 | tf_op jit(solution)/shard_map/residual/ppermute | solution.py:383
  34.2 2.4 %collective-permute-start.3 = (bf16[64,1024]{1,0:T(8,128)(2,1)S(1)}, bf16[64,1024]{1,0:T(8,128)(2,1)S(1)}, u32[]{:S(2)}, u32[]{:S(2)}) collective-permute-start(bf16[64,1024]{1,0:T(8,128)(2,1)S(1)} %correct.1), channel_id=1, source_target_pairs={{0,1},{1,0},{2,3},{3,2},{4,5},{5,4},{6,7},{7,6},{8,9},{9,8},{10,11... | collective-permute-start | bytes 393224 | tf_op jit(solution)/shard_map/gather_gated/ppermute | solution.py:392
  35.6 5.2 %copy-start.3 = (bf16[64,1152]{1,0:T(8,128)(2,1)}, bf16[64,1152]{1,0:T(8,128)(2,1)S(1)}, u32[]{:S(2)}) copy-start(bf16[64,1152]{1,0:T(8,128)(2,1)S(1)} %collective-permute-done.14.second_ref) | copy-start | bytes 442372
  36.6 27.9 %collective-permute-start.12 = (bf16[64,2048]{1,0:T(8,128)(2,1)S(1)}, bf16[64,2048]{1,0:T(8,128)(2,1)S(1)}, u32[]{:S(2)}, u32[]{:S(2)}) collective-permute-start(bf16[64,2048]{1,0:T(8,128)(2,1)S(1)} %pad_maximum_fusion.first_ref), channel_id=1, source_target_pairs={{4,0},{6,2},{0,4},{2,6},{13,9},{15,11},{9,13},{11,15},{20,16},{22,... | collective-permute-start | bytes 786440 | tf_op jit(solution)/shard_map/gather_gated/ppermute | solution.py:383
  39.5 10.2 %collective-permute-start.5 = (bf16[64,2048]{1,0:T(8,128)(2,1)S(1)}, bf16[64,2048]{1,0:T(8,128)(2,1)S(1)}, u32[]{:S(2)}, u32[]{:S(2)}) collective-permute-start(bf16[64,2048]{1,0:T(8,128)(2,1)S(1)} %pad_maximum_fusion.first_ref), channel_id=1, source_target_pairs={{12,0},{14,2},{8,4},{10,6},{5,9},{7,11},{1,13},{3,15},{28,16},{30,... | collective-permute-start | bytes 786440 | tf_op jit(solution)/shard_map/gather_gated/ppermute | solution.py:383
  40.9 15.8 %collective-permute-start.4 = (bf16[64,2048]{1,0:T(8,128)(2,1)S(1)}, bf16[64,2048]{1,0:T(8,128)(2,1)S(1)}, u32[]{:S(2)}, u32[]{:S(2)}) collective-permute-start(bf16[64,2048]{1,0:T(8,128)(2,1)S(1)} %pad_maximum_fusion.first_ref), channel_id=1, source_target_pairs={{8,0},{10,2},{12,4},{14,6},{1,9},{3,11},{5,13},{7,15},{24,16},{26,... | collective-permute-start | bytes 786440 | tf_op jit(solution)/shard_map/gather_gated/ppermute | solution.py:383
  42.8 0.7 copy-start.7
  56.7 1.6 copy-start
  60.2 11.5 %collective-permute-start.7 = (bf16[128,1024]{1,0:T(8,128)(2,1)S(1)}, bf16[128,1024]{1,0:T(8,128)(2,1)S(1)}, u32[]{:S(2)}, u32[]{:S(2)}) collective-permute-start(bf16[128,1024]{1,0:T(8,128)(2,1)S(1)} %project.2.own_ref), channel_id=1, source_target_pairs={{0,2},{2,0},{4,6},{6,4},{9,11},{11,9},{13,15},{15,13},{16,18},{18,... | collective-permute-start | bytes 786440 | tf_op jit(solution)/shard_map/sum_exp/ppermute | solution.py:383
  64.5 1.6 copy-start.1
  68.1 12.7 %collective-permute-start.13 = (bf16[128,1024]{1,0:T(8,128)(2,1)S(1)}, bf16[128,1024]{1,0:T(8,128)(2,1)S(1)}, u32[]{:S(2)}, u32[]{:S(2)}) collective-permute-start(bf16[128,1024]{1,0:T(8,128)(2,1)S(1)} %project.3.own_ref), channel_id=1, source_target_pairs={{0,2},{2,0},{4,6},{6,4},{9,11},{11,9},{13,15},{15,13},{16,18},{18,... | collective-permute-start | bytes 786440 | tf_op jit(solution)/shard_map/sum_exp/ppermute | solution.py:383
  71.8 0.9 copy-start.6
  72.7 0.9 copy-start.8
  73.6 0.7 copy-start.14
  76.1 12.0 %collective-permute-start.19 = (bf16[80,1152]{1,0:T(8,128)(2,1)S(1)}, bf16[80,1152]{1,0:T(8,128)(2,1)S(1)}, u32[]{:S(2)}, u32[]{:S(2)}) collective-permute-start(bf16[80,1152]{1,0:T(8,128)(2,1)S(1)} %get-tuple-element.45), channel_id=1, source_target_pairs={{0,4},{2,6},{4,0},{6,2},{9,13},{11,15},{13,9},{15,11},{16,20},{18,... | collective-permute-start | bytes 552968 | tf_op jit(solution)/shard_map/dispatch/ppermute | solution.py:383
  78.2 11.3 %collective-permute-start.20 = (bf16[80,1152]{1,0:T(8,128)(2,1)S(1)}, bf16[80,1152]{1,0:T(8,128)(2,1)S(1)}, u32[]{:S(2)}, u32[]{:S(2)}) collective-permute-start(bf16[80,1152]{1,0:T(8,128)(2,1)S(1)} %get-tuple-element.46), channel_id=1, source_target_pairs={{0,8},{2,10},{4,12},{6,14},{9,1},{11,3},{13,5},{15,7},{16,24},{18,... | collective-permute-start | bytes 552968 | tf_op jit(solution)/shard_map/dispatch/ppermute | solution.py:383
  79.5 10.0 %collective-permute-start.21 = (bf16[80,1152]{1,0:T(8,128)(2,1)S(1)}, bf16[80,1152]{1,0:T(8,128)(2,1)S(1)}, u32[]{:S(2)}, u32[]{:S(2)}) collective-permute-start(bf16[80,1152]{1,0:T(8,128)(2,1)S(1)} %get-tuple-element.47), channel_id=1, source_target_pairs={{0,12},{2,14},{4,8},{6,10},{9,5},{11,7},{13,1},{15,3},{16,28},{18,... | collective-permute-start | bytes 552968 | tf_op jit(solution)/shard_map/dispatch/ppermute | solution.py:383
  80.8 0.9 copy-start.4
  82.9 21.4 %copy-start.11 = (bf16[64,1024]{1,0:T(8,128)(2,1)}, bf16[64,1024]{1,0:T(8,128)(2,1)S(1)}, u32[]{:S(2)}) copy-start(bf16[64,1024]{1,0:T(8,128)(2,1)S(1)} %get-tuple-element.39) | copy-start | bytes 393220
  82.9 7.7 %collective-permute-start.16 = (bf16[80,1152]{1,0:T(8,128)(2,1)S(1)}, bf16[80,1152]{1,0:T(8,128)(2,1)S(1)}, u32[]{:S(2)}, u32[]{:S(2)}) collective-permute-start(bf16[80,1152]{1,0:T(8,128)(2,1)S(1)} %get-tuple-element.41), channel_id=1, source_target_pairs={{0,4},{2,6},{4,0},{6,2},{9,13},{11,15},{13,9},{15,11},{16,20},{18,... | collective-permute-start | bytes 552968 | tf_op jit(solution)/shard_map/dispatch/ppermute | solution.py:383
  86.9 5.1 %collective-permute-start.17 = (bf16[80,1152]{1,0:T(8,128)(2,1)S(1)}, bf16[80,1152]{1,0:T(8,128)(2,1)S(1)}, u32[]{:S(2)}, u32[]{:S(2)}) collective-permute-start(bf16[80,1152]{1,0:T(8,128)(2,1)S(1)} %get-tuple-element.42), channel_id=1, source_target_pairs={{0,8},{2,10},{4,12},{6,14},{9,1},{11,3},{13,5},{15,7},{16,24},{18,... | collective-permute-start | bytes 552968 | tf_op jit(solution)/shard_map/dispatch/ppermute | solution.py:383
  88.2 5.7 %collective-permute-start.18 = (bf16[80,1152]{1,0:T(8,128)(2,1)S(1)}, bf16[80,1152]{1,0:T(8,128)(2,1)S(1)}, u32[]{:S(2)}, u32[]{:S(2)}) collective-permute-start(bf16[80,1152]{1,0:T(8,128)(2,1)S(1)} %get-tuple-element.43), channel_id=1, source_target_pairs={{0,12},{2,14},{4,8},{6,10},{9,5},{11,7},{13,1},{15,3},{16,28},{18,... | collective-permute-start | bytes 552968 | tf_op jit(solution)/shard_map/dispatch/ppermute | solution.py:383
  104.3 15.2 %collective-permute-start.25 = (bf16[160,2048]{1,0:T(8,128)(2,1)}, bf16[160,2048]{1,0:T(8,128)(2,1)}, u32[]{:S(2)}, u32[]{:S(2)}) collective-permute-start(bf16[160,2048]{1,0:T(8,128)(2,1)} %get-tuple-element.51.refs_0_), channel_id=1, source_target_pairs={{0,1},{1,0},{2,3},{3,2},{4,5},{5,4},{6,7},{7,6},{8,9},{9,8},{10,11... | collective-permute-start | bytes 1966088 | tf_op jit(solution)/shard_map/gate_up/ppermute | solution.py:392
  106.8 10.8 %copy-start.19 = (s32[64,2]{1,0:T(8,128)S(1)}, s32[64,2]{1,0:T(8,128)}, u32[]{:S(2)}) copy-start(s32[64,2]{1,0:T(8,128)} %get-tuple-element.60) | copy-start | bytes 1540
  106.8 11.3 %copy-start.20 = (f32[64,2]{0,1:T(2,128)S(1)}, f32[64,2]{0,1:T(2,128)}, u32[]{:S(2)}) copy-start(f32[64,2]{0,1:T(2,128)} %param.26) | copy-start | bytes 1540
  106.8 12.7 %collective-permute-start.26 = (bf16[160,2048]{1,0:T(8,128)(2,1)}, bf16[160,2048]{1,0:T(8,128)(2,1)}, u32[]{:S(2)}, u32[]{:S(2)}) collective-permute-start(bf16[160,2048]{1,0:T(8,128)(2,1)} %get-tuple-element.52.refs_2_), channel_id=1, source_target_pairs={{0,1},{1,0},{2,3},{3,2},{4,5},{5,4},{6,7},{7,6},{8,9},{9,8},{10,11... | collective-permute-start | bytes 1966088 | tf_op jit(solution)/shard_map/gate_up/ppermute | solution.py:392
  117.1 11.5 %collective-permute-start.22 = (bf16[160,2048]{1,0:T(8,128)(2,1)S(1)}, bf16[160,2048]{1,0:T(8,128)(2,1)S(1)}, u32[]{:S(2)}, u32[]{:S(2)}) collective-permute-start(bf16[160,2048]{1,0:T(8,128)(2,1)S(1)} %get-tuple-element.48.refs_0_), channel_id=1, source_target_pairs={{0,1},{1,0},{2,3},{3,2},{4,5},{5,4},{6,7},{7,6},{8,9},{9,8},{10,11... | collective-permute-start | bytes 1966088 | tf_op jit(solution)/shard_map/gate_up/ppermute | solution.py:392
  117.6 11.1 %collective-permute-start.23 = (bf16[160,2048]{1,0:T(8,128)(2,1)S(1)}, bf16[160,2048]{1,0:T(8,128)(2,1)}, u32[]{:S(2)}, u32[]{:S(2)}) collective-permute-start(bf16[160,2048]{1,0:T(8,128)(2,1)S(1)} %get-tuple-element.49.refs_2_), channel_id=1, source_target_pairs={{0,1},{1,0},{2,3},{3,2},{4,5},{5,4},{6,7},{7,6},{8,9},{9,8},{10,11... | collective-permute-start | bytes 1966088 | tf_op jit(solution)/shard_map/gate_up/ppermute | solution.py:392
  117.7 1.8 %collective-permute-start.24 = (f32[160,128]{1,0:T(8,128)S(1)}, f32[160,128]{1,0:T(8,128)S(1)}, u32[]{:S(2)}, u32[]{:S(2)}) collective-permute-start(f32[160,128]{1,0:T(8,128)S(1)} %get-tuple-element.50.refs_4_), channel_id=1, source_target_pairs={{0,1},{1,0},{2,3},{3,2},{4,5},{5,4},{6,7},{7,6},{8,9},{9,8},{10,11... | collective-permute-start | bytes 245768 | tf_op jit(solution)/shard_map/gate_up/ppermute | solution.py:392
  134.6 24.1 %collective-permute-start.27 = (bf16[160,1024]{1,0:T(8,128)(2,1)}, bf16[160,1024]{1,0:T(8,128)(2,1)}, u32[]{:S(2)}, u32[]{:S(2)}) collective-permute-start(bf16[160,1024]{1,0:T(8,128)(2,1)} %down.5), channel_id=1, source_target_pairs={{0,2},{2,0},{1,3},{3,1},{4,6},{6,4},{5,7},{7,5},{8,10},{10,8},{9,1... | collective-permute-start | bytes 983048 | tf_op jit(solution)/shard_map/reply/ppermute | solution.py:569
  141.8 18.2 %collective-permute-start.10 = (bf16[64,1024]{1,0:T(8,128)(2,1)}, bf16[64,1024]{1,0:T(8,128)(2,1)}, u32[]{:S(2)}, u32[]{:S(2)}) collective-permute-start(bf16[64,1024]{1,0:T(8,128)(2,1)} %copy-done.17), channel_id=1, source_target_pairs={{0,12},{6,10},{9,5},{15,3},{16,28},{22,26},{25,21},{31,19}} | collective-permute-start | bytes 393224 | tf_op jit(solution)/shard_map/stream_home/ppermute | solution.py:383
  147.5 16.8 %collective-permute-start.11 = (bf16[64,1024]{1,0:T(8,128)(2,1)}, bf16[64,1024]{1,0:T(8,128)(2,1)}, u32[]{:S(2)}, u32[]{:S(2)}) collective-permute-start(bf16[64,1024]{1,0:T(8,128)(2,1)} %copy-done.16), channel_id=1, source_target_pairs={{0,8},{6,14},{9,1},{15,7},{16,24},{22,30},{25,17},{31,23}} | collective-permute-start | bytes 393224 | tf_op jit(solution)/shard_map/stream_home/ppermute | solution.py:383
  149.9 14.4 %collective-permute-start.15 = (bf16[64,1024]{1,0:T(8,128)(2,1)}, bf16[64,1024]{1,0:T(8,128)(2,1)}, u32[]{:S(2)}, u32[]{:S(2)}) collective-permute-start(bf16[64,1024]{1,0:T(8,128)(2,1)} %copy-done.18), channel_id=1, source_target_pairs={{0,4},{6,2},{9,13},{15,11},{16,20},{22,18},{25,29},{31,27}} | collective-permute-start | bytes 393224 | tf_op jit(solution)/shard_map/stream_home/ppermute | solution.py:383
  152.7 11.6 %copy-start.12 = (bf16[64,1024]{1,0:T(8,128)(2,1)S(1)}, bf16[64,1024]{1,0:T(8,128)(2,1)}, u32[]{:S(2)}) copy-start(bf16[64,1024]{1,0:T(8,128)(2,1)} %copy-done.11) | copy-start | bytes 393220
  159.8 5.5 %collective-permute-start.28 = (bf16[40,1024]{1,0:T(8,128)(2,1)S(1)}, bf16[40,1024]{1,0:T(8,128)(2,1)S(1)}, u32[]{:S(2)}, u32[]{:S(2)}) collective-permute-start(bf16[40,1024]{1,0:T(8,128)(2,1)S(1)} %get-tuple-element.54), channel_id=1, source_target_pairs={{0,4},{1,5},{2,6},{3,7},{4,0},{5,1},{6,2},{7,3},{8,12},{9,13},{10,... | collective-permute-start | bytes 245768 | tf_op jit(solution)/shard_map/reply/ppermute | solution.py:383
  159.9 8.3 %collective-permute-start.29 = (bf16[40,1024]{1,0:T(8,128)(2,1)S(1)}, bf16[40,1024]{1,0:T(8,128)(2,1)S(1)}, u32[]{:S(2)}, u32[]{:S(2)}) collective-permute-start(bf16[40,1024]{1,0:T(8,128)(2,1)S(1)} %get-tuple-element.55), channel_id=1, source_target_pairs={{0,8},{1,9},{2,10},{3,11},{4,12},{5,13},{6,14},{7,15},{8,0},{9,1},... | collective-permute-start | bytes 245768 | tf_op jit(solution)/shard_map/reply/ppermute | solution.py:383
  160.0 8.2 %collective-permute-start.30 = (bf16[40,1024]{1,0:T(8,128)(2,1)S(1)}, bf16[40,1024]{1,0:T(8,128)(2,1)S(1)}, u32[]{:S(2)}, u32[]{:S(2)}) collective-permute-start(bf16[40,1024]{1,0:T(8,128)(2,1)S(1)} %get-tuple-element.56), channel_id=1, source_target_pairs={{0,12},{1,13},{2,14},{3,15},{4,8},{5,9},{6,10},{7,11},{8,4},{9,5},... | collective-permute-start | bytes 245768 | tf_op jit(solution)/shard_map/reply/ppermute | solution.py:383
  (4 other events, 2.6 us)

commit v2 on v0

--- a/solution.py
+++ b/solution.py
@@ -1,6 +1,10 @@
+import functools
+
 import jax
 import jax.numpy as jnp
 from jax import lax
+from jax.experimental import pallas as pl
+from jax.experimental.pallas import tpu as pltpu
 from jax.sharding import PartitionSpec as P
 
 EXPERTS = 4
@@ -132,6 +136,538 @@
     return (own_stream + moe_piece).astype(jnp.bfloat16)
 
 
+LOG2E = 1.4426950408889634
+AXES = ("ctx", "exp", "tp")
+f32 = jnp.float32
+bf16 = jnp.bfloat16
+
+
+def lanes_to_rows(store_ref, value):
+    rows, width = value.shape
+    count = width // 128
+    for k in range(count):
+        store_ref[pl.ds(k, rows, stride=count), :] = value[:, k * 128 : (k + 1) * 128]
+
+
+def scan_kernel(
+    b_ref, c_ref, dt_ref, conv_ref, z_ref, alog_ref, skip_ref,
+    base_ref, cum_ref, silu_ref, rate_ref, pack_ref, step_s, in_s, z_s, alog_s,
+):
+    tokens, width = dt_ref.shape
+    states = alog_ref.shape[0]
+    g = width // 128
+    lanes_to_rows(step_s, jax.nn.softplus(dt_ref[...]))
+    lanes_to_rows(in_s, conv_ref[...].astype(f32))
+    lanes_to_rows(z_s, z_ref[...].astype(f32))
+    lanes_to_rows(alog_s, alog_ref[...])
+    rate_ref[...] = -jnp.exp(alog_s[...]) * LOG2E
+    skip = skip_ref[...]
+
+    def advance(t, carry):
+        state, cum = carry
+        rows = pl.ds(pl.multiple_of(t * g, g), g)
+        step = step_s[rows, :]
+        inp = in_s[rows, :]
+        drive = step * inp
+        out = skip * inp
+        after = []
+        for n in range(states):
+            now = jnp.exp2(step * rate_ref[n * g : (n + 1) * g, :]) * state[n] + b_ref[n, t] * drive
+            out = out + c_ref[n, t] * now
+            after.append(now)
+        cum = cum + step
+        base_ref[rows, :] = out
+        cum_ref[rows, :] = cum
+        return (tuple(after), cum)
+
+    zero = jnp.zeros((g, 128), f32)
+    state, cum = lax.fori_loop(0, tokens, advance, ((zero,) * states, zero), unroll=2)
+    z = z_s[...]
+    silu_ref[...] = z / (1.0 + jnp.exp(-z))
+    pack_ref[...] = jnp.concatenate(list(state) + [cum, zero], axis=0).astype(bf16)
+
+
+def correct_kernel(c_ref, one_ref, two_ref, three_ref, base_ref, cum_ref, silu_ref, rate_ref, out_ref, gated_s):
+    tokens, width = out_ref.shape
+    g = width // 128
+    states = rate_ref.shape[0] // g
+    top = states * g
+
+    def halves(ref):
+        both = ref[...].astype(f32)
+        return both[:top].reshape(states, g, 128), both[top : top + g]
+
+    rate = rate_ref[...].reshape(states, g, 128)
+    ctx = lax.axis_index("ctx")
+    s1, c1 = halves(one_ref)
+    s2, c2 = halves(two_ref)
+    s3, c3 = halves(three_ref)
+    near, near_sum = jnp.where(ctx == 2, s3, s1), jnp.where(ctx == 2, c3, c1)
+    far = jnp.where(ctx == 3, s3, 0.0)
+    middle = s2 + jnp.exp2(c2[None] * rate) * far
+    entering = near + jnp.exp2(near_sum[None] * rate) * jnp.where(ctx >= 2, middle, 0.0)
+    entering = jnp.where(ctx == 0, 0.0, entering)
+
+    def one(t, _):
+        rows = pl.ds(pl.multiple_of(t * g, g), g)
+        cum = cum_ref[rows, :]
+        out = base_ref[rows, :]
+        for n in range(states):
+            out = out + c_ref[n, t] * (jnp.exp2(cum * rate_ref[n * g : (n + 1) * g, :]) * entering[n])
+        gated_s[rows, :] = out * silu_ref[rows, :]
+        return 0
+
+    lax.fori_loop(0, tokens, one, 0, unroll=2)
+    for k in range(g):
+        out_ref[:, k * 128 : (k + 1) * 128] = gated_s[pl.ds(k, tokens, stride=g), :].astype(bf16)
+
+
+def place_pair(scratch, odd, first, second):
+    rows = first.shape[0]
+    scratch[pl.ds(pl.multiple_of(odd * rows, rows), rows), :] = first
+    scratch[pl.ds(pl.multiple_of((1 - odd) * rows, rows), rows), :] = second
+
+
+def route_kernel(ids_ref, lanes_ref, cols_ref):
+    count = cols_ref.shape[0]
+    ids = ids_ref[...].astype(f32)
+    first, second = ids[0:1, :], ids[1:2, :]
+    expert = lax.broadcasted_iota(jnp.int32, (8, 128), 0).astype(f32)
+    member = (jnp.where(expert == first, 1.0, 0.0) + jnp.where(expert == second, 1.0, 0.0)).astype(bf16)
+    before = lax.broadcasted_iota(jnp.int32, (128, 128), 0)
+    token = lax.broadcasted_iota(jnp.int32, (128, 128), 1)
+    token = jnp.where(token >= count, token - count, token)
+    earlier = jnp.where((before < token) & (before < count), 1.0, 0.0).astype(bf16)
+    rank = jnp.dot(member, earlier, preferred_element_type=f32)
+    slot = [
+        which * CAP + jnp.sum(jnp.where(expert == which, rank, 0.0), axis=0, keepdims=True) for which in (first, second)
+    ]
+    row = lax.broadcasted_iota(jnp.int32, (128, 128), 0)
+    both = jnp.where(row == 0, slot[0], jnp.where(row == 1, slot[1], 0.0))
+    lanes_ref[...] = both[:8]
+    cols_ref[...] = both.T[:count].astype(bf16)
+
+
+def pack_kernel(own_ref, peer_ref, resid_ref, slots_ref, m0_ref, m1_ref, m2_ref, m3_ref):
+    ctx, exp = lax.axis_index("ctx"), lax.axis_index("exp")
+    width = own_ref.shape[1]
+    part = m0_ref.shape[1] - 2 * width - 128
+    for p, ref in enumerate((m0_ref, m1_ref, m2_ref, m3_ref)):
+        ref[:, :width] = own_ref[...]
+        ref[:, width : 2 * width] = peer_ref[...]
+        begin = pl.multiple_of((ctx ^ p) * 2 * part + exp * part, 128)
+        ref[:, 2 * width : 2 * width + part] = resid_ref[:, pl.ds(begin, part)]
+        ref[:, 2 * width + part :] = slots_ref[...]
+
+
+def hold_kernel(own_ref, peer_ref, out_ref, sems):
+    half = own_ref.shape[0]
+    copies = [
+        pltpu.make_async_copy(ref, out_ref.at[pl.ds(k * half, half)], sems.at[k]) for k, ref in enumerate((own_ref, peer_ref))
+    ]
+    for copy in copies:
+        copy.start()
+    for copy in copies:
+        copy.wait()
+
+
+def place_pair(scratch, odd, first, second):
+    rows = first.shape[0]
+    scratch[pl.ds(pl.multiple_of(odd * rows, rows), rows), :] = first
+    scratch[pl.ds(pl.multiple_of((1 - odd) * rows, rows), rows), :] = second
+
+
+def project_kernel(first_ref, second_ref, w_ref, out_ref, slots_ref, rows_s):
+    place_pair(rows_s, lax.axis_index("ctx") % 2, first_ref[...], second_ref[...])
+    exp = lax.axis_index("exp")
+    depth = w_ref.shape[0]
+    part = out_ref.shape[1] // 2
+    resid = rows_s[:, depth : depth + part].astype(f32)
+    feats = rows_s[:, :depth]
+    for side in range(2):
+        value = jnp.dot(feats, w_ref[:, side * part : (side + 1) * part], preferred_element_type=f32)
+        out_ref[:, side * part : (side + 1) * part] = (value + jnp.where(exp == side, resid, 0.0)).astype(bf16)
+    slots_ref[...] = rows_s[:, depth + part :]
+
+
+def select_kernel(
+    own_ref, peer_ref, slots_ref, gain_ref, stream_first_ref, stream_second_ref, d0_ref, d1_ref, d2_ref, d3_ref, rows_s
+):
+    ctx = lax.axis_index("ctx")
+    odd = ctx % 2
+    block = stream_first_ref.shape[0]
+    width = own_ref.shape[1]
+    rows_s[...] = (own_ref[...].astype(f32) + peer_ref[...].astype(f32)).astype(bf16)
+    stream_first_ref[...] = rows_s[pl.ds(pl.multiple_of(odd * block, block), block), :]
+    stream_second_ref[...] = rows_s[pl.ds(pl.multiple_of((1 - odd) * block, block), block), :]
+    wide = rows_s[...].astype(f32)
+    squares = jnp.sum(wide * wide, axis=1, keepdims=True)
+    high = squares.astype(bf16).astype(f32)
+    lane = lax.broadcasted_iota(jnp.int32, (2 * block, 128), 1)
+    stats = jnp.where(lane == 0, high, jnp.where(lane == 1, squares - high, 0.0)).astype(bf16)
+    feats = (wide * gain_ref[...]).astype(bf16)
+    slots = slots_ref[...].astype(f32).T
+    count = d0_ref.shape[0]
+    row = lax.broadcasted_iota(jnp.int32, (count, 2 * block), 0)
+    lane = lax.broadcasted_iota(jnp.int32, (count, 2 * block), 1)
+    late = row >= CAP
+    mine = late == (lane >= block)
+    want = jnp.where(late, row - CAP, row).astype(f32)
+    for p, ref in enumerate((d0_ref, d1_ref, d2_ref, d3_ref)):
+        base = ((ctx ^ p) * CAP).astype(f32)
+        hit = mine & ((slots[0:1, :] == want + base) | (slots[1:2, :] == want + base))
+        pick = jnp.where(hit, 1.0, 0.0).astype(bf16)
+        ref[:, :width] = jnp.dot(pick, feats, preferred_element_type=f32).astype(bf16)
+        ref[:, width:] = jnp.dot(pick, stats, preferred_element_type=f32).astype(bf16)
+
+
+def gate_up_copies(wg_ref, wu_ref, held_ref, sems, begin):
+    depth = wg_ref.shape[0]
+    width = held_ref.shape[1]
+    return [
+        pltpu.make_async_copy(
+            ref.at[:, pl.ds(begin, width)], held_ref.at[pl.ds(k * depth, depth)], sems.at[k]
+        )
+        for k, ref in enumerate((wg_ref, wu_ref))
+    ]
+
+
+def hold_first_kernel(wg_ref, wu_ref, held_ref, sems):
+    copies = gate_up_copies(wg_ref, wu_ref, held_ref, sems, 0)
+    for copy in copies:
+        copy.start()
+    for copy in copies:
+        copy.wait()
+
+
+def gate_up(feats, held_ref, out_ref):
+    depth = feats.shape[1]
+    width = held_ref.shape[1]
+    block = min(512, width)
+    for k in range(2):
+        for n in range(0, width, block):
+            out_ref[:, k * width + n : k * width + n + block] = jnp.dot(
+                feats, held_ref[k * depth : (k + 1) * depth, n : n + block], preferred_element_type=f32
+            ).astype(bf16)
+
+
+def first_half_kernel(
+    a0_ref, a1_ref, a2_ref, a3_ref, b0_ref, b1_ref, b2_ref, b3_ref, held_ref, wg_ref, wu_ref,
+    out_ref, squares_ref, feats_ref, next_ref, sems,
+):
+    copies = gate_up_copies(wg_ref, wu_ref, next_ref, sems, held_ref.shape[1])
+    for copy in copies:
+        copy.start()
+    expert = lax.axis_index("ctx")
+    tp = lax.axis_index("tp")
+    here = expert // 2 == tp
+    count = a0_ref.shape[0]
+    width = a0_ref.shape[1] - 128
+
+    def put(group, near_ref, far_ref):
+        rows = pl.ds(pl.multiple_of((tp ^ group) * count, count), count)
+        for side, ref in ((expert % 2, near_ref), (1 - expert % 2, far_ref)):
+            feats_ref[rows, pl.ds(pl.multiple_of(side * width, width), width)] = ref[:, :width]
+        squares_ref[rows, :] = near_ref[:, width:].astype(f32) + far_ref[:, width:].astype(f32)
+
+    @pl.when(here)
+    def _():
+        put(0, a0_ref, a1_ref)
+        put(1, b0_ref, b1_ref)
+
+    @pl.when(jnp.logical_not(here))
+    def _():
+        put(0, a2_ref, a3_ref)
+        put(1, b2_ref, b3_ref)
+
+    gate_up(feats_ref[...], held_ref, out_ref)
+    for copy in copies:
+        copy.wait()
+
+
+def second_half_kernel(feats_ref, held_ref, wd_ref, out_ref, next_ref, sem):
+    copy = pltpu.make_async_copy(wd_ref, next_ref, sem)
+    copy.start()
+    gate_up(feats_ref[...], held_ref, out_ref)
+    copy.wait()
+
+
+def hidden_of(own_ref, peer_ref, sq0, sq1, features):
+    squares = sq0[...] + sq1[...]
+    scale = lax.rsqrt((squares[:, 0:1] + squares[:, 1:2]) * (1.0 / features) + 1e-06)
+    width = own_ref.shape[1] // 2
+    gate = (own_ref[:, :width].astype(f32) + peer_ref[:, :width].astype(f32)) * scale
+    up = (own_ref[:, width:].astype(f32) + peer_ref[:, width:].astype(f32)) * scale
+    return (gate / (1.0 + jnp.exp(-gate)) * up).astype(bf16)
+
+
+def down_first_kernel(features, own_ref, peer_ref, sq0, sq1, held_ref, out_ref):
+    hidden = hidden_of(own_ref, peer_ref, sq0, sq1, features)
+    depth = hidden.shape[1]
+    block = min(512, out_ref.shape[1])
+    for n in range(0, out_ref.shape[1], block):
+        out_ref[:, n : n + block] = jnp.dot(hidden, held_ref[:depth, n : n + block], preferred_element_type=f32)
+
+
+def down_piece(hidden, held_ref, acc_ref, near_ref, far_ref, sum_s, piece):
+    depth = hidden.shape[1]
+    count, width = near_ref.shape
+    cols = pl.ds(pl.multiple_of(piece * width, width), width)
+    sum_s[...] = acc_ref[:, cols] + jnp.dot(hidden, held_ref[depth:, cols], preferred_element_type=f32)
+    pair = lax.axis_index("ctx") // 2
+    near_ref[...] = sum_s[pl.ds(pl.multiple_of(pair * count, count), count), :].astype(bf16)
+    far_ref[...] = sum_s[pl.ds(pl.multiple_of((1 - pair) * count, count), count), :].astype(bf16)
+
+
+def down_theirs_kernel(
+    features, own_ref, peer_ref, sq0, sq1, held_ref, acc_ref, near_ref, far_ref, hidden_ref, sum_s
+):
+    hidden_ref[...] = hidden_of(own_ref, peer_ref, sq0, sq1, features)
+    down_piece(hidden_ref[...], held_ref, acc_ref, near_ref, far_ref, sum_s, 1 - lax.axis_index("exp"))
+
+
+def down_mine_kernel(hidden_ref, held_ref, acc_ref, near_ref, far_ref, sum_s):
+    down_piece(hidden_ref[...], held_ref, acc_ref, near_ref, far_ref, sum_s, lax.axis_index("exp"))
+
+
+def reply_kernel(own_ref, peer_ref, first_ref, second_ref, sum_s):
+    odd = lax.axis_index("ctx") % 2
+    sum_s[...] = own_ref[...].astype(f32) + peer_ref[...].astype(f32)
+    count = first_ref.shape[0]
+    for place, ref in ((odd, first_ref), (1 - odd, second_ref)):
+        ref[...] = sum_s[pl.ds(pl.multiple_of(place * count, 8), count), :].astype(bf16)
+
+
+def finish_kernel(
+    s0_ref, s1_ref, s2_ref, s3_ref, slots_ref, weights_ref, r0_ref, r1_ref, r2_ref, r3_ref, out_ref
+):
+    ctx = lax.axis_index("ctx")
+    apart = ctx ^ (lax.axis_index("tp") * lax.axis_size("exp") + lax.axis_index("exp"))
+    tokens = out_ref.shape[0]
+    stream = s0_ref[...]
+    for p, ref in ((1, s1_ref), (2, s2_ref), (3, s3_ref)):
+        stream = jnp.where(apart == p, ref[...], stream)
+    total = stream.astype(f32)
+    over_rows = (((0,), (0,)), ((), ()))
+    want = lax.broadcasted_iota(jnp.int32, (r0_ref.shape[0], tokens), 0).astype(f32)
+    for p, ref in enumerate((r0_ref, r1_ref, r2_ref, r3_ref)):
+        base = ((ctx ^ p) * CAP).astype(f32)
+        weight = jnp.zeros(want.shape, f32)
+        for k in range(2):
+            weight = weight + jnp.where(slots_ref[k : k + 1, :tokens] == want + base, weights_ref[k : k + 1, :], 0.0)
+        high = weight.astype(bf16)
+        low = (weight - high.astype(f32)).astype(bf16)
+        rows = ref[...]
+        total = total + lax.dot_general(high, rows, over_rows, preferred_element_type=f32)
+        total = total + lax.dot_general(low, rows, over_rows, preferred_element_type=f32)
+    out_ref[...] = total.astype(bf16)
+
+
+VM = pl.BlockSpec(memory_space=pltpu.VMEM)
+SM = pl.BlockSpec(memory_space=pltpu.SMEM)
+HB = pl.BlockSpec(memory_space=pltpu.HBM)
+AN = pl.BlockSpec(memory_space=pl.ANY)
+
+
+def call(kernel, out, ins, scratch=(), args=(), limit=8, us=1.0):
+    return pl.pallas_call(
+        kernel, out_shape=out, in_specs=ins, out_specs=jax.tree.map(lambda _: VM, out), scratch_shapes=list(scratch),
+        compiler_params=pltpu.CompilerParams(vmem_limit_bytes=limit * 1024 * 1024),
+        cost_estimate=pl.CostEstimate(flops=0, transcendentals=0, bytes_accessed=int(us * 3.0e6)),
+    )(*args)
+
+
+def shape(rows, cols, kind):
+    return jax.ShapeDtypeStruct((rows, cols), kind)
+
+
+def in_hbm(x):
+    return pltpu.with_memory_space_constraint(x, pltpu.HBM)
+
+
+def in_vmem(x):
+    return pltpu.with_memory_space_constraint(x, pltpu.VMEM)
+
+
+def fast_body(
+    resid, conv_out, gate_z, dt_raw, b_proj, c_proj, a_log, d_skip, out_weight, norm_gain,
+    route_ids, route_weight, w_gate, w_up, w_down,
+):
+    tokens, model_width = resid.shape
+    ctx_count, exp_count, tp_count = (lax.axis_size(a) for a in AXES)
+    ctx = lax.axis_index("ctx")
+    channels = conv_out.shape[1]
+    states = a_log.shape[0]
+    block_cols = out_weight.shape[1]
+    half_width = model_width // tp_count
+    piece_width = half_width // exp_count
+    g = channels // 128
+
+    def number(c, x, t):
+        return (c * exp_count + x) * tp_count + t
+
+    def owner(c):
+        return c // (ctx_count // tp_count)
+
+    chips = [(c, x) for c in range(ctx_count) for x in range(exp_count)]
+    away = range(1, ctx_count)
+
+    def permute(x, pairs):
+        return lax.ppermute(x, AXES, pairs)
+
+    def to_owner(x, p):
+        return permute(x, [(number(c ^ p, e, owner(c)), number(c, e, owner(c))) for c, e in chips])
+
+    def from_owner(x, p):
+        return permute(x, [(number(c, e, owner(c)), number(c ^ p, e, owner(c))) for c, e in chips])
+
+    def swap_tp(x):
+        return lax.ppermute(x, "tp", [(i, tp_count - 1 - i) for i in range(tp_count)])
+
+    peer_weight = swap_tp(out_weight)
+    with jax.named_scope("scan"):
+        flat = shape(tokens * g, 128, f32)
+        b_rows, c_rows = b_proj.T, c_proj.T
+        base, cum, silu_z, rate, pack = call(
+            scan_kernel,
+            (flat, flat, flat, shape(states * g, 128, f32), shape((states + 2) * g, 128, bf16)),
+            [SM, SM] + [VM] * 5,
+            [pltpu.VMEM((tokens * g, 128), f32)] * 3 + [pltpu.VMEM((states * g, 128), f32)],
+            tuple(in_hbm(v) for v in (b_rows, c_rows, dt_raw, conv_out, gate_z, a_log, d_skip.reshape(g, 128))), us=3.0,
+        )
+    with jax.named_scope("relay"):
+        entered = [
+            permute(pack, [(number(c, x, t), number(c ^ p, x, t)) for c, x in chips for t in range(tp_count)])
+            for p in away
+        ]
+    with jax.named_scope("correct"):
+        gated = call(
+            correct_kernel, shape(tokens, channels, bf16), [SM] + [VM] * 7, [pltpu.VMEM((tokens * g, 128), f32)],
+            (in_hbm(c_rows), *entered, base, cum, silu_z, rate), us=2.0,
+        )
+    gated, route_ids, norm_gain = lax.optimization_barrier((gated, route_ids, norm_gain))
+    with jax.named_scope("gather_gated"):
+        peer_gated = swap_tp(gated)
+    with jax.named_scope("route"):
+        ids = route_ids.T
+        slot_lanes, slot_cols = call(
+            route_kernel, (shape(8, 128, f32), shape(tokens, 128, bf16)), [VM], (), (jnp.concatenate([ids, ids], axis=1),)
+        )
+    with jax.named_scope("gather_gated"):
+        message = shape(tokens, 2 * channels + block_cols // 2 + 128, bf16)
+        messages = call(
+            pack_kernel, (message,) * 4, [VM] * 4, (), (gated, peer_gated, in_hbm(resid), slot_cols)
+        )
+        blocks = [messages[0]] + [to_owner(messages[p], p) for p in away]
+
+    def hold_out(after):
+        own_rows, peer_rows, _ = lax.optimization_barrier((out_weight, peer_weight, after))
+        with jax.named_scope("hold_out_weight"):
+            return call(
+                hold_kernel, pltpu.VMEM((2 * own_rows.shape[0], block_cols), bf16), [HB, AN], [pltpu.SemaphoreType.DMA((2,))],
+                (in_hbm(own_rows), peer_rows), us=1.6,
+            )
+
+    held_out = hold_out(messages[0])
+    gain = lax.dynamic_slice_in_dim(norm_gain, ctx * block_cols, block_cols, 0)[None, :]
+
+    streams = []
+    sent = []
+    for group in range(2):
+        with jax.named_scope("project"):
+            own, slots = call(
+                project_kernel, (shape(2 * tokens, block_cols, bf16), shape(2 * tokens, 128, bf16)), [VM] * 3,
+                [pltpu.VMEM((2 * tokens, message.shape[1]), bf16)],
+                (blocks[2 * group], blocks[2 * group + 1], in_vmem(held_out)),
+            )
+        if group == 0:
+            held_out = hold_out(own)
+        with jax.named_scope("sum_exp"):
+            peer = permute(own, [(number(c, x, owner(c)), number(c, 1 - x, owner(c))) for c, x in chips])
+        with jax.named_scope("select"):
+            block = shape(tokens, block_cols, bf16)
+            routed = shape(2 * CAP, block_cols + 128, bf16)
+            first, second, *out = call(
+                select_kernel, (block, block) + (routed,) * 4, [VM] * 4, [pltpu.VMEM((2 * tokens, block_cols), bf16)],
+                (own, peer, slots, gain),
+            )
+            streams += [first, second]
+            if group == 0:
+                *out, blocks[2], blocks[3] = lax.optimization_barrier((*out, blocks[2], blocks[3]))
+        with jax.named_scope("dispatch"):
+            sent.append([out[0]] + [from_owner(out[p], p) for p in away])
+
+    slots_total = EXPERTS * CAP
+    part_width = w_gate.shape[1] // 2
+    wg, wu, wd = (in_hbm(v) for v in (w_gate, w_up, w_down))
+    dma = pltpu.SemaphoreType.DMA
+    with jax.named_scope("hold_weights"):
+        held_kind = pltpu.VMEM((2 * half_width, part_width), bf16)
+        held = call(hold_first_kernel, held_kind, [HB, HB], [dma((2,))], (wg, wu), us=5.8)
+    with jax.named_scope("gate_up"):
+        both = shape(slots_total, 2 * part_width, bf16)
+        first, squares, feats, held = call(
+            first_half_kernel,
+            (both, shape(slots_total, 128, f32), shape(slots_total, half_width, bf16), held_kind),
+            [VM] * 9 + [HB] * 2, [dma((2,))],
+            (*sent[0], *sent[1], in_vmem(held), wg, wu), us=5.8,
+        )
+        peer_squares = swap_tp(squares)
+        peer_first = swap_tp(first)
+        second, held = call(
+            second_half_kernel, (both, pltpu.VMEM(w_down.shape, bf16)), [VM, VM, HB], [dma], (feats, in_vmem(held), wd), us=5.8
+        )
+        peer_second = swap_tp(second)
+    with jax.named_scope("down"):
+        held = in_vmem(held)
+        acc = call(
+            functools.partial(down_first_kernel, model_width), shape(slots_total, half_width, f32), [VM] * 5, (),
+            (first, peer_first, squares, peer_squares, held), us=2.0,
+        )
+        piece = shape(slots_total // 2, piece_width, bf16)
+        total = pltpu.VMEM((slots_total, piece_width), f32)
+        theirs_near, theirs_far, hidden = call(
+            functools.partial(down_theirs_kernel, model_width), (piece, piece, shape(slots_total, part_width, bf16)),
+            [VM] * 6, [total], (second, peer_second, squares, peer_squares, held, acc), us=1.4,
+        )
+    with jax.named_scope("sum_experts"):
+        swap = [(0, 1), (1, 0)]
+        peer_far = lax.ppermute(theirs_far, "exp", swap)
+        theirs_near, _ = lax.optimization_barrier((theirs_near, theirs_far))
+        peer_near = lax.ppermute(theirs_near, "exp", swap)
+        mine_near, mine_far = call(down_mine_kernel, (piece, piece), [VM] * 3, [total], (hidden, held, acc))
+    with jax.named_scope("stream_home"):
+        *streams, mine_far = lax.optimization_barrier((*streams, mine_far))
+        home = [
+            permute(
+                streams[p],
+                [(number(c, c % exp_count, owner(c)), number(c ^ p, c % exp_count, owner(c))) for c in range(ctx_count)],
+            )
+            for p in away
+        ]
+
+    def reply(own, peer):
+        small = shape(CAP, piece_width, bf16)
+        return call(
+            reply_kernel, (small, small), [VM] * 2, [pltpu.VMEM((slots_total // 2, piece_width), f32)], (own, peer)
+        )
+
+    def send(x, p):
+        return permute(x, [(number(c, x_at, t), number(c ^ p, x_at, t)) for c, x_at in chips for t in range(tp_count)])
+
+    with jax.named_scope("reply"):
+        r2, r3 = reply(mine_far, peer_far)
+        far = [send(r2, 2), send(r3, 3)]
+        mine_near, peer_near, _ = lax.optimization_barrier((mine_near, peer_near, r2))
+        r0, r1 = reply(mine_near, peer_near)
+        replies = [r0, send(r1, 1), *far]
+    with jax.named_scope("finish"):
+        return call(
+            finish_kernel, shape(tokens, piece_width, bf16), [VM] * 10, (),
+            (streams[0], *home, slot_lanes, route_weight.T, *replies),
+        )
+
+
 def solution(mesh):
     in_specs = (
         P(("groups", "ctx"), None),
@@ -151,4 +687,7 @@
         P(("ctx", "exp"), "tp"),
     )
     out_specs = P(("groups", "ctx"), ("tp", "exp"))
-    return jax.shard_map(body, mesh=mesh, in_specs=in_specs, out_specs=out_specs, check_vma=False)
+    sizes = dict(mesh.shape)
+    small = (sizes["ctx"], sizes["exp"], sizes["tp"]) == (EXPERTS, 2, 2)
+    chosen = fast_body if small else body
+    return jax.shard_map(chosen, mesh=mesh, in_specs=in_specs, out_specs=out_specs, check_vma=False)

time: 322 us -> 108 us (0.34)
  waiting for transfers between devices: 218 us -> 20.2 us
  matrix products: 37.9 us -> 0 us
  Pallas kernels: 0 us -> 36.2 us
  starting transfers between devices: 19.2 us -> 48.9 us
  blocking collectives: 21.2 us -> 0 us
  between operations: 13.3 us -> 0.35 us
  other arithmetic: 9.74 us -> 0.83 us
    all_gather x1 -> x0, waiting for transfers between devices: 123 us -> none  [body(): lax.all_gather(out_weight, 'ctx', axis=1, tiled=True)]
    psum x2 -> x0, waiting for transfers between devices: 57.4 us -> none  [the longest x1 36.2 us: body(): mamba_out = lax.psum(partial_value, ('exp', 'tp'))]
    dot_general x7 -> x0, matrix products: 37.9 us -> none  [the longest x1 10.6 us: body(): jnp.dot(hidden, w_down, preferred_element_type=jnp.float32)]
    pallas_call x0 -> x19, Pallas kernels: none -> 36.2 us  [call(): pl.pallas_call(kernel, out_shape=out, in_specs=ins, out_specs=jax.tree.ma...]
    ppermute x3 -> x27, starting transfers between devices: 14.3 us -> 48.9 us  [the longest x20 43.8 us: permute(): return lax.ppermute(x, AXES, pairs)]
    all_to_all x1 -> x0, blocking collectives: 21.2 us -> none  [body(): lax.all_to_all(outgoing, 'ctx', split_axis=0, concat_axis=0, tiled=True)]
    all_to_all x1 -> x0, waiting for transfers between devices: 17.6 us -> none  [body(): lax.all_to_all(answer, 'ctx', split_axis=0, concat_axis=0, tiled=True)]
    ppermute x3 -> x27, waiting for transfers between devices: 8.32 us -> 20.2 us  [the longest x20 17.3 us: permute(): return lax.ppermute(x, AXES, pairs)]
  transfers between devices with their start and end apart: 8 -> 27, of which waited for: 8 -> 9; matrix products, arithmetic and copies ran while one was open for 3% -> 1% of each run, Pallas kernels for 0% -> 25%
where the time goes in v2:
time: 108 us; the launch traced here: 107 us
  starting transfers between devices  48.9 us (45%)
  Pallas kernels  36.2 us (34%)
  waiting for transfers between devices  20.2 us (19%)
    ppermute x20, starting transfers between devices, permute(): return lax.ppermute(x, AXES, pairs)  43.8 us
    pallas_call x19, Pallas kernels, call(): pl.pallas_call(kernel, out_shape=out, in_specs=ins, out_specs=jax.tree.ma...  36.2 us
    ppermute x20, waiting for transfers between devices, permute(): return lax.ppermute(x, AXES, pairs)  17.3 us
    ppermute x5, starting transfers between devices, swap_tp(): lax.ppermute(x, 'tp', [(i, tp_count - 1 - i) for i in range(tp_count)])  2.97 us
    ppermute x5, waiting for transfers between devices, swap_tp(): lax.ppermute(x, 'tp', [(i, tp_count - 1 - i) for i in range(tp_count)])  2.94 us
  transfers between devices with their start and end apart: 27, of which 9 were waited for; matrix products, arithmetic and copies ran while one was open for 1% of the time, Pallas kernels for 25%

profile of v2, /device:TPU:0, one launch (start us, length us, event | category | flops | bytes accessed | tf_op | source)
XLA Modules:
  0.0 107.2 jit_solution(6498302236065210493)
XLA Ops:
  0.5 3.1 %scan.1 = (f32[512,128]{1,0:T(8,128)S(1)}, f32[512,128]{1,0:T(8,128)S(1)}, f32[512,128]{1,0:T(8,128)S(1)}, f32[128,128]{1,0:T(8,128)S(1)}, bf16[144,128]{1,0:T(8,128)(2,1)S(1)}) custom-call(f32[16,64]{1,0:T(8,128)} %bitcast.11, f32[16,64]{1,0:T(8,128)} %bitcast.9, f32[64,1024]{1,0:T(8,128)} %dt_ref.1, bf16[64,1024]{1,0:T(8,128)(2,1)} %conv_ref.1, ...), custom_call_target="tpu_custom_call" | custom-call | bytes 9000000 | tf_op jit(solution)/shard_map/scan/pallas_call | solution.py:473
  3.5 4.7 %collective-permute-start.2 = (bf16[144,128]{1,0:T(8,128)(2,1)S(1)}, bf16[144,128]{1,0:T(8,128)(2,1)S(1)}, u32[]{:S(2)}, u32[]{:S(2)}) collective-permute-start(bf16[144,128]{1,0:T(8,128)(2,1)S(1)} %get-tuple-element.68), channel_id=1, source_target_pairs={{0,12},{1,13},{2,14},{3,15},{4,8},{5,9},{6,10},{7,11},{8,4},{9,5},... | collective-permute-start | bytes 110600 | tf_op jit(solution)/shard_map/relay/ppermute | solution.py:516
  8.2 0.6 collective-permute-start
  8.8 1.5 %collective-permute-done.2.three_ref = bf16[144,128]{1,0:T(8,128)(2,1)S(1)} collective-permute-done((bf16[144,128]{1,0:T(8,128)(2,1)S(1)}, bf16[144,128]{1,0:T(8,128)(2,1)S(1)}, u32[]{:S(2)}, u32[]{:S(2)}) %collective-permute-start.2) | collective-permute-done | bytes 36896 | tf_op jit(solution)/shard_map/relay/ppermute | solution.py:516
  10.4 2.7 %collective-permute-done.1.two_ref = bf16[144,128]{1,0:T(8,128)(2,1)S(1)} collective-permute-done((bf16[144,128]{1,0:T(8,128)(2,1)S(1)}, bf16[144,128]{1,0:T(8,128)(2,1)S(1)}, u32[]{:S(2)}, u32[]{:S(2)}) %collective-permute-start.1) | collective-permute-done | bytes 36896 | tf_op jit(solution)/shard_map/relay/ppermute | solution.py:516
  13.1 2.1 %correct.1.own_ref = bf16[64,1024]{1,0:T(8,128)(2,1)S(1)} custom-call(f32[16,64]{1,0:T(8,128)} %bitcast.10, bf16[144,128]{1,0:T(8,128)(2,1)S(1)} %collective-permute-done.one_ref, bf16[144,128]{1,0:T(8,128)(2,1)S(1)} %collective-permute-done.1.two_ref, bf16[144,128]{1,0:T(8,128)(2,1)S(1)} %collective-permute-done.2.three_ref, ...), custom_call_target="tpu_custom_call" | custom-call | bytes 6000000 | tf_op jit(solution)/shard_map/correct/pallas_call | solution.py:473
  15.3 0.8 pad_add_fusion.ids_ref
  16.6 2.0 %gather_gated.1 = (bf16[64,2688]{1,0:T(8,128)(2,1)S(1)}, bf16[64,2688]{1,0:T(8,128)(2,1)S(1)}, bf16[64,2688]{1,0:T(8,128)(2,1)}, bf16[64,2688]{1,0:T(8,128)(2,1)}) custom-call(bf16[64,1024]{1,0:T(8,128)(2,1)S(1)} %correct.1.own_ref, bf16[64,1024]{1,0:T(8,128)(2,1)S(1)} %collective-permute-done.3.peer_ref, bf16[64,4096]{1,0:T(8,128)(2,1)} %resid_ref.1, ...), custom_call_target="tpu_custom_call" | custom-call | bytes 3000000 | tf_op jit(solution)/shard_map/gather_gated/pallas_call | solution.py:473
  18.6 2.5 %collective-permute-start.4 = (bf16[64,2688]{1,0:T(8,128)(2,1)S(1)}, bf16[64,2688]{1,0:T(8,128)(2,1)S(1)}, u32[]{:S(2)}, u32[]{:S(2)}) collective-permute-start(bf16[64,2688]{1,0:T(8,128)(2,1)S(1)} %get-tuple-element.77), channel_id=1, source_target_pairs={{4,0},{6,2},{0,4},{2,6},{13,9},{15,11},{9,13},{11,15},{20,16},{22,... | collective-permute-start | bytes 1032200 | tf_op jit(solution)/shard_map/gather_gated/ppermute | solution.py:516
  21.1 1.3 %collective-permute-start.7 = (bf16[64,2688]{1,0:T(8,128)(2,1)}, bf16[64,2688]{1,0:T(8,128)(2,1)S(1)}, u32[]{:S(2)}, u32[]{:S(2)}) collective-permute-start(bf16[64,2688]{1,0:T(8,128)(2,1)} %get-tuple-element.89), channel_id=1, source_target_pairs={{8,0},{10,2},{12,4},{14,6},{1,9},{3,11},{5,13},{7,15},{24,16},{26,... | collective-permute-start | bytes 1032200 | tf_op jit(solution)/shard_map/gather_gated/ppermute | solution.py:516
  22.4 1.3 %collective-permute-start.8 = (bf16[64,2688]{1,0:T(8,128)(2,1)}, bf16[64,2688]{1,0:T(8,128)(2,1)S(1)}, u32[]{:S(2)}, u32[]{:S(2)}) collective-permute-start(bf16[64,2688]{1,0:T(8,128)(2,1)} %get-tuple-element.90), channel_id=1, source_target_pairs={{12,0},{14,2},{8,4},{10,6},{5,9},{7,11},{1,13},{3,15},{28,16},{30,... | collective-permute-start | bytes 1032200 | tf_op jit(solution)/shard_map/gather_gated/ppermute | solution.py:516
  23.7 1.6 %hold_out_weight.2.w_ref = bf16[2048,1024]{1,0:T(8,128)(2,1)S(1)} custom-call(bf16[1024,1024]{1,0:T(8,128)(2,1)} %own_ref.1, bf16[1024,1024]{1,0:T(8,128)(2,1)S(1)} %collective-permute-done.5.peer_ref), custom_call_target="tpu_custom_call" | custom-call | bytes 4800000 | tf_op jit(solution)/shard_map/hold_out_weight/pallas_call | solution.py:473
  25.4 2.4 %collective-permute-done.4.second_ref = bf16[64,2688]{1,0:T(8,128)(2,1)S(1)} collective-permute-done((bf16[64,2688]{1,0:T(8,128)(2,1)S(1)}, bf16[64,2688]{1,0:T(8,128)(2,1)S(1)}, u32[]{:S(2)}, u32[]{:S(2)}) %collective-permute-start.4) | collective-permute-done | bytes 344096 | tf_op jit(solution)/shard_map/gather_gated/ppermute | solution.py:516
  27.8 0.8 project.2
  28.6 3.4 %collective-permute-start.6 = (bf16[128,1024]{1,0:T(8,128)(2,1)S(1)}, bf16[128,1024]{1,0:T(8,128)(2,1)S(1)}, u32[]{:S(2)}, u32[]{:S(2)}) collective-permute-start(bf16[128,1024]{1,0:T(8,128)(2,1)S(1)} %get-tuple-element.80.own_ref), channel_id=1, source_target_pairs={{0,2},{2,0},{4,6},{6,4},{9,11},{11,9},{13,15},{15,13},{16,18},{18,... | collective-permute-start | bytes 786440 | tf_op jit(solution)/shard_map/sum_exp/ppermute | solution.py:516
  32.0 0.7 dynamic_slice.3
  32.7 1.6 %hold_out_weight.3.w_ref = bf16[2048,1024]{1,0:T(8,128)(2,1)S(1)} custom-call(bf16[1024,1024]{1,0:T(8,128)(2,1)} %own_ref.1, bf16[1024,1024]{1,0:T(8,128)(2,1)S(1)} %collective-permute-done.5.peer_ref), custom_call_target="tpu_custom_call" | custom-call | bytes 4800000 | tf_op jit(solution)/shard_map/hold_out_weight/pallas_call | solution.py:473
  34.3 2.5 %collective-permute-done.6.peer_ref = bf16[128,1024]{1,0:T(8,128)(2,1)S(1)} collective-permute-done((bf16[128,1024]{1,0:T(8,128)(2,1)S(1)}, bf16[128,1024]{1,0:T(8,128)(2,1)S(1)}, u32[]{:S(2)}, u32[]{:S(2)}) %collective-permute-start.6) | collective-permute-done | bytes 262176 | tf_op jit(solution)/shard_map/sum_exp/ppermute | solution.py:516
  36.8 0.5 select.2
  37.4 1.4 %collective-permute-done.7.first_ref = bf16[64,2688]{1,0:T(8,128)(2,1)S(1)} collective-permute-done((bf16[64,2688]{1,0:T(8,128)(2,1)}, bf16[64,2688]{1,0:T(8,128)(2,1)S(1)}, u32[]{:S(2)}, u32[]{:S(2)}) %collective-permute-start.7) | collective-permute-done | bytes 344096 | tf_op jit(solution)/shard_map/gather_gated/ppermute | solution.py:516
  38.8 0.8 project.3
  39.6 3.4 %collective-permute-start.9 = (bf16[128,1024]{1,0:T(8,128)(2,1)S(1)}, bf16[128,1024]{1,0:T(8,128)(2,1)S(1)}, u32[]{:S(2)}, u32[]{:S(2)}) collective-permute-start(bf16[128,1024]{1,0:T(8,128)(2,1)S(1)} %get-tuple-element.95.own_ref), channel_id=1, source_target_pairs={{0,2},{2,0},{4,6},{6,4},{9,11},{11,9},{13,15},{15,13},{16,18},{18,... | collective-permute-start | bytes 786440 | tf_op jit(solution)/shard_map/sum_exp/ppermute | solution.py:516
  43.0 6.2 %collective-permute-start.10 = (bf16[80,1152]{1,0:T(8,128)(2,1)S(1)}, bf16[80,1152]{1,0:T(8,128)(2,1)S(1)}, u32[]{:S(2)}, u32[]{:S(2)}) collective-permute-start(bf16[80,1152]{1,0:T(8,128)(2,1)S(1)} %get-tuple-element.100), channel_id=1, source_target_pairs={{0,4},{2,6},{4,0},{6,2},{9,13},{11,15},{13,9},{15,11},{16,20},{18,... | collective-permute-start | bytes 552968 | tf_op jit(solution)/shard_map/dispatch/ppermute | solution.py:516
  49.2 1.3 %collective-permute-start.11 = (bf16[80,1152]{1,0:T(8,128)(2,1)S(1)}, bf16[80,1152]{1,0:T(8,128)(2,1)S(1)}, u32[]{:S(2)}, u32[]{:S(2)}) collective-permute-start(bf16[80,1152]{1,0:T(8,128)(2,1)S(1)} %get-tuple-element.101), channel_id=1, source_target_pairs={{0,8},{2,10},{4,12},{6,14},{9,1},{11,3},{13,5},{15,7},{16,24},{18,... | collective-permute-start | bytes 552968 | tf_op jit(solution)/shard_map/dispatch/ppermute | solution.py:516
  50.5 1.3 %collective-permute-start.12 = (bf16[80,1152]{1,0:T(8,128)(2,1)S(1)}, bf16[80,1152]{1,0:T(8,128)(2,1)S(1)}, u32[]{:S(2)}, u32[]{:S(2)}) collective-permute-start(bf16[80,1152]{1,0:T(8,128)(2,1)S(1)} %get-tuple-element.102), channel_id=1, source_target_pairs={{0,12},{2,14},{4,8},{6,10},{9,5},{11,7},{13,1},{15,3},{16,28},{18,... | collective-permute-start | bytes 552968 | tf_op jit(solution)/shard_map/dispatch/ppermute | solution.py:516
  51.8 0.5 select.3
  52.3 2.2 %collective-permute-start.13 = (bf16[80,1152]{1,0:T(8,128)(2,1)S(1)}, bf16[80,1152]{1,0:T(8,128)(2,1)S(1)}, u32[]{:S(2)}, u32[]{:S(2)}) collective-permute-start(bf16[80,1152]{1,0:T(8,128)(2,1)S(1)} %get-tuple-element.104), channel_id=1, source_target_pairs={{0,4},{2,6},{4,0},{6,2},{9,13},{11,15},{13,9},{15,11},{16,20},{18,... | collective-permute-start | bytes 552968 | tf_op jit(solution)/shard_map/dispatch/ppermute | solution.py:516
  54.5 1.3 %collective-permute-start.14 = (bf16[80,1152]{1,0:T(8,128)(2,1)S(1)}, bf16[80,1152]{1,0:T(8,128)(2,1)S(1)}, u32[]{:S(2)}, u32[]{:S(2)}) collective-permute-start(bf16[80,1152]{1,0:T(8,128)(2,1)S(1)} %get-tuple-element.105), channel_id=1, source_target_pairs={{0,8},{2,10},{4,12},{6,14},{9,1},{11,3},{13,5},{15,7},{16,24},{18,... | collective-permute-start | bytes 552968 | tf_op jit(solution)/shard_map/dispatch/ppermute | solution.py:516
  55.8 1.3 %collective-permute-start.15 = (bf16[80,1152]{1,0:T(8,128)(2,1)S(1)}, bf16[80,1152]{1,0:T(8,128)(2,1)S(1)}, u32[]{:S(2)}, u32[]{:S(2)}) collective-permute-start(bf16[80,1152]{1,0:T(8,128)(2,1)S(1)} %get-tuple-element.106), channel_id=1, source_target_pairs={{0,12},{2,14},{4,8},{6,10},{9,5},{11,7},{13,1},{15,3},{16,28},{18,... | collective-permute-start | bytes 552968 | tf_op jit(solution)/shard_map/dispatch/ppermute | solution.py:516
  57.1 5.8 %hold_weights.1.held_ref = bf16[4096,2048]{1,0:T(8,128)(2,1)S(1)} custom-call(bf16[2048,4096]{1,0:T(8,128)(2,1)} %wg_ref.3, bf16[2048,4096]{1,0:T(8,128)(2,1)} %wu_ref.3), custom_call_target="tpu_custom_call" | custom-call | bytes 17400000 | tf_op jit(solution)/shard_map/hold_weights/pallas_call | solution.py:473
  63.0 5.8 %gate_up.2 = (bf16[160,4096]{1,0:T(8,128)(2,1)S(1)}, f32[160,128]{1,0:T(8,128)S(1)}, bf16[160,2048]{1,0:T(8,128)(2,1)S(1)}, bf16[4096,2048]{1,0:T(8,128)(2,1)S(1)}) custom-call(bf16[80,1152]{1,0:T(8,128)(2,1)S(1)} %get-tuple-element.99.a0_ref, bf16[80,1152]{1,0:T(8,128)(2,1)S(1)} %collective-permute-done.10.a1_ref, ...), custom_call_target="tpu_custom_call" | custom-call | bytes 17400000 | tf_op jit(solution)/shard_map/gate_up/pallas_call | solution.py:473
  68.8 1.9 %collective-permute-start.18 = (bf16[160,4096]{1,0:T(8,128)(2,1)S(1)}, bf16[160,4096]{1,0:T(8,128)(2,1)S(1)}, u32[]{:S(2)}, u32[]{:S(2)}) collective-permute-start(bf16[160,4096]{1,0:T(8,128)(2,1)S(1)} %get-tuple-element.112.own_ref), channel_id=1, source_target_pairs={{0,1},{1,0},{2,3},{3,2},{4,5},{5,4},{6,7},{7,6},{8,9},{9,8},{10,11... | collective-permute-start | bytes 3932168 | tf_op jit(solution)/shard_map/gate_up/ppermute | solution.py:525
  70.7 5.8 %gate_up.3 = (bf16[160,4096]{1,0:T(8,128)(2,1)S(1)}, bf16[4096,2048]{1,0:T(8,128)(2,1)S(1)}) custom-call(bf16[160,2048]{1,0:T(8,128)(2,1)S(1)} %get-tuple-element.107.feats_ref, bf16[4096,2048]{1,0:T(8,128)(2,1)S(1)} %get-tuple-element.108.held_ref, bf16[4096,2048]{1,0:T(8,128)(2,1)} %wd_ref.1), custom_call_target="tpu_custom_call" | custom-call | bytes 17400000 | tf_op jit(solution)/shard_map/gate_up/pallas_call | solution.py:473
  76.5 0.5 collective-permute-start.17
  77.0 2.6 %collective-permute-done.17.sq1 = f32[160,128]{1,0:T(8,128)S(1)} collective-permute-done((f32[160,128]{1,0:T(8,128)S(1)}, f32[160,128]{1,0:T(8,128)S(1)}, u32[]{:S(2)}, u32[]{:S(2)}) %collective-permute-start.17) | collective-permute-done | bytes 81952 | tf_op jit(solution)/shard_map/gate_up/ppermute | solution.py:525
  79.7 2.0 %down.2.acc_ref = f32[160,2048]{1,0:T(8,128)S(1)} custom-call(bf16[160,4096]{1,0:T(8,128)(2,1)S(1)} %get-tuple-element.112.own_ref, bf16[160,4096]{1,0:T(8,128)(2,1)S(1)} %collective-permute-done.18.peer_ref, f32[160,128]{1,0:T(8,128)S(1)} %get-tuple-element.110.sq0, f32[160,128]{1,0:T(8,128)S(1)} %collective-permute-done.17.sq1, ...), custom_call_target="tpu_custom_call" | custom-call | bytes 6000000 | tf_op jit(solution)/shard_map/down/pallas_call | solution.py:473
  81.7 1.4 %down.3 = (bf16[80,1024]{1,0:T(8,128)(2,1)S(1)}, bf16[80,1024]{1,0:T(8,128)(2,1)S(1)}, bf16[160,2048]{1,0:T(8,128)(2,1)S(1)}) custom-call(bf16[160,4096]{1,0:T(8,128)(2,1)S(1)} %get-tuple-element.109.own_ref, bf16[160,4096]{1,0:T(8,128)(2,1)S(1)} %collective-permute-done.16.peer_ref, f32[160,128]{1,0:T(8,128)S(1)} %get-tuple-element.110.sq0, ...), custom_call_target="tpu_custom_call" | custom-call | bytes 4200000 | tf_op jit(solution)/shard_map/down/pallas_call | solution.py:473
  83.1 0.5 collective-permute-start.23
  83.7 1.5 %collective-permute-start.22 = (bf16[80,1024]{1,0:T(8,128)(2,1)S(1)}, bf16[80,1024]{1,0:T(8,128)(2,1)S(1)}, u32[]{:S(2)}, u32[]{:S(2)}) collective-permute-start(bf16[80,1024]{1,0:T(8,128)(2,1)S(1)} %get-tuple-element.123), channel_id=1, source_target_pairs={{0,2},{2,0},{1,3},{3,1},{4,6},{6,4},{5,7},{7,5},{8,10},{10,8},{9,1... | collective-permute-start | bytes 491528 | tf_op jit(solution)/shard_map/sum_experts/ppermute | solution.py:637
  85.2 0.9 sum_experts.1
  86.1 4.6 %collective-permute-start.19 = (bf16[64,1024]{1,0:T(8,128)(2,1)S(1)}, bf16[64,1024]{1,0:T(8,128)(2,1)S(1)}, u32[]{:S(2)}, u32[]{:S(2)}) collective-permute-start(bf16[64,1024]{1,0:T(8,128)(2,1)S(1)} %get-tuple-element.116), channel_id=1, source_target_pairs={{0,4},{6,2},{9,13},{15,11},{16,20},{22,18},{25,29},{31,27}} | collective-permute-start | bytes 393224 | tf_op jit(solution)/shard_map/stream_home/ppermute | solution.py:516
  90.7 2.6 %collective-permute-start.20 = (bf16[64,1024]{1,0:T(8,128)(2,1)S(1)}, bf16[64,1024]{1,0:T(8,128)(2,1)S(1)}, u32[]{:S(2)}, u32[]{:S(2)}) collective-permute-start(bf16[64,1024]{1,0:T(8,128)(2,1)S(1)} %get-tuple-element.117), channel_id=1, source_target_pairs={{0,8},{6,14},{9,1},{15,7},{16,24},{22,30},{25,17},{31,23}} | collective-permute-start | bytes 393224 | tf_op jit(solution)/shard_map/stream_home/ppermute | solution.py:516
  93.3 1.3 %collective-permute-start.21 = (bf16[64,1024]{1,0:T(8,128)(2,1)S(1)}, bf16[64,1024]{1,0:T(8,128)(2,1)S(1)}, u32[]{:S(2)}, u32[]{:S(2)}) collective-permute-start(bf16[64,1024]{1,0:T(8,128)(2,1)S(1)} %get-tuple-element.118), channel_id=1, source_target_pairs={{0,12},{6,10},{9,5},{15,3},{16,28},{22,26},{25,21},{31,19}} | collective-permute-start | bytes 393224 | tf_op jit(solution)/shard_map/stream_home/ppermute | solution.py:516
  94.8 1.2 %collective-permute-start.24 = (bf16[40,1024]{1,0:T(8,128)(2,1)S(1)}, bf16[40,1024]{1,0:T(8,128)(2,1)S(1)}, u32[]{:S(2)}, u32[]{:S(2)}) collective-permute-start(bf16[40,1024]{1,0:T(8,128)(2,1)S(1)} %get-tuple-element.129), channel_id=1, source_target_pairs={{0,4},{1,5},{2,6},{3,7},{4,0},{5,1},{6,2},{7,3},{8,12},{9,13},{10,... | collective-permute-start | bytes 245768 | tf_op jit(solution)/shard_map/reply/ppermute | solution.py:516
  96.0 3.4 %collective-permute-start.26 = (bf16[40,1024]{1,0:T(8,128)(2,1)S(1)}, bf16[40,1024]{1,0:T(8,128)(2,1)S(1)}, u32[]{:S(2)}, u32[]{:S(2)}) collective-permute-start(bf16[40,1024]{1,0:T(8,128)(2,1)S(1)} %get-tuple-element.130), channel_id=1, source_target_pairs={{0,12},{1,13},{2,14},{3,15},{4,8},{5,9},{6,10},{7,11},{8,4},{9,5},... | collective-permute-start | bytes 245768 | tf_op jit(solution)/shard_map/reply/ppermute | solution.py:516
  99.4 4.5 %collective-permute-done.26.r3_ref = bf16[40,1024]{1,0:T(8,128)(2,1)S(1)} collective-permute-done((bf16[40,1024]{1,0:T(8,128)(2,1)S(1)}, bf16[40,1024]{1,0:T(8,128)(2,1)S(1)}, u32[]{:S(2)}, u32[]{:S(2)}) %collective-permute-start.26) | collective-permute-done | bytes 81952 | tf_op jit(solution)/shard_map/reply/ppermute | solution.py:516
  103.9 2.2 %collective-permute-done.25.r2_ref = bf16[40,1024]{1,0:T(8,128)(2,1)S(1)} collective-permute-done((bf16[40,1024]{1,0:T(8,128)(2,1)S(1)}, bf16[40,1024]{1,0:T(8,128)(2,1)S(1)}, u32[]{:S(2)}, u32[]{:S(2)}) %collective-permute-start.25) | collective-permute-done | bytes 81952 | tf_op jit(solution)/shard_map/reply/ppermute | solution.py:516
  106.1 1.1 %finish.1 = bf16[64,1024]{1,0:T(8,128)(2,1)} custom-call(bf16[64,1024]{1,0:T(8,128)(2,1)S(1)} %get-tuple-element.115.s0_ref, bf16[64,1024]{1,0:T(8,128)(2,1)S(1)} %collective-permute-done.19.s1_ref, bf16[64,1024]{1,0:T(8,128)(2,1)S(1)} %collective-permute-done.20.s2_ref, bf16[64,1024]{1,0:T(8,128)(2,1)S(1)} %collective-permute-done.21.s3_ref, ...), custom_call_target="tpu_custom_call" | custom-call | bytes 3000000 | tf_op jit(solution)/shard_map/finish/pallas_call | solution.py:473
  (29 shorter events, 1.3 us)
Async XLA Ops:
  0.0 23.7 %collective-permute-start.5 = (bf16[1024,1024]{1,0:T(8,128)(2,1)}, bf16[1024,1024]{1,0:T(8,128)(2,1)S(1)}, u32[]{:S(2)}, u32[]{:S(2)}) collective-permute-start(bf16[1024,1024]{1,0:T(8,128)(2,1)} %own_ref.1), channel_id=1, source_target_pairs={{0,1},{1,0},{2,3},{3,2},{4,5},{5,4},{6,7},{7,6},{8,9},{9,8},{10,11... | collective-permute-start | bytes 6291464 | tf_op jit(solution)/shard_map/ppermute | solution.py:525
  3.5 6.8 %collective-permute-start.2 = (bf16[144,128]{1,0:T(8,128)(2,1)S(1)}, bf16[144,128]{1,0:T(8,128)(2,1)S(1)}, u32[]{:S(2)}, u32[]{:S(2)}) collective-permute-start(bf16[144,128]{1,0:T(8,128)(2,1)S(1)} %get-tuple-element.68), channel_id=1, source_target_pairs={{0,12},{1,13},{2,14},{3,15},{4,8},{5,9},{6,10},{7,11},{8,4},{9,5},... | collective-permute-start | bytes 110600 | tf_op jit(solution)/shard_map/relay/ppermute | solution.py:516
  8.2 4.9 %collective-permute-start.1 = (bf16[144,128]{1,0:T(8,128)(2,1)S(1)}, bf16[144,128]{1,0:T(8,128)(2,1)S(1)}, u32[]{:S(2)}, u32[]{:S(2)}) collective-permute-start(bf16[144,128]{1,0:T(8,128)(2,1)S(1)} %get-tuple-element.68), channel_id=1, source_target_pairs={{0,8},{1,9},{2,10},{3,11},{4,12},{5,13},{6,14},{7,15},{8,0},{9,1},... | collective-permute-start | bytes 110600 | tf_op jit(solution)/shard_map/relay/ppermute | solution.py:516
  8.2 4.9 %collective-permute-start = (bf16[144,128]{1,0:T(8,128)(2,1)S(1)}, bf16[144,128]{1,0:T(8,128)(2,1)S(1)}, u32[]{:S(2)}, u32[]{:S(2)}) collective-permute-start(bf16[144,128]{1,0:T(8,128)(2,1)S(1)} %get-tuple-element.68), channel_id=1, source_target_pairs={{0,4},{1,5},{2,6},{3,7},{4,0},{5,1},{6,2},{7,3},{8,12},{9,13},{10,... | collective-permute-start | bytes 110600 | tf_op jit(solution)/shard_map/relay/ppermute | solution.py:516
  15.2 1.4 %collective-permute-start.3 = (bf16[64,1024]{1,0:T(8,128)(2,1)S(1)}, bf16[64,1024]{1,0:T(8,128)(2,1)S(1)}, u32[]{:S(2)}, u32[]{:S(2)}) collective-permute-start(bf16[64,1024]{1,0:T(8,128)(2,1)S(1)} %correct.1.own_ref), channel_id=1, source_target_pairs={{0,1},{1,0},{2,3},{3,2},{4,5},{5,4},{6,7},{7,6},{8,9},{9,8},{10,11... | collective-permute-start | bytes 393224 | tf_op jit(solution)/shard_map/gather_gated/ppermute | solution.py:525
  18.6 9.1 %collective-permute-start.4 = (bf16[64,2688]{1,0:T(8,128)(2,1)S(1)}, bf16[64,2688]{1,0:T(8,128)(2,1)S(1)}, u32[]{:S(2)}, u32[]{:S(2)}) collective-permute-start(bf16[64,2688]{1,0:T(8,128)(2,1)S(1)} %get-tuple-element.77), channel_id=1, source_target_pairs={{4,0},{6,2},{0,4},{2,6},{13,9},{15,11},{9,13},{11,15},{20,16},{22,... | collective-permute-start | bytes 1032200 | tf_op jit(solution)/shard_map/gather_gated/ppermute | solution.py:516
  21.1 17.6 %collective-permute-start.7 = (bf16[64,2688]{1,0:T(8,128)(2,1)}, bf16[64,2688]{1,0:T(8,128)(2,1)S(1)}, u32[]{:S(2)}, u32[]{:S(2)}) collective-permute-start(bf16[64,2688]{1,0:T(8,128)(2,1)} %get-tuple-element.89), channel_id=1, source_target_pairs={{8,0},{10,2},{12,4},{14,6},{1,9},{3,11},{5,13},{7,15},{24,16},{26,... | collective-permute-start | bytes 1032200 | tf_op jit(solution)/shard_map/gather_gated/ppermute | solution.py:516
  22.4 16.3 %collective-permute-start.8 = (bf16[64,2688]{1,0:T(8,128)(2,1)}, bf16[64,2688]{1,0:T(8,128)(2,1)S(1)}, u32[]{:S(2)}, u32[]{:S(2)}) collective-permute-start(bf16[64,2688]{1,0:T(8,128)(2,1)} %get-tuple-element.90), channel_id=1, source_target_pairs={{12,0},{14,2},{8,4},{10,6},{5,9},{7,11},{1,13},{3,15},{28,16},{30,... | collective-permute-start | bytes 1032200 | tf_op jit(solution)/shard_map/gather_gated/ppermute | solution.py:516
  28.6 8.3 %collective-permute-start.6 = (bf16[128,1024]{1,0:T(8,128)(2,1)S(1)}, bf16[128,1024]{1,0:T(8,128)(2,1)S(1)}, u32[]{:S(2)}, u32[]{:S(2)}) collective-permute-start(bf16[128,1024]{1,0:T(8,128)(2,1)S(1)} %get-tuple-element.80.own_ref), channel_id=1, source_target_pairs={{0,2},{2,0},{4,6},{6,4},{9,11},{11,9},{13,15},{15,13},{16,18},{18,... | collective-permute-start | bytes 786440 | tf_op jit(solution)/shard_map/sum_exp/ppermute | solution.py:516
  39.6 12.2 %collective-permute-start.9 = (bf16[128,1024]{1,0:T(8,128)(2,1)S(1)}, bf16[128,1024]{1,0:T(8,128)(2,1)S(1)}, u32[]{:S(2)}, u32[]{:S(2)}) collective-permute-start(bf16[128,1024]{1,0:T(8,128)(2,1)S(1)} %get-tuple-element.95.own_ref), channel_id=1, source_target_pairs={{0,2},{2,0},{4,6},{6,4},{9,11},{11,9},{13,15},{15,13},{16,18},{18,... | collective-permute-start | bytes 786440 | tf_op jit(solution)/shard_map/sum_exp/ppermute | solution.py:516
  43.0 12.8 %collective-permute-start.10 = (bf16[80,1152]{1,0:T(8,128)(2,1)S(1)}, bf16[80,1152]{1,0:T(8,128)(2,1)S(1)}, u32[]{:S(2)}, u32[]{:S(2)}) collective-permute-start(bf16[80,1152]{1,0:T(8,128)(2,1)S(1)} %get-tuple-element.100), channel_id=1, source_target_pairs={{0,4},{2,6},{4,0},{6,2},{9,13},{11,15},{13,9},{15,11},{16,20},{18,... | collective-permute-start | bytes 552968 | tf_op jit(solution)/shard_map/dispatch/ppermute | solution.py:516
  49.2 13.8 %collective-permute-start.11 = (bf16[80,1152]{1,0:T(8,128)(2,1)S(1)}, bf16[80,1152]{1,0:T(8,128)(2,1)S(1)}, u32[]{:S(2)}, u32[]{:S(2)}) collective-permute-start(bf16[80,1152]{1,0:T(8,128)(2,1)S(1)} %get-tuple-element.101), channel_id=1, source_target_pairs={{0,8},{2,10},{4,12},{6,14},{9,1},{11,3},{13,5},{15,7},{16,24},{18,... | collective-permute-start | bytes 552968 | tf_op jit(solution)/shard_map/dispatch/ppermute | solution.py:516
  50.5 12.5 %collective-permute-start.12 = (bf16[80,1152]{1,0:T(8,128)(2,1)S(1)}, bf16[80,1152]{1,0:T(8,128)(2,1)S(1)}, u32[]{:S(2)}, u32[]{:S(2)}) collective-permute-start(bf16[80,1152]{1,0:T(8,128)(2,1)S(1)} %get-tuple-element.102), channel_id=1, source_target_pairs={{0,12},{2,14},{4,8},{6,10},{9,5},{11,7},{13,1},{15,3},{16,28},{18,... | collective-permute-start | bytes 552968 | tf_op jit(solution)/shard_map/dispatch/ppermute | solution.py:516
  52.3 10.6 %collective-permute-start.13 = (bf16[80,1152]{1,0:T(8,128)(2,1)S(1)}, bf16[80,1152]{1,0:T(8,128)(2,1)S(1)}, u32[]{:S(2)}, u32[]{:S(2)}) collective-permute-start(bf16[80,1152]{1,0:T(8,128)(2,1)S(1)} %get-tuple-element.104), channel_id=1, source_target_pairs={{0,4},{2,6},{4,0},{6,2},{9,13},{11,15},{13,9},{15,11},{16,20},{18,... | collective-permute-start | bytes 552968 | tf_op jit(solution)/shard_map/dispatch/ppermute | solution.py:516
  54.5 8.5 %collective-permute-start.14 = (bf16[80,1152]{1,0:T(8,128)(2,1)S(1)}, bf16[80,1152]{1,0:T(8,128)(2,1)S(1)}, u32[]{:S(2)}, u32[]{:S(2)}) collective-permute-start(bf16[80,1152]{1,0:T(8,128)(2,1)S(1)} %get-tuple-element.105), channel_id=1, source_target_pairs={{0,8},{2,10},{4,12},{6,14},{9,1},{11,3},{13,5},{15,7},{16,24},{18,... | collective-permute-start | bytes 552968 | tf_op jit(solution)/shard_map/dispatch/ppermute | solution.py:516
  55.8 7.2 %collective-permute-start.15 = (bf16[80,1152]{1,0:T(8,128)(2,1)S(1)}, bf16[80,1152]{1,0:T(8,128)(2,1)S(1)}, u32[]{:S(2)}, u32[]{:S(2)}) collective-permute-start(bf16[80,1152]{1,0:T(8,128)(2,1)S(1)} %get-tuple-element.106), channel_id=1, source_target_pairs={{0,12},{2,14},{4,8},{6,10},{9,5},{11,7},{13,1},{15,3},{16,28},{18,... | collective-permute-start | bytes 552968 | tf_op jit(solution)/shard_map/dispatch/ppermute | solution.py:516
  68.8 10.9 %collective-permute-start.18 = (bf16[160,4096]{1,0:T(8,128)(2,1)S(1)}, bf16[160,4096]{1,0:T(8,128)(2,1)S(1)}, u32[]{:S(2)}, u32[]{:S(2)}) collective-permute-start(bf16[160,4096]{1,0:T(8,128)(2,1)S(1)} %get-tuple-element.112.own_ref), channel_id=1, source_target_pairs={{0,1},{1,0},{2,3},{3,2},{4,5},{5,4},{6,7},{7,6},{8,9},{9,8},{10,11... | collective-permute-start | bytes 3932168 | tf_op jit(solution)/shard_map/gate_up/ppermute | solution.py:525
  76.5 5.2 %collective-permute-start.16 = (bf16[160,4096]{1,0:T(8,128)(2,1)S(1)}, bf16[160,4096]{1,0:T(8,128)(2,1)S(1)}, u32[]{:S(2)}, u32[]{:S(2)}) collective-permute-start(bf16[160,4096]{1,0:T(8,128)(2,1)S(1)} %get-tuple-element.109.own_ref), channel_id=1, source_target_pairs={{0,1},{1,0},{2,3},{3,2},{4,5},{5,4},{6,7},{7,6},{8,9},{9,8},{10,11... | collective-permute-start | bytes 3932168 | tf_op jit(solution)/shard_map/gate_up/ppermute | solution.py:525
  76.5 3.1 %collective-permute-start.17 = (f32[160,128]{1,0:T(8,128)S(1)}, f32[160,128]{1,0:T(8,128)S(1)}, u32[]{:S(2)}, u32[]{:S(2)}) collective-permute-start(f32[160,128]{1,0:T(8,128)S(1)} %get-tuple-element.110.sq0), channel_id=1, source_target_pairs={{0,1},{1,0},{2,3},{3,2},{4,5},{5,4},{6,7},{7,6},{8,9},{9,8},{10,11... | collective-permute-start | bytes 245768 | tf_op jit(solution)/shard_map/gate_up/ppermute | solution.py:525
  83.1 11.5 %collective-permute-start.23 = (bf16[80,1024]{1,0:T(8,128)(2,1)S(1)}, bf16[80,1024]{1,0:T(8,128)(2,1)S(1)}, u32[]{:S(2)}, u32[]{:S(2)}) collective-permute-start(bf16[80,1024]{1,0:T(8,128)(2,1)S(1)} %get-tuple-element.122), channel_id=1, source_target_pairs={{0,2},{2,0},{1,3},{3,1},{4,6},{6,4},{5,7},{7,5},{8,10},{10,8},{9,1... | collective-permute-start | bytes 491528 | tf_op jit(solution)/shard_map/sum_experts/ppermute | solution.py:635
  83.7 11.0 %collective-permute-start.22 = (bf16[80,1024]{1,0:T(8,128)(2,1)S(1)}, bf16[80,1024]{1,0:T(8,128)(2,1)S(1)}, u32[]{:S(2)}, u32[]{:S(2)}) collective-permute-start(bf16[80,1024]{1,0:T(8,128)(2,1)S(1)} %get-tuple-element.123), channel_id=1, source_target_pairs={{0,2},{2,0},{1,3},{3,1},{4,6},{6,4},{5,7},{7,5},{8,10},{10,8},{9,1... | collective-permute-start | bytes 491528 | tf_op jit(solution)/shard_map/sum_experts/ppermute | solution.py:637
  85.2 20.9 %copy-start = (f32[64,2]{0,1:T(2,128)S(1)}, f32[64,2]{0,1:T(2,128)}, u32[]{:S(2)}) copy-start(f32[64,2]{0,1:T(2,128)} %param.26) | copy-start | bytes 1540
  86.1 13.3 %collective-permute-start.19 = (bf16[64,1024]{1,0:T(8,128)(2,1)S(1)}, bf16[64,1024]{1,0:T(8,128)(2,1)S(1)}, u32[]{:S(2)}, u32[]{:S(2)}) collective-permute-start(bf16[64,1024]{1,0:T(8,128)(2,1)S(1)} %get-tuple-element.116), channel_id=1, source_target_pairs={{0,4},{6,2},{9,13},{15,11},{16,20},{22,18},{25,29},{31,27}} | collective-permute-start | bytes 393224 | tf_op jit(solution)/shard_map/stream_home/ppermute | solution.py:516
  90.7 8.7 %collective-permute-start.20 = (bf16[64,1024]{1,0:T(8,128)(2,1)S(1)}, bf16[64,1024]{1,0:T(8,128)(2,1)S(1)}, u32[]{:S(2)}, u32[]{:S(2)}) collective-permute-start(bf16[64,1024]{1,0:T(8,128)(2,1)S(1)} %get-tuple-element.117), channel_id=1, source_target_pairs={{0,8},{6,14},{9,1},{15,7},{16,24},{22,30},{25,17},{31,23}} | collective-permute-start | bytes 393224 | tf_op jit(solution)/shard_map/stream_home/ppermute | solution.py:516
  93.3 6.1 %collective-permute-start.21 = (bf16[64,1024]{1,0:T(8,128)(2,1)S(1)}, bf16[64,1024]{1,0:T(8,128)(2,1)S(1)}, u32[]{:S(2)}, u32[]{:S(2)}) collective-permute-start(bf16[64,1024]{1,0:T(8,128)(2,1)S(1)} %get-tuple-element.118), channel_id=1, source_target_pairs={{0,12},{6,10},{9,5},{15,3},{16,28},{22,26},{25,21},{31,19}} | collective-permute-start | bytes 393224 | tf_op jit(solution)/shard_map/stream_home/ppermute | solution.py:516
  94.8 4.6 %collective-permute-start.24 = (bf16[40,1024]{1,0:T(8,128)(2,1)S(1)}, bf16[40,1024]{1,0:T(8,128)(2,1)S(1)}, u32[]{:S(2)}, u32[]{:S(2)}) collective-permute-start(bf16[40,1024]{1,0:T(8,128)(2,1)S(1)} %get-tuple-element.129), channel_id=1, source_target_pairs={{0,4},{1,5},{2,6},{3,7},{4,0},{5,1},{6,2},{7,3},{8,12},{9,13},{10,... | collective-permute-start | bytes 245768 | tf_op jit(solution)/shard_map/reply/ppermute | solution.py:516
  96.0 7.9 %collective-permute-start.26 = (bf16[40,1024]{1,0:T(8,128)(2,1)S(1)}, bf16[40,1024]{1,0:T(8,128)(2,1)S(1)}, u32[]{:S(2)}, u32[]{:S(2)}) collective-permute-start(bf16[40,1024]{1,0:T(8,128)(2,1)S(1)} %get-tuple-element.130), channel_id=1, source_target_pairs={{0,12},{1,13},{2,14},{3,15},{4,8},{5,9},{6,10},{7,11},{8,4},{9,5},... | collective-permute-start | bytes 245768 | tf_op jit(solution)/shard_map/reply/ppermute | solution.py:516
  99.4 6.7 %collective-permute-start.25 = (bf16[40,1024]{1,0:T(8,128)(2,1)S(1)}, bf16[40,1024]{1,0:T(8,128)(2,1)S(1)}, u32[]{:S(2)}, u32[]{:S(2)}) collective-permute-start(bf16[40,1024]{1,0:T(8,128)(2,1)S(1)} %get-tuple-element.125), channel_id=1, source_target_pairs={{0,8},{1,9},{2,10},{3,11},{4,12},{5,13},{6,14},{7,15},{8,0},{9,1},... | collective-permute-start | bytes 245768 | tf_op jit(solution)/shard_map/reply/ppermute | solution.py:516

commit v3 on v2

--- a/solution.py
+++ b/solution.py
@@ -137,6 +137,9 @@
 
 
 LOG2E = 1.4426950408889634
+HOLD = 3.0
+HOLD_B = 5.0
+ORDER = 5.0
 AXES = ("ctx", "exp", "tp")
 f32 = jnp.float32
 bf16 = jnp.bfloat16
@@ -187,7 +190,25 @@
     pack_ref[...] = jnp.concatenate(list(state) + [cum, zero], axis=0).astype(bf16)
 
 
-def correct_kernel(c_ref, one_ref, two_ref, three_ref, base_ref, cum_ref, silu_ref, rate_ref, out_ref, gated_s):
+def spread_kernel(c_ref, base_ref, cum_ref, silu_ref, rate_ref, out_ref, weight_ref):
+    states = c_ref.shape[0]
+    g = rate_ref.shape[0] // states
+    tokens = base_ref.shape[0] // g
+    out_ref[...] = base_ref[...] * silu_ref[...]
+
+    def one(t, _):
+        rows = pl.ds(pl.multiple_of(t * g, g), g)
+        cum, silu = cum_ref[rows, :], silu_ref[rows, :]
+        for n in range(states):
+            weight_ref[pl.ds(pl.multiple_of(t * (g * states) + n * g, g), g), :] = (
+                jnp.exp2(cum * rate_ref[n * g : (n + 1) * g, :]) * (c_ref[n, t] * silu)
+            )
+        return 0
+
+    lax.fori_loop(0, tokens, one, 0, unroll=2)
+
+
+def correct_kernel(one_ref, two_ref, three_ref, base_ref, weight_ref, rate_ref, out_ref, gated_s):
     tokens, width = out_ref.shape
     g = width // 128
     states = rate_ref.shape[0] // g
@@ -210,42 +231,35 @@
 
     def one(t, _):
         rows = pl.ds(pl.multiple_of(t * g, g), g)
-        cum = cum_ref[rows, :]
         out = base_ref[rows, :]
         for n in range(states):
-            out = out + c_ref[n, t] * (jnp.exp2(cum * rate_ref[n * g : (n + 1) * g, :]) * entering[n])
-        gated_s[rows, :] = out * silu_ref[rows, :]
+            out = out + weight_ref[pl.ds(pl.multiple_of(t * (g * states) + n * g, g), g), :] * entering[n]
+        gated_s[rows, :] = out
         return 0
 
-    lax.fori_loop(0, tokens, one, 0, unroll=2)
+    lax.fori_loop(0, tokens, one, 0, unroll=4)
     for k in range(g):
         out_ref[:, k * 128 : (k + 1) * 128] = gated_s[pl.ds(k, tokens, stride=g), :].astype(bf16)
-
-
-def place_pair(scratch, odd, first, second):
-    rows = first.shape[0]
-    scratch[pl.ds(pl.multiple_of(odd * rows, rows), rows), :] = first
-    scratch[pl.ds(pl.multiple_of((1 - odd) * rows, rows), rows), :] = second
 
 
 def route_kernel(ids_ref, lanes_ref, cols_ref):
     count = cols_ref.shape[0]
     ids = ids_ref[...].astype(f32)
     first, second = ids[0:1, :], ids[1:2, :]
-    expert = lax.broadcasted_iota(jnp.int32, (8, 128), 0).astype(f32)
+    expert = lax.broadcasted_iota(jnp.int32, (8, count), 0).astype(f32)
     member = (jnp.where(expert == first, 1.0, 0.0) + jnp.where(expert == second, 1.0, 0.0)).astype(bf16)
-    before = lax.broadcasted_iota(jnp.int32, (128, 128), 0)
-    token = lax.broadcasted_iota(jnp.int32, (128, 128), 1)
-    token = jnp.where(token >= count, token - count, token)
-    earlier = jnp.where((before < token) & (before < count), 1.0, 0.0).astype(bf16)
-    rank = jnp.dot(member, earlier, preferred_element_type=f32)
+    before = lax.broadcasted_iota(jnp.int32, (count, count), 0)
+    token = lax.broadcasted_iota(jnp.int32, (count, count), 1)
+    rank = jnp.dot(member, jnp.where(before < token, 1.0, 0.0).astype(bf16), preferred_element_type=f32)
     slot = [
         which * CAP + jnp.sum(jnp.where(expert == which, rank, 0.0), axis=0, keepdims=True) for which in (first, second)
     ]
-    row = lax.broadcasted_iota(jnp.int32, (128, 128), 0)
-    both = jnp.where(row == 0, slot[0], jnp.where(row == 1, slot[1], 0.0))
-    lanes_ref[...] = both[:8]
-    cols_ref[...] = both.T[:count].astype(bf16)
+    both = jnp.where(expert == 0, slot[0], jnp.where(expert == 1, slot[1], 0.0))
+    lanes_ref[...] = both
+    same = lax.broadcasted_iota(jnp.int32, (8, 128), 0) == lax.broadcasted_iota(jnp.int32, (8, 128), 1)
+    cols_ref[...] = lax.dot_general(
+        both.astype(bf16), jnp.where(same, 1.0, 0.0).astype(bf16), (((0,), (0,)), ((), ())), preferred_element_type=f32
+    ).astype(bf16)
 
 
 def pack_kernel(own_ref, peer_ref, resid_ref, slots_ref, m0_ref, m1_ref, m2_ref, m3_ref):
@@ -260,7 +274,7 @@
         ref[:, 2 * width + part :] = slots_ref[...]
 
 
-def hold_kernel(own_ref, peer_ref, out_ref, sems):
+def hold_out_kernel(own_ref, peer_ref, after_ref, out_ref, sems):
     half = own_ref.shape[0]
     copies = [
         pltpu.make_async_copy(ref, out_ref.at[pl.ds(k * half, half)], sems.at[k]) for k, ref in enumerate((own_ref, peer_ref))
@@ -271,13 +285,17 @@
         copy.wait()
 
 
+def after_kernel(earlier_ref, token_ref):
+    token_ref[...] = jnp.zeros_like(token_ref)
+
+
 def place_pair(scratch, odd, first, second):
     rows = first.shape[0]
     scratch[pl.ds(pl.multiple_of(odd * rows, rows), rows), :] = first
     scratch[pl.ds(pl.multiple_of((1 - odd) * rows, rows), rows), :] = second
 
 
-def project_kernel(first_ref, second_ref, w_ref, out_ref, slots_ref, rows_s):
+def project_kernel(first_ref, second_ref, w_ref, after_ref, out_ref, slots_ref, rows_s):
     place_pair(rows_s, lax.axis_index("ctx") % 2, first_ref[...], second_ref[...])
     exp = lax.axis_index("exp")
     depth = w_ref.shape[0]
@@ -291,21 +309,15 @@
 
 
 def select_kernel(
-    own_ref, peer_ref, slots_ref, gain_ref, stream_first_ref, stream_second_ref, d0_ref, d1_ref, d2_ref, d3_ref, rows_s
+    own_ref, peer_ref, slots_ref, after_ref, stream_first_ref, stream_second_ref, d0_ref, d1_ref, d2_ref, d3_ref, rows_s
 ):
     ctx = lax.axis_index("ctx")
     odd = ctx % 2
     block = stream_first_ref.shape[0]
-    width = own_ref.shape[1]
     rows_s[...] = (own_ref[...].astype(f32) + peer_ref[...].astype(f32)).astype(bf16)
     stream_first_ref[...] = rows_s[pl.ds(pl.multiple_of(odd * block, block), block), :]
     stream_second_ref[...] = rows_s[pl.ds(pl.multiple_of((1 - odd) * block, block), block), :]
-    wide = rows_s[...].astype(f32)
-    squares = jnp.sum(wide * wide, axis=1, keepdims=True)
-    high = squares.astype(bf16).astype(f32)
-    lane = lax.broadcasted_iota(jnp.int32, (2 * block, 128), 1)
-    stats = jnp.where(lane == 0, high, jnp.where(lane == 1, squares - high, 0.0)).astype(bf16)
-    feats = (wide * gain_ref[...]).astype(bf16)
+    feats = rows_s[...]
     slots = slots_ref[...].astype(f32).T
     count = d0_ref.shape[0]
     row = lax.broadcasted_iota(jnp.int32, (count, 2 * block), 0)
@@ -317,27 +329,36 @@
         base = ((ctx ^ p) * CAP).astype(f32)
         hit = mine & ((slots[0:1, :] == want + base) | (slots[1:2, :] == want + base))
         pick = jnp.where(hit, 1.0, 0.0).astype(bf16)
-        ref[:, :width] = jnp.dot(pick, feats, preferred_element_type=f32).astype(bf16)
-        ref[:, width:] = jnp.dot(pick, stats, preferred_element_type=f32).astype(bf16)
-
-
-def gate_up_copies(wg_ref, wu_ref, held_ref, sems, begin):
-    depth = wg_ref.shape[0]
-    width = held_ref.shape[1]
-    return [
-        pltpu.make_async_copy(
-            ref.at[:, pl.ds(begin, width)], held_ref.at[pl.ds(k * depth, depth)], sems.at[k]
-        )
-        for k, ref in enumerate((wg_ref, wu_ref))
-    ]
-
-
-def hold_first_kernel(wg_ref, wu_ref, held_ref, sems):
-    copies = gate_up_copies(wg_ref, wu_ref, held_ref, sems, 0)
+        ref[...] = jnp.dot(pick, feats, preferred_element_type=f32).astype(bf16)
+
+
+def part_copy(source_ref, begin, held_ref, place, sem, rows=None):
+    height, cols = source_ref.shape[0], held_ref.shape[1]
+    first, count = rows or (0, height)
+    return pltpu.make_async_copy(
+        source_ref.at[pl.ds(first, count), pl.ds(begin, cols)], held_ref.at[pl.ds(place * height + first, count)], sem
+    )
+
+
+def wait_all(copies):
     for copy in copies:
         copy.start()
     for copy in copies:
         copy.wait()
+
+
+def hold_early_kernel(gate_ref, up_ref, after_ref, token_ref, held_ref, sems):
+    token_ref[...] = jnp.zeros_like(token_ref)
+    rows = up_ref.shape[0] // 2
+    wait_all([part_copy(gate_ref, 0, held_ref, 0, sems.at[0]), part_copy(up_ref, 0, held_ref, 1, sems.at[1], (0, rows))])
+
+
+def hold_late_kernel(gate_ref, up_ref, after_ref, held_second_ref, held_ref, sems):
+    rows = up_ref.shape[0] // 2
+    wait_all([
+        part_copy(up_ref, 0, held_ref, 1, sems.at[0], (rows, rows)),
+        part_copy(gate_ref, held_ref.shape[1], held_second_ref, 0, sems.at[1]),
+    ])
 
 
 def gate_up(feats, held_ref, out_ref):
@@ -352,23 +373,26 @@
 
 
 def first_half_kernel(
-    a0_ref, a1_ref, a2_ref, a3_ref, b0_ref, b1_ref, b2_ref, b3_ref, held_ref, wg_ref, wu_ref,
-    out_ref, squares_ref, feats_ref, next_ref, sems,
+    a0_ref, a1_ref, a2_ref, a3_ref, b0_ref, b1_ref, b2_ref, b3_ref, gain_ref, wu_ref,
+    out_ref, feats_ref, held_ref, held_second_ref, squares_s, sem,
 ):
-    copies = gate_up_copies(wg_ref, wu_ref, next_ref, sems, held_ref.shape[1])
-    for copy in copies:
-        copy.start()
+    begin = held_ref.shape[1]
+    copy = part_copy(wu_ref, begin, held_second_ref, 1, sem)
+    copy.start()
     expert = lax.axis_index("ctx")
     tp = lax.axis_index("tp")
     here = expert // 2 == tp
-    count = a0_ref.shape[0]
-    width = a0_ref.shape[1] - 128
+    count, width = a0_ref.shape
 
     def put(group, near_ref, far_ref):
         rows = pl.ds(pl.multiple_of((tp ^ group) * count, count), count)
+        squares = jnp.zeros((count, 1), f32)
         for side, ref in ((expert % 2, near_ref), (1 - expert % 2, far_ref)):
-            feats_ref[rows, pl.ds(pl.multiple_of(side * width, width), width)] = ref[:, :width]
-        squares_ref[rows, :] = near_ref[:, width:].astype(f32) + far_ref[:, width:].astype(f32)
+            cols = pl.ds(pl.multiple_of(side * width, width), width)
+            wide = ref[...].astype(f32)
+            squares = squares + jnp.sum(wide * wide, axis=1, keepdims=True)
+            feats_ref[rows, cols] = (wide * gain_ref[:, pl.ds(pl.multiple_of(tp * 2 * width + side * width, width), width)]).astype(bf16)
+        squares_s[rows, :] = jnp.broadcast_to(squares, (count, 128))
 
     @pl.when(here)
     def _():
@@ -380,29 +404,38 @@
         put(0, a2_ref, a3_ref)
         put(1, b2_ref, b3_ref)
 
+    squares = squares_s[...]
+    high = squares.astype(bf16).astype(f32)
+    lane = lax.broadcasted_iota(jnp.int32, squares.shape, 1)
+    out_ref[:, 2 * begin :] = jnp.where(lane == 0, high, jnp.where(lane == 1, squares - high, 0.0)).astype(bf16)
     gate_up(feats_ref[...], held_ref, out_ref)
-    for copy in copies:
-        copy.wait()
-
-
-def second_half_kernel(feats_ref, held_ref, wd_ref, out_ref, next_ref, sem):
-    copy = pltpu.make_async_copy(wd_ref, next_ref, sem)
+    copy.wait()
+
+
+def second_half_kernel(feats_ref, wd_ref, out_ref, down_ref, held_ref, sem):
+    copy = pltpu.make_async_copy(wd_ref, down_ref, sem)
     copy.start()
     gate_up(feats_ref[...], held_ref, out_ref)
     copy.wait()
 
 
-def hidden_of(own_ref, peer_ref, sq0, sq1, features):
-    squares = sq0[...] + sq1[...]
-    scale = lax.rsqrt((squares[:, 0:1] + squares[:, 1:2]) * (1.0 / features) + 1e-06)
-    width = own_ref.shape[1] // 2
+def scale_of(own_ref, peer_ref, features):
+    width = own_ref.shape[1]
+    total = own_ref[:, width - 128 :].astype(f32) + peer_ref[:, width - 128 :].astype(f32)
+    scale = lax.rsqrt((total[:, 0:1] + total[:, 1:2]) * (1.0 / features) + 1e-06)
+    return jnp.broadcast_to(scale, total.shape)
+
+
+def hidden_of(own_ref, peer_ref, scale):
+    width = own_ref.shape[1] // 256 * 128
     gate = (own_ref[:, :width].astype(f32) + peer_ref[:, :width].astype(f32)) * scale
-    up = (own_ref[:, width:].astype(f32) + peer_ref[:, width:].astype(f32)) * scale
+    up = (own_ref[:, width : 2 * width].astype(f32) + peer_ref[:, width : 2 * width].astype(f32)) * scale
     return (gate / (1.0 + jnp.exp(-gate)) * up).astype(bf16)
 
 
-def down_first_kernel(features, own_ref, peer_ref, sq0, sq1, held_ref, out_ref):
-    hidden = hidden_of(own_ref, peer_ref, sq0, sq1, features)
+def down_first_kernel(features, own_ref, peer_ref, held_ref, out_ref, scale_ref):
+    scale_ref[...] = scale_of(own_ref, peer_ref, features)
+    hidden = hidden_of(own_ref, peer_ref, scale_ref[:, 0:1])
     depth = hidden.shape[1]
     block = min(512, out_ref.shape[1])
     for n in range(0, out_ref.shape[1], block):
@@ -420,9 +453,9 @@
 
 
 def down_theirs_kernel(
-    features, own_ref, peer_ref, sq0, sq1, held_ref, acc_ref, near_ref, far_ref, hidden_ref, sum_s
+    own_ref, peer_ref, scale_ref, held_ref, acc_ref, near_ref, far_ref, hidden_ref, sum_s
 ):
-    hidden_ref[...] = hidden_of(own_ref, peer_ref, sq0, sq1, features)
+    hidden_ref[...] = hidden_of(own_ref, peer_ref, scale_ref[:, 0:1])
     down_piece(hidden_ref[...], held_ref, acc_ref, near_ref, far_ref, sum_s, 1 - lax.axis_index("exp"))
 
 
@@ -454,7 +487,7 @@
         base = ((ctx ^ p) * CAP).astype(f32)
         weight = jnp.zeros(want.shape, f32)
         for k in range(2):
-            weight = weight + jnp.where(slots_ref[k : k + 1, :tokens] == want + base, weights_ref[k : k + 1, :], 0.0)
+            weight = weight + jnp.where(slots_ref[k : k + 1, :] == want + base, weights_ref[k : k + 1, :], 0.0)
         high = weight.astype(bf16)
         low = (weight - high.astype(f32)).astype(bf16)
         rows = ref[...]
@@ -469,12 +502,26 @@
 AN = pl.BlockSpec(memory_space=pl.ANY)
 
 
-def call(kernel, out, ins, scratch=(), args=(), limit=8, us=1.0):
-    return pl.pallas_call(
-        kernel, out_shape=out, in_specs=ins, out_specs=jax.tree.map(lambda _: VM, out), scratch_shapes=list(scratch),
+def call(kernel, out, ins, scratch=(), args=(), limit=8, us=0.0, keep=(), show=False):
+    single = not isinstance(out, tuple)
+    outs = (out,) if single else out
+    first, last = len(ins), len(ins) + len(keep)
+
+    def body_kernel(*refs):
+        results = refs[last : last + len(outs) + (len(keep) if show else 0)]
+        kernel(*refs[:first], *results, *refs[last + len(outs) + len(keep) :])
+
+    result = pl.pallas_call(
+        body_kernel,
+        out_shape=outs + tuple(pltpu.VMEM(x.shape, x.dtype) for x in keep),
+        in_specs=[*ins, *[VM] * len(keep)],
+        out_specs=(VM,) * (len(outs) + len(keep)),
+        scratch_shapes=list(scratch),
+        input_output_aliases={first + k: len(outs) + k for k in range(len(keep))},
         compiler_params=pltpu.CompilerParams(vmem_limit_bytes=limit * 1024 * 1024),
-        cost_estimate=pl.CostEstimate(flops=0, transcendentals=0, bytes_accessed=int(us * 3.0e6)),
-    )(*args)
+        cost_estimate=pl.CostEstimate(flops=int(us * 1.0e9), transcendentals=0, bytes_accessed=0),
+    )(*args, *[in_vmem(x) for x in keep])
+    return result[0] if single and not keep else result
 
 
 def shape(rows, cols, kind):
@@ -533,25 +580,30 @@
             (flat, flat, flat, shape(states * g, 128, f32), shape((states + 2) * g, 128, bf16)),
             [SM, SM] + [VM] * 5,
             [pltpu.VMEM((tokens * g, 128), f32)] * 3 + [pltpu.VMEM((states * g, 128), f32)],
-            tuple(in_hbm(v) for v in (b_rows, c_rows, dt_raw, conv_out, gate_z, a_log, d_skip.reshape(g, 128))), us=3.0,
+            tuple(in_hbm(v) for v in (b_rows, c_rows, dt_raw, conv_out, gate_z, a_log, d_skip.reshape(g, 128))),
         )
     with jax.named_scope("relay"):
         entered = [
             permute(pack, [(number(c, x, t), number(c ^ p, x, t)) for c, x in chips for t in range(tp_count)])
             for p in away
         ]
+    with jax.named_scope("spread"):
+        base, spread = call(
+            spread_kernel, (flat, shape(tokens * states * g, 128, f32)), [SM] + [VM] * 4, (),
+            (in_hbm(c_rows), base, cum, silu_z, rate), us=2.0,
+        )
     with jax.named_scope("correct"):
         gated = call(
-            correct_kernel, shape(tokens, channels, bf16), [SM] + [VM] * 7, [pltpu.VMEM((tokens * g, 128), f32)],
-            (in_hbm(c_rows), *entered, base, cum, silu_z, rate), us=2.0,
-        )
-    gated, route_ids, norm_gain = lax.optimization_barrier((gated, route_ids, norm_gain))
+            correct_kernel, shape(tokens, channels, bf16), [VM] * 6, [pltpu.VMEM((tokens * g, 128), f32)],
+            (*entered, base, spread, rate),
+        )
+    gated, route_ids = lax.optimization_barrier((gated, route_ids))
     with jax.named_scope("gather_gated"):
         peer_gated = swap_tp(gated)
+    gain = norm_gain[None, :]
     with jax.named_scope("route"):
-        ids = route_ids.T
         slot_lanes, slot_cols = call(
-            route_kernel, (shape(8, 128, f32), shape(tokens, 128, bf16)), [VM], (), (jnp.concatenate([ids, ids], axis=1),)
+            route_kernel, (shape(8, tokens, f32), shape(tokens, 128, bf16)), [VM], (), (in_hbm(route_ids.T),)
         )
     with jax.named_scope("gather_gated"):
         message = shape(tokens, 2 * channels + block_cols // 2 + 128, bf16)
@@ -560,75 +612,87 @@
         )
         blocks = [messages[0]] + [to_owner(messages[p], p) for p in away]
 
-    def hold_out(after):
-        own_rows, peer_rows, _ = lax.optimization_barrier((out_weight, peer_weight, after))
-        with jax.named_scope("hold_out_weight"):
-            return call(
-                hold_kernel, pltpu.VMEM((2 * own_rows.shape[0], block_cols), bf16), [HB, AN], [pltpu.SemaphoreType.DMA((2,))],
-                (in_hbm(own_rows), peer_rows), us=1.6,
-            )
-
-    held_out = hold_out(messages[0])
-    gain = lax.dynamic_slice_in_dim(norm_gain, ctx * block_cols, block_cols, 0)[None, :]
-
-    streams = []
-    sent = []
-    for group in range(2):
-        with jax.named_scope("project"):
-            own, slots = call(
-                project_kernel, (shape(2 * tokens, block_cols, bf16), shape(2 * tokens, 128, bf16)), [VM] * 3,
-                [pltpu.VMEM((2 * tokens, message.shape[1]), bf16)],
-                (blocks[2 * group], blocks[2 * group + 1], in_vmem(held_out)),
-            )
-        if group == 0:
-            held_out = hold_out(own)
-        with jax.named_scope("sum_exp"):
-            peer = permute(own, [(number(c, x, owner(c)), number(c, 1 - x, owner(c))) for c, x in chips])
-        with jax.named_scope("select"):
-            block = shape(tokens, block_cols, bf16)
-            routed = shape(2 * CAP, block_cols + 128, bf16)
-            first, second, *out = call(
-                select_kernel, (block, block) + (routed,) * 4, [VM] * 4, [pltpu.VMEM((2 * tokens, block_cols), bf16)],
-                (own, peer, slots, gain),
-            )
-            streams += [first, second]
-            if group == 0:
-                *out, blocks[2], blocks[3] = lax.optimization_barrier((*out, blocks[2], blocks[3]))
-        with jax.named_scope("dispatch"):
-            sent.append([out[0]] + [from_owner(out[p], p) for p in away])
-
+    token_kind = shape(8, 128, f32)
+    with jax.named_scope("hold_out_weight"):
+        held_out = call(
+            hold_out_kernel, pltpu.VMEM((2 * out_weight.shape[0], block_cols), bf16), [HB, AN, AN],
+            [pltpu.SemaphoreType.DMA((2,))], (in_hbm(out_weight), peer_weight, messages[0]),
+        )
     slots_total = EXPERTS * CAP
     part_width = w_gate.shape[1] // 2
     wg, wu, wd = (in_hbm(v) for v in (w_gate, w_up, w_down))
     dma = pltpu.SemaphoreType.DMA
+    held_kind = pltpu.VMEM((2 * half_width, part_width), bf16)
+
+    def project(first, second, token, keep):
+        with jax.named_scope("project"):
+            return call(
+                project_kernel, (shape(2 * tokens, block_cols, bf16), shape(2 * tokens, 128, bf16)), [VM] * 3 + [AN],
+                [pltpu.VMEM((2 * tokens, message.shape[1]), bf16)], (first, second, in_vmem(held_out), token), keep=keep,
+            )
+
+    def sum_exp(own):
+        with jax.named_scope("sum_exp"):
+            return permute(own, [(number(c, x, owner(c)), number(c, 1 - x, owner(c))) for c, x in chips])
+
+    def select(own, peer, slots, token, keep):
+        with jax.named_scope("select"):
+            block = shape(tokens, block_cols, bf16)
+            routed = shape(2 * CAP, block_cols, bf16)
+            return call(
+                select_kernel, (block, block) + (routed,) * 4, [VM] * 3 + [AN], [pltpu.VMEM((2 * tokens, block_cols), bf16)],
+                (own, peer, slots, token), keep=keep,
+            )
+
+    def dispatch(out):
+        with jax.named_scope("dispatch"):
+            return [out[0]] + [from_owner(out[p], p) for p in away]
+
+    own, slots, held_out = project(blocks[0], blocks[1], slot_lanes, (held_out,))
+    peer = sum_exp(own)
     with jax.named_scope("hold_weights"):
-        held_kind = pltpu.VMEM((2 * half_width, part_width), bf16)
-        held = call(hold_first_kernel, held_kind, [HB, HB], [dma((2,))], (wg, wu), us=5.8)
+        token, held = call(
+            hold_early_kernel, (token_kind, held_kind), [HB, HB, AN], [dma((2,))], (wg, wu, own), us=HOLD
+        )
+    first, second, *out, held_out, held = select(own, peer, slots, token, (held_out, held))
+    streams = [first, second]
+    sent = [dispatch(out)]
+    token = call(after_kernel, token_kind, [AN], (), (out[0],), us=ORDER)
+    own, slots, held = project(blocks[2], blocks[3], token, (held,))
+    peer = sum_exp(own)
+    token = call(after_kernel, token_kind, [AN], (), (own,), us=ORDER)
+    first, second, *out, held = select(own, peer, slots, token, (held,))
+    streams += [first, second]
+    sent.append(dispatch(out))
+    with jax.named_scope("hold_weights"):
+        held_second, held = call(
+            hold_late_kernel, (held_kind,), [HB, HB, AN], [dma((2,))], (wg, wu, out[0]), us=HOLD, keep=(held,), show=True
+        )
     with jax.named_scope("gate_up"):
-        both = shape(slots_total, 2 * part_width, bf16)
-        first, squares, feats, held = call(
+        first, feats, held, held_second = call(
             first_half_kernel,
-            (both, shape(slots_total, 128, f32), shape(slots_total, half_width, bf16), held_kind),
-            [VM] * 9 + [HB] * 2, [dma((2,))],
-            (*sent[0], *sent[1], in_vmem(held), wg, wu), us=5.8,
-        )
-        peer_squares = swap_tp(squares)
+            (shape(slots_total, 2 * part_width + 128, bf16), shape(slots_total, half_width, bf16)),
+            [VM] * 9 + [HB], [pltpu.VMEM((slots_total, 128), f32), dma],
+            (*sent[0], *sent[1], in_hbm(gain), wu), keep=(held, held_second), show=True,
+        )
         peer_first = swap_tp(first)
-        second, held = call(
-            second_half_kernel, (both, pltpu.VMEM(w_down.shape, bf16)), [VM, VM, HB], [dma], (feats, in_vmem(held), wd), us=5.8
+        second, held, _ = call(
+            second_half_kernel, (shape(slots_total, 2 * part_width, bf16),), [VM, HB], [dma],
+            (feats, wd), keep=(held, held_second), show=True,
         )
         peer_second = swap_tp(second)
     with jax.named_scope("down"):
         held = in_vmem(held)
-        acc = call(
-            functools.partial(down_first_kernel, model_width), shape(slots_total, half_width, f32), [VM] * 5, (),
-            (first, peer_first, squares, peer_squares, held), us=2.0,
+        acc, scale = call(
+            functools.partial(down_first_kernel, model_width),
+            (shape(slots_total, half_width, f32), shape(slots_total, 128, f32)), [VM] * 3, (),
+            (first, peer_first, held),
         )
         piece = shape(slots_total // 2, piece_width, bf16)
         total = pltpu.VMEM((slots_total, piece_width), f32)
         theirs_near, theirs_far, hidden = call(
-            functools.partial(down_theirs_kernel, model_width), (piece, piece, shape(slots_total, part_width, bf16)),
-            [VM] * 6, [total], (second, peer_second, squares, peer_squares, held, acc), us=1.4,
+            down_theirs_kernel, (piece, piece, shape(slots_total, part_width, bf16)),
+            [VM] * 5, [total], (second, peer_second, scale, held, acc),
         )
     with jax.named_scope("sum_experts"):
         swap = [(0, 1), (1, 0)]
@@ -636,16 +700,6 @@
         theirs_near, _ = lax.optimization_barrier((theirs_near, theirs_far))
         peer_near = lax.ppermute(theirs_near, "exp", swap)
         mine_near, mine_far = call(down_mine_kernel, (piece, piece), [VM] * 3, [total], (hidden, held, acc))
-    with jax.named_scope("stream_home"):
-        *streams, mine_far = lax.optimization_barrier((*streams, mine_far))
-        home = [
-            permute(
-                streams[p],
-                [(number(c, c % exp_count, owner(c)), number(c ^ p, c % exp_count, owner(c))) for c in range(ctx_count)],
-            )
-            for p in away
-        ]
-
     def reply(own, peer):
         small = shape(CAP, piece_width, bf16)
         return call(
@@ -655,12 +709,22 @@
     def send(x, p):
         return permute(x, [(number(c, x_at, t), number(c ^ p, x_at, t)) for c, x_at in chips for t in range(tp_count)])
 
+    def send_home(p, after):
+        stream, _ = lax.optimization_barrier((streams[p], after))
+        with jax.named_scope("stream_home"):
+            return permute(
+                stream,
+                [(number(c, c % exp_count, owner(c)), number(c ^ p, c % exp_count, owner(c))) for c in range(ctx_count)],
+            )
+
     with jax.named_scope("reply"):
+        far_home = [send_home(p, mine_far) for p in (2, 3)]
         r2, r3 = reply(mine_far, peer_far)
         far = [send(r2, 2), send(r3, 3)]
         mine_near, peer_near, _ = lax.optimization_barrier((mine_near, peer_near, r2))
         r0, r1 = reply(mine_near, peer_near)
         replies = [r0, send(r1, 1), *far]
+        home = [send_home(1, r1), *far_home]
     with jax.named_scope("finish"):
         return call(
             finish_kernel, shape(tokens, piece_width, bf16), [VM] * 10, (),

time: 108 us -> 101 us (0.935)
  waiting for transfers between devices: 20.2 us -> 16 us
  starting transfers between devices: 48.9 us -> 46.6 us
    ppermute x20, waiting for transfers between devices: 17.3 us -> 15.1 us  [permute(): return lax.ppermute(x, AXES, pairs)]
    ppermute x5 -> x4, waiting for transfers between devices: 2.94 us -> 0.87 us  [swap_tp(): lax.ppermute(x, 'tp', [(i, tp_count - 1 - i) for i in range(tp_count)])]
    ppermute x5 -> x4, starting transfers between devices: 2.97 us -> 1.15 us  [swap_tp(): lax.ppermute(x, 'tp', [(i, tp_count - 1 - i) for i in range(tp_count)])]
    pallas_call x19 -> x22, Pallas kernels: 36.2 us -> 36.5 us  [call(): pl.pallas_call(body_kernel, out_shape=outs + tuple((pltpu.VMEM(x.shape, x...]
  transfers between devices with their start and end apart: 27 -> 26, of which waited for: 9 -> 9; matrix products, arithmetic and copies ran while one was open for 1% -> 0% of each run, Pallas kernels for 25% -> 30%
where the time goes in v3:
time: 101 us; the launch traced here: 99.9 us
  starting transfers between devices  46.6 us (46%)
  Pallas kernels  36.5 us (36%)
  waiting for transfers between devices  16 us (16%)
    ppermute x20, starting transfers between devices, permute(): return lax.ppermute(x, AXES, pairs)  43.3 us
    pallas_call x22, Pallas kernels, call(): pl.pallas_call(body_kernel, out_shape=outs + tuple((pltpu.VMEM(x.shape, x...  36.5 us
    ppermute x20, waiting for transfers between devices, permute(): return lax.ppermute(x, AXES, pairs)  15.1 us
  transfers between devices with their start and end apart: 26, of which 9 were waited for; matrix products, arithmetic and copies ran while one was open for 0% of the time, Pallas kernels for 30%

profile of v3, /device:TPU:0, one launch (start us, length us, event | category | flops | bytes accessed | tf_op | source)
XLA Modules:
  0.0 99.9 jit_solution(14981815009209252738)
XLA Ops:
  0.0 0.5 collective-permute-start.5
  0.5 3.1 %scan.1 = (f32[512,128]{1,0:T(8,128)S(1)}, f32[512,128]{1,0:T(8,128)S(1)}, f32[512,128]{1,0:T(8,128)S(1)}, f32[128,128]{1,0:T(8,128)S(1)}, bf16[144,128]{1,0:T(8,128)(2,1)S(1)}) custom-call(f32[16,64]{1,0:T(8,128)} %bitcast.8, f32[16,64]{1,0:T(8,128)} %bitcast.9, f32[64,1024]{1,0:T(8,128)} %refs_2_.2, bf16[64,1024]{1,0:T(8,128)(2,1)} %refs_3_.1, ...), custom_call_target="tpu_custom_call" | custom-call | tf_op jit(solution)/shard_map/scan/pallas_call | solution.py:514
  3.5 4.7 %collective-permute-start.2 = (bf16[144,128]{1,0:T(8,128)(2,1)S(1)}, bf16[144,128]{1,0:T(8,128)(2,1)S(1)}, u32[]{:S(2)}, u32[]{:S(2)}) collective-permute-start(bf16[144,128]{1,0:T(8,128)(2,1)S(1)} %get-tuple-element.68), channel_id=1, source_target_pairs={{0,12},{1,13},{2,14},{3,15},{4,8},{5,9},{6,10},{7,11},{8,4},{9,5},... | collective-permute-start | bytes 110600 | tf_op jit(solution)/shard_map/relay/ppermute | solution.py:563
  8.2 0.6 collective-permute-start
  8.8 1.9 %spread.1 = (f32[512,128]{1,0:T(8,128)S(1)}, f32[8192,128]{1,0:T(8,128)S(1)}) custom-call(f32[16,64]{1,0:T(8,128)} %bitcast.10, f32[512,128]{1,0:T(8,128)S(1)} %get-tuple-element.69.refs_1_, f32[512,128]{1,0:T(8,128)S(1)} %get-tuple-element.70.refs_2_, f32[512,128]{1,0:T(8,128)S(1)} %get-tuple-element.71.refs_3_, ...), custom_call_target="tpu_custom_call" | custom-call | flops 2000000000 | tf_op jit(solution)/shard_map/spread/pallas_call | solution.py:514
  10.8 2.3 %collective-permute-done.1.refs_1_ = bf16[144,128]{1,0:T(8,128)(2,1)S(1)} collective-permute-done((bf16[144,128]{1,0:T(8,128)(2,1)S(1)}, bf16[144,128]{1,0:T(8,128)(2,1)S(1)}, u32[]{:S(2)}, u32[]{:S(2)}) %collective-permute-start.1) | collective-permute-done | bytes 36896 | tf_op jit(solution)/shard_map/relay/ppermute | solution.py:563
  13.1 0.5 correct.1.refs_0_
  13.7 1.0 route.1
  15.0 1.1 %gather_gated.1 = (bf16[64,2688]{1,0:T(8,128)(2,1)S(1)}, bf16[64,2688]{1,0:T(8,128)(2,1)S(1)}, bf16[64,2688]{1,0:T(8,128)(2,1)S(1)}, bf16[64,2688]{1,0:T(8,128)(2,1)S(1)}) custom-call(bf16[64,1024]{1,0:T(8,128)(2,1)S(1)} %correct.1.refs_0_, bf16[64,1024]{1,0:T(8,128)(2,1)S(1)} %collective-permute-done.3.refs_1_, bf16[64,4096]{1,0:T(8,128)(2,1)} %refs_2_.3, ...), custom_call_target="tpu_custom_call" | custom-call | tf_op jit(solution)/shard_map/gather_gated/pallas_call | solution.py:514
  16.1 2.5 %collective-permute-start.4 = (bf16[64,2688]{1,0:T(8,128)(2,1)S(1)}, bf16[64,2688]{1,0:T(8,128)(2,1)S(1)}, u32[]{:S(2)}, u32[]{:S(2)}) collective-permute-start(bf16[64,2688]{1,0:T(8,128)(2,1)S(1)} %get-tuple-element.79), channel_id=1, source_target_pairs={{4,0},{6,2},{0,4},{2,6},{13,9},{15,11},{9,13},{11,15},{20,16},{22,... | collective-permute-start | bytes 1032200 | tf_op jit(solution)/shard_map/gather_gated/ppermute | solution.py:563
  18.6 1.3 %collective-permute-start.10 = (bf16[64,2688]{1,0:T(8,128)(2,1)S(1)}, bf16[64,2688]{1,0:T(8,128)(2,1)S(1)}, u32[]{:S(2)}, u32[]{:S(2)}) collective-permute-start(bf16[64,2688]{1,0:T(8,128)(2,1)S(1)} %get-tuple-element.92), channel_id=1, source_target_pairs={{8,0},{10,2},{12,4},{14,6},{1,9},{3,11},{5,13},{7,15},{24,16},{26,... | collective-permute-start | bytes 1032200 | tf_op jit(solution)/shard_map/gather_gated/ppermute | solution.py:563
  19.9 1.3 %collective-permute-start.11 = (bf16[64,2688]{1,0:T(8,128)(2,1)S(1)}, bf16[64,2688]{1,0:T(8,128)(2,1)S(1)}, u32[]{:S(2)}, u32[]{:S(2)}) collective-permute-start(bf16[64,2688]{1,0:T(8,128)(2,1)S(1)} %get-tuple-element.93), channel_id=1, source_target_pairs={{12,0},{14,2},{8,4},{10,6},{5,9},{7,11},{1,13},{3,15},{28,16},{30,... | collective-permute-start | bytes 1032200 | tf_op jit(solution)/shard_map/gather_gated/ppermute | solution.py:563
  21.3 1.6 %hold_out_weight.1.refs_2_ = bf16[2048,1024]{1,0:T(8,128)(2,1)S(1)} custom-call(bf16[1024,1024]{1,0:T(8,128)(2,1)} %refs_0_.3, bf16[1024,1024]{1,0:T(8,128)(2,1)S(1)} %collective-permute-done.5.refs_1_, bf16[64,2688]{1,0:T(8,128)(2,1)S(1)} %get-tuple-element.78.refs_2_.refs_0_), custom_call_target="tpu_custom_call" | custom-call | tf_op jit(solution)/shard_map/hold_out_weight/pallas_call | solution.py:514
  22.9 0.4 copy.26.refs_4_
  23.3 3.0 %collective-permute-done.4.refs_1_ = bf16[64,2688]{1,0:T(8,128)(2,1)S(1)} collective-permute-done((bf16[64,2688]{1,0:T(8,128)(2,1)S(1)}, bf16[64,2688]{1,0:T(8,128)(2,1)S(1)}, u32[]{:S(2)}, u32[]{:S(2)}) %collective-permute-start.4) | collective-permute-done | bytes 344096 | tf_op jit(solution)/shard_map/gather_gated/ppermute | solution.py:563
  26.3 0.8 project.2
  27.1 3.4 %collective-permute-start.6 = (bf16[128,1024]{1,0:T(8,128)(2,1)S(1)}, bf16[128,1024]{1,0:T(8,128)(2,1)S(1)}, u32[]{:S(2)}, u32[]{:S(2)}) collective-permute-start(bf16[128,1024]{1,0:T(8,128)(2,1)S(1)} %get-tuple-element.81.refs_2_.refs_0_), channel_id=1, source_target_pairs={{0,2},{2,0},{4,6},{6,4},{9,11},{11,9},{13,15},{15,13},{16,18},{18,... | collective-permute-start | bytes 786440 | tf_op jit(solution)/shard_map/sum_exp/ppermute | solution.py:563
  30.5 4.6 %hold_weights.2 = (f32[8,128]{1,0:T(8,128)S(1)}, bf16[4096,2048]{1,0:T(8,128)(2,1)S(1)}) custom-call(bf16[2048,4096]{1,0:T(8,128)(2,1)} %refs_0_.5, bf16[2048,4096]{1,0:T(8,128)(2,1)} %refs_9_.1, bf16[128,1024]{1,0:T(8,128)(2,1)S(1)} %get-tuple-element.81.refs_2_.refs_0_), custom_call_target="tpu_custom_call" | custom-call | flops 3000000000 | tf_op jit(solution)/shard_map/hold_weights/pallas_call | solution.py:514
  35.4 0.4 select.2
  35.8 2.6 %collective-permute-start.7 = (bf16[80,1024]{1,0:T(8,128)(2,1)S(1)}, bf16[80,1024]{1,0:T(8,128)(2,1)S(1)}, u32[]{:S(2)}, u32[]{:S(2)}) collective-permute-start(bf16[80,1024]{1,0:T(8,128)(2,1)S(1)} %get-tuple-element.89), channel_id=1, source_target_pairs={{0,4},{2,6},{4,0},{6,2},{9,13},{11,15},{13,9},{15,11},{16,20},{18,... | collective-permute-start | bytes 491528 | tf_op jit(solution)/shard_map/dispatch/ppermute | solution.py:563
  38.4 0.8 project.3
  39.2 3.4 %collective-permute-start.12 = (bf16[128,1024]{1,0:T(8,128)(2,1)S(1)}, bf16[128,1024]{1,0:T(8,128)(2,1)S(1)}, u32[]{:S(2)}, u32[]{:S(2)}) collective-permute-start(bf16[128,1024]{1,0:T(8,128)(2,1)S(1)} %get-tuple-element.96.refs_0_), channel_id=1, source_target_pairs={{0,2},{2,0},{4,6},{6,4},{9,11},{11,9},{13,15},{15,13},{16,18},{18,... | collective-permute-start | bytes 786440 | tf_op jit(solution)/shard_map/sum_exp/ppermute | solution.py:563
  42.7 1.3 %collective-permute-start.8 = (bf16[80,1024]{1,0:T(8,128)(2,1)S(1)}, bf16[80,1024]{1,0:T(8,128)(2,1)S(1)}, u32[]{:S(2)}, u32[]{:S(2)}) collective-permute-start(bf16[80,1024]{1,0:T(8,128)(2,1)S(1)} %get-tuple-element.90), channel_id=1, source_target_pairs={{0,8},{2,10},{4,12},{6,14},{9,1},{11,3},{13,5},{15,7},{16,24},{18,... | collective-permute-start | bytes 491528 | tf_op jit(solution)/shard_map/dispatch/ppermute | solution.py:563
  44.0 1.3 %collective-permute-start.9 = (bf16[80,1024]{1,0:T(8,128)(2,1)S(1)}, bf16[80,1024]{1,0:T(8,128)(2,1)S(1)}, u32[]{:S(2)}, u32[]{:S(2)}) collective-permute-start(bf16[80,1024]{1,0:T(8,128)(2,1)S(1)} %get-tuple-element.91), channel_id=1, source_target_pairs={{0,12},{2,14},{4,8},{6,10},{9,5},{11,7},{13,1},{15,3},{16,28},{18,... | collective-permute-start | bytes 491528 | tf_op jit(solution)/shard_map/dispatch/ppermute | solution.py:563
  45.3 2.2 %collective-permute-done.12.refs_1_ = bf16[128,1024]{1,0:T(8,128)(2,1)S(1)} collective-permute-done((bf16[128,1024]{1,0:T(8,128)(2,1)S(1)}, bf16[128,1024]{1,0:T(8,128)(2,1)S(1)}, u32[]{:S(2)}, u32[]{:S(2)}) %collective-permute-start.12) | collective-permute-done | bytes 262176 | tf_op jit(solution)/shard_map/sum_exp/ppermute | solution.py:563
  47.5 0.4 select.3
  47.9 3.8 %collective-permute-start.13 = (bf16[80,1024]{1,0:T(8,128)(2,1)S(1)}, bf16[80,1024]{1,0:T(8,128)(2,1)S(1)}, u32[]{:S(2)}, u32[]{:S(2)}) collective-permute-start(bf16[80,1024]{1,0:T(8,128)(2,1)S(1)} %get-tuple-element.100), channel_id=1, source_target_pairs={{0,4},{2,6},{4,0},{6,2},{9,13},{11,15},{13,9},{15,11},{16,20},{18,... | collective-permute-start | bytes 491528 | tf_op jit(solution)/shard_map/dispatch/ppermute | solution.py:563
  51.7 1.3 %collective-permute-start.14 = (bf16[80,1024]{1,0:T(8,128)(2,1)S(1)}, bf16[80,1024]{1,0:T(8,128)(2,1)S(1)}, u32[]{:S(2)}, u32[]{:S(2)}) collective-permute-start(bf16[80,1024]{1,0:T(8,128)(2,1)S(1)} %get-tuple-element.101), channel_id=1, source_target_pairs={{0,8},{2,10},{4,12},{6,14},{9,1},{11,3},{13,5},{15,7},{16,24},{18,... | collective-permute-start | bytes 491528 | tf_op jit(solution)/shard_map/dispatch/ppermute | solution.py:563
  53.0 1.3 %collective-permute-start.15 = (bf16[80,1024]{1,0:T(8,128)(2,1)S(1)}, bf16[80,1024]{1,0:T(8,128)(2,1)S(1)}, u32[]{:S(2)}, u32[]{:S(2)}) collective-permute-start(bf16[80,1024]{1,0:T(8,128)(2,1)S(1)} %get-tuple-element.102), channel_id=1, source_target_pairs={{0,12},{2,14},{4,8},{6,10},{9,5},{11,7},{13,1},{15,3},{16,28},{18,... | collective-permute-start | bytes 491528 | tf_op jit(solution)/shard_map/dispatch/ppermute | solution.py:563
  54.3 4.7 %hold_weights.3 = (bf16[4096,2048]{1,0:T(8,128)(2,1)S(1)}, bf16[4096,2048]{1,0:T(8,128)(2,1)S(1)}) custom-call(bf16[2048,4096]{1,0:T(8,128)(2,1)} %refs_0_.5, bf16[2048,4096]{1,0:T(8,128)(2,1)} %refs_9_.1, bf16[80,1024]{1,0:T(8,128)(2,1)S(1)} %get-tuple-element.99.refs_2_.refs_4_, ...), custom_call_target="tpu_custom_call", output_to_operand_aliasing={{1}: (3, {})} | custom-call | flops 3000000000 | tf_op jit(solution)/shard_map/hold_weights/pallas_call | solution.py:514
  59.1 4.1 %gate_up.2 = (bf16[160,4224]{1,0:T(8,128)(2,1)S(1)}, bf16[160,2048]{1,0:T(8,128)(2,1)S(1)}, bf16[4096,2048]{1,0:T(8,128)(2,1)S(1)}, bf16[4096,2048]{1,0:T(8,128)(2,1)S(1)}) custom-call(bf16[80,1024]{1,0:T(8,128)(2,1)S(1)} %get-tuple-element.88.refs_0_, ...), custom_call_target="tpu_custom_call", output_to_operand_aliasing={{2}: (10, {}), {3}: (11, {})} | custom-call | tf_op jit(solution)/shard_map/gate_up/pallas_call | solution.py:514
  63.3 5.8 %gate_up.3 = (bf16[160,4096]{1,0:T(8,128)(2,1)S(1)}, bf16[4096,2048]{1,0:T(8,128)(2,1)S(1)}, bf16[4096,2048]{1,0:T(8,128)(2,1)S(1)}) custom-call(bf16[160,2048]{1,0:T(8,128)(2,1)S(1)} %get-tuple-element.106.refs_0_, bf16[4096,2048]{1,0:T(8,128)(2,1)} %refs_1_.5, ...), custom_call_target="tpu_custom_call", output_to_operand_aliasing={{1}: (2, {}), {2}: (3, {})} | custom-call | tf_op jit(solution)/shard_map/gate_up/pallas_call | solution.py:514
  69.1 0.6 collective-permute-start.16
  69.7 2.1 %down.2 = (f32[160,2048]{1,0:T(8,128)S(1)}, f32[160,128]{1,0:T(8,128)S(1)}) custom-call(bf16[160,4224]{1,0:T(8,128)(2,1)S(1)} %get-tuple-element.110.refs_0_, bf16[160,4224]{1,0:T(8,128)(2,1)S(1)} %collective-permute-done.17.refs_1_, bf16[4096,2048]{1,0:T(8,128)(2,1)S(1)} %get-tuple-element.111.refs_2_.refs_3_.refs_1_), custom_call_target="tpu_custom_call" | custom-call | tf_op jit(solution)/shard_map/down/pallas_call | solution.py:514
  71.8 0.5 collective-permute-done.16.refs_1_
  72.3 1.4 %down.3 = (bf16[80,1024]{1,0:T(8,128)(2,1)S(1)}, bf16[80,1024]{1,0:T(8,128)(2,1)S(1)}, bf16[160,2048]{1,0:T(8,128)(2,1)S(1)}) custom-call(bf16[160,4096]{1,0:T(8,128)(2,1)S(1)} %get-tuple-element.109.refs_0_, bf16[160,4096]{1,0:T(8,128)(2,1)S(1)} %collective-permute-done.16.refs_1_, f32[160,128]{1,0:T(8,128)S(1)} %get-tuple-element.112.refs_2_, ...), custom_call_target="tpu_custom_call" | custom-call | tf_op jit(solution)/shard_map/down/pallas_call | solution.py:514
  73.7 1.6 %collective-permute-start.19 = (bf16[80,1024]{1,0:T(8,128)(2,1)S(1)}, bf16[80,1024]{1,0:T(8,128)(2,1)S(1)}, u32[]{:S(2)}, u32[]{:S(2)}) collective-permute-start(bf16[80,1024]{1,0:T(8,128)(2,1)S(1)} %get-tuple-element.117), channel_id=1, source_target_pairs={{0,2},{2,0},{1,3},{3,1},{4,6},{6,4},{5,7},{7,5},{8,10},{10,8},{9,1... | collective-permute-start | bytes 491528 | tf_op jit(solution)/shard_map/sum_experts/ppermute | solution.py:699
  75.3 0.5 collective-permute-start.18
  75.8 0.9 sum_experts.1
  76.7 6.0 %collective-permute-start.21 = (bf16[64,1024]{1,0:T(8,128)(2,1)S(1)}, bf16[64,1024]{1,0:T(8,128)(2,1)S(1)}, u32[]{:S(2)}, u32[]{:S(2)}) collective-permute-start(bf16[64,1024]{1,0:T(8,128)(2,1)S(1)} %get-tuple-element.126), channel_id=1, source_target_pairs={{0,8},{6,14},{9,1},{15,7},{16,24},{22,30},{25,17},{31,23}} | collective-permute-start | bytes 393224 | tf_op jit(solution)/shard_map/reply/stream_home/ppermute | solution.py:563
  82.7 1.3 %collective-permute-start.22 = (bf16[64,1024]{1,0:T(8,128)(2,1)S(1)}, bf16[64,1024]{1,0:T(8,128)(2,1)S(1)}, u32[]{:S(2)}, u32[]{:S(2)}) collective-permute-start(bf16[64,1024]{1,0:T(8,128)(2,1)S(1)} %get-tuple-element.128), channel_id=1, source_target_pairs={{0,12},{6,10},{9,5},{15,3},{16,28},{22,26},{25,21},{31,19}} | collective-permute-start | bytes 393224 | tf_op jit(solution)/shard_map/reply/stream_home/ppermute | solution.py:563
  84.2 3.7 %collective-permute-start.20 = (bf16[64,1024]{1,0:T(8,128)(2,1)S(1)}, bf16[64,1024]{1,0:T(8,128)(2,1)S(1)}, u32[]{:S(2)}, u32[]{:S(2)}) collective-permute-start(bf16[64,1024]{1,0:T(8,128)(2,1)S(1)} %get-tuple-element.124), channel_id=1, source_target_pairs={{0,4},{6,2},{9,13},{15,11},{16,20},{22,18},{25,29},{31,27}} | collective-permute-start | bytes 393224 | tf_op jit(solution)/shard_map/reply/stream_home/ppermute | solution.py:563
  88.0 2.1 %collective-permute-start.25 = (bf16[40,1024]{1,0:T(8,128)(2,1)S(1)}, bf16[40,1024]{1,0:T(8,128)(2,1)S(1)}, u32[]{:S(2)}, u32[]{:S(2)}) collective-permute-start(bf16[40,1024]{1,0:T(8,128)(2,1)S(1)} %get-tuple-element.130), channel_id=1, source_target_pairs={{0,12},{1,13},{2,14},{3,15},{4,8},{5,9},{6,10},{7,11},{8,4},{9,5},... | collective-permute-start | bytes 245768 | tf_op jit(solution)/shard_map/reply/ppermute | solution.py:563
  90.1 1.3 %collective-permute-start.24 = (bf16[40,1024]{1,0:T(8,128)(2,1)S(1)}, bf16[40,1024]{1,0:T(8,128)(2,1)S(1)}, u32[]{:S(2)}, u32[]{:S(2)}) collective-permute-start(bf16[40,1024]{1,0:T(8,128)(2,1)S(1)} %get-tuple-element.120), channel_id=1, source_target_pairs={{0,8},{1,9},{2,10},{3,11},{4,12},{5,13},{6,14},{7,15},{8,0},{9,1},... | collective-permute-start | bytes 245768 | tf_op jit(solution)/shard_map/reply/ppermute | solution.py:563
  91.4 1.1 %collective-permute-done.23.refs_7_ = bf16[40,1024]{1,0:T(8,128)(2,1)S(1)} collective-permute-done((bf16[40,1024]{1,0:T(8,128)(2,1)S(1)}, bf16[40,1024]{1,0:T(8,128)(2,1)S(1)}, u32[]{:S(2)}, u32[]{:S(2)}) %collective-permute-start.23) | collective-permute-done | bytes 81952 | tf_op jit(solution)/shard_map/reply/ppermute | solution.py:563
  92.5 2.8 %collective-permute-done.25.refs_9_ = bf16[40,1024]{1,0:T(8,128)(2,1)S(1)} collective-permute-done((bf16[40,1024]{1,0:T(8,128)(2,1)S(1)}, bf16[40,1024]{1,0:T(8,128)(2,1)S(1)}, u32[]{:S(2)}, u32[]{:S(2)}) %collective-permute-start.25) | collective-permute-done | bytes 81952 | tf_op jit(solution)/shard_map/reply/ppermute | solution.py:563
  95.3 3.4 %collective-permute-done.24.refs_8_ = bf16[40,1024]{1,0:T(8,128)(2,1)S(1)} collective-permute-done((bf16[40,1024]{1,0:T(8,128)(2,1)S(1)}, bf16[40,1024]{1,0:T(8,128)(2,1)S(1)}, u32[]{:S(2)}, u32[]{:S(2)}) %collective-permute-start.24) | collective-permute-done | bytes 81952 | tf_op jit(solution)/shard_map/reply/ppermute | solution.py:563
  98.8 1.1 %finish.1 = bf16[64,1024]{1,0:T(8,128)(2,1)} custom-call(bf16[64,1024]{1,0:T(8,128)(2,1)S(1)} %get-tuple-element.86.refs_0_, bf16[64,1024]{1,0:T(8,128)(2,1)S(1)} %collective-permute-done.20.refs_1_, bf16[64,1024]{1,0:T(8,128)(2,1)S(1)} %collective-permute-done.21.refs_2_, bf16[64,1024]{1,0:T(8,128)(2,1)S(1)} %collective-permute-done.22.refs_3_, ...), custom_call_target="tpu_custom_call" | custom-call | tf_op jit(solution)/shard_map/finish/pallas_call | solution.py:514
  (29 shorter events, 1.0 us)
Async XLA Ops:
  0.0 21.3 %collective-permute-start.5 = (bf16[1024,1024]{1,0:T(8,128)(2,1)}, bf16[1024,1024]{1,0:T(8,128)(2,1)S(1)}, u32[]{:S(2)}, u32[]{:S(2)}) collective-permute-start(bf16[1024,1024]{1,0:T(8,128)(2,1)} %refs_0_.3), channel_id=1, source_target_pairs={{0,1},{1,0},{2,3},{3,2},{4,5},{5,4},{6,7},{7,6},{8,9},{9,8},{10,11... | collective-permute-start | bytes 6291464 | tf_op jit(solution)/shard_map/ppermute | solution.py:572
  3.5 7.2 %collective-permute-start.2 = (bf16[144,128]{1,0:T(8,128)(2,1)S(1)}, bf16[144,128]{1,0:T(8,128)(2,1)S(1)}, u32[]{:S(2)}, u32[]{:S(2)}) collective-permute-start(bf16[144,128]{1,0:T(8,128)(2,1)S(1)} %get-tuple-element.68), channel_id=1, source_target_pairs={{0,12},{1,13},{2,14},{3,15},{4,8},{5,9},{6,10},{7,11},{8,4},{9,5},... | collective-permute-start | bytes 110600 | tf_op jit(solution)/shard_map/relay/ppermute | solution.py:563
  8.2 4.9 %collective-permute-start.1 = (bf16[144,128]{1,0:T(8,128)(2,1)S(1)}, bf16[144,128]{1,0:T(8,128)(2,1)S(1)}, u32[]{:S(2)}, u32[]{:S(2)}) collective-permute-start(bf16[144,128]{1,0:T(8,128)(2,1)S(1)} %get-tuple-element.68), channel_id=1, source_target_pairs={{0,8},{1,9},{2,10},{3,11},{4,12},{5,13},{6,14},{7,15},{8,0},{9,1},... | collective-permute-start | bytes 110600 | tf_op jit(solution)/shard_map/relay/ppermute | solution.py:563
  8.2 4.9 %collective-permute-start = (bf16[144,128]{1,0:T(8,128)(2,1)S(1)}, bf16[144,128]{1,0:T(8,128)(2,1)S(1)}, u32[]{:S(2)}, u32[]{:S(2)}) collective-permute-start(bf16[144,128]{1,0:T(8,128)(2,1)S(1)} %get-tuple-element.68), channel_id=1, source_target_pairs={{0,4},{1,5},{2,6},{3,7},{4,0},{5,1},{6,2},{7,3},{8,12},{9,13},{10,... | collective-permute-start | bytes 110600 | tf_op jit(solution)/shard_map/relay/ppermute | solution.py:563
  13.6 1.4 %collective-permute-start.3 = (bf16[64,1024]{1,0:T(8,128)(2,1)S(1)}, bf16[64,1024]{1,0:T(8,128)(2,1)S(1)}, u32[]{:S(2)}, u32[]{:S(2)}) collective-permute-start(bf16[64,1024]{1,0:T(8,128)(2,1)S(1)} %correct.1.refs_0_), channel_id=1, source_target_pairs={{0,1},{1,0},{2,3},{3,2},{4,5},{5,4},{6,7},{7,6},{8,9},{9,8},{10,11... | collective-permute-start | bytes 393224 | tf_op jit(solution)/shard_map/gather_gated/ppermute | solution.py:572
  16.1 10.2 %collective-permute-start.4 = (bf16[64,2688]{1,0:T(8,128)(2,1)S(1)}, bf16[64,2688]{1,0:T(8,128)(2,1)S(1)}, u32[]{:S(2)}, u32[]{:S(2)}) collective-permute-start(bf16[64,2688]{1,0:T(8,128)(2,1)S(1)} %get-tuple-element.79), channel_id=1, source_target_pairs={{4,0},{6,2},{0,4},{2,6},{13,9},{15,11},{9,13},{11,15},{20,16},{22,... | collective-permute-start | bytes 1032200 | tf_op jit(solution)/shard_map/gather_gated/ppermute | solution.py:563
  18.6 19.7 %collective-permute-start.10 = (bf16[64,2688]{1,0:T(8,128)(2,1)S(1)}, bf16[64,2688]{1,0:T(8,128)(2,1)S(1)}, u32[]{:S(2)}, u32[]{:S(2)}) collective-permute-start(bf16[64,2688]{1,0:T(8,128)(2,1)S(1)} %get-tuple-element.92), channel_id=1, source_target_pairs={{8,0},{10,2},{12,4},{14,6},{1,9},{3,11},{5,13},{7,15},{24,16},{26,... | collective-permute-start | bytes 1032200 | tf_op jit(solution)/shard_map/gather_gated/ppermute | solution.py:563
  19.9 18.5 %collective-permute-start.11 = (bf16[64,2688]{1,0:T(8,128)(2,1)S(1)}, bf16[64,2688]{1,0:T(8,128)(2,1)S(1)}, u32[]{:S(2)}, u32[]{:S(2)}) collective-permute-start(bf16[64,2688]{1,0:T(8,128)(2,1)S(1)} %get-tuple-element.93), channel_id=1, source_target_pairs={{12,0},{14,2},{8,4},{10,6},{5,9},{7,11},{1,13},{3,15},{28,16},{30,... | collective-permute-start | bytes 1032200 | tf_op jit(solution)/shard_map/gather_gated/ppermute | solution.py:563
  27.1 8.3 %collective-permute-start.6 = (bf16[128,1024]{1,0:T(8,128)(2,1)S(1)}, bf16[128,1024]{1,0:T(8,128)(2,1)S(1)}, u32[]{:S(2)}, u32[]{:S(2)}) collective-permute-start(bf16[128,1024]{1,0:T(8,128)(2,1)S(1)} %get-tuple-element.81.refs_2_.refs_0_), channel_id=1, source_target_pairs={{0,2},{2,0},{4,6},{6,4},{9,11},{11,9},{13,15},{15,13},{16,18},{18,... | collective-permute-start | bytes 786440 | tf_op jit(solution)/shard_map/sum_exp/ppermute | solution.py:563
  35.8 17.3 %collective-permute-start.7 = (bf16[80,1024]{1,0:T(8,128)(2,1)S(1)}, bf16[80,1024]{1,0:T(8,128)(2,1)S(1)}, u32[]{:S(2)}, u32[]{:S(2)}) collective-permute-start(bf16[80,1024]{1,0:T(8,128)(2,1)S(1)} %get-tuple-element.89), channel_id=1, source_target_pairs={{0,4},{2,6},{4,0},{6,2},{9,13},{11,15},{13,9},{15,11},{16,20},{18,... | collective-permute-start | bytes 491528 | tf_op jit(solution)/shard_map/dispatch/ppermute | solution.py:563
  39.2 8.3 %collective-permute-start.12 = (bf16[128,1024]{1,0:T(8,128)(2,1)S(1)}, bf16[128,1024]{1,0:T(8,128)(2,1)S(1)}, u32[]{:S(2)}, u32[]{:S(2)}) collective-permute-start(bf16[128,1024]{1,0:T(8,128)(2,1)S(1)} %get-tuple-element.96.refs_0_), channel_id=1, source_target_pairs={{0,2},{2,0},{4,6},{6,4},{9,11},{11,9},{13,15},{15,13},{16,18},{18,... | collective-permute-start | bytes 786440 | tf_op jit(solution)/shard_map/sum_exp/ppermute | solution.py:563
  42.7 16.4 %collective-permute-start.8 = (bf16[80,1024]{1,0:T(8,128)(2,1)S(1)}, bf16[80,1024]{1,0:T(8,128)(2,1)S(1)}, u32[]{:S(2)}, u32[]{:S(2)}) collective-permute-start(bf16[80,1024]{1,0:T(8,128)(2,1)S(1)} %get-tuple-element.90), channel_id=1, source_target_pairs={{0,8},{2,10},{4,12},{6,14},{9,1},{11,3},{13,5},{15,7},{16,24},{18,... | collective-permute-start | bytes 491528 | tf_op jit(solution)/shard_map/dispatch/ppermute | solution.py:563
  44.0 15.1 %collective-permute-start.9 = (bf16[80,1024]{1,0:T(8,128)(2,1)S(1)}, bf16[80,1024]{1,0:T(8,128)(2,1)S(1)}, u32[]{:S(2)}, u32[]{:S(2)}) collective-permute-start(bf16[80,1024]{1,0:T(8,128)(2,1)S(1)} %get-tuple-element.91), channel_id=1, source_target_pairs={{0,12},{2,14},{4,8},{6,10},{9,5},{11,7},{13,1},{15,3},{16,28},{18,... | collective-permute-start | bytes 491528 | tf_op jit(solution)/shard_map/dispatch/ppermute | solution.py:563
  47.9 11.2 %collective-permute-start.13 = (bf16[80,1024]{1,0:T(8,128)(2,1)S(1)}, bf16[80,1024]{1,0:T(8,128)(2,1)S(1)}, u32[]{:S(2)}, u32[]{:S(2)}) collective-permute-start(bf16[80,1024]{1,0:T(8,128)(2,1)S(1)} %get-tuple-element.100), channel_id=1, source_target_pairs={{0,4},{2,6},{4,0},{6,2},{9,13},{11,15},{13,9},{15,11},{16,20},{18,... | collective-permute-start | bytes 491528 | tf_op jit(solution)/shard_map/dispatch/ppermute | solution.py:563
  51.7 7.3 %collective-permute-start.14 = (bf16[80,1024]{1,0:T(8,128)(2,1)S(1)}, bf16[80,1024]{1,0:T(8,128)(2,1)S(1)}, u32[]{:S(2)}, u32[]{:S(2)}) collective-permute-start(bf16[80,1024]{1,0:T(8,128)(2,1)S(1)} %get-tuple-element.101), channel_id=1, source_target_pairs={{0,8},{2,10},{4,12},{6,14},{9,1},{11,3},{13,5},{15,7},{16,24},{18,... | collective-permute-start | bytes 491528 | tf_op jit(solution)/shard_map/dispatch/ppermute | solution.py:563
  53.0 6.0 %collective-permute-start.15 = (bf16[80,1024]{1,0:T(8,128)(2,1)S(1)}, bf16[80,1024]{1,0:T(8,128)(2,1)S(1)}, u32[]{:S(2)}, u32[]{:S(2)}) collective-permute-start(bf16[80,1024]{1,0:T(8,128)(2,1)S(1)} %get-tuple-element.102), channel_id=1, source_target_pairs={{0,12},{2,14},{4,8},{6,10},{9,5},{11,7},{13,1},{15,3},{16,28},{18,... | collective-permute-start | bytes 491528 | tf_op jit(solution)/shard_map/dispatch/ppermute | solution.py:563
  63.2 6.4 %collective-permute-start.17 = (bf16[160,4224]{1,0:T(8,128)(2,1)S(1)}, bf16[160,4224]{1,0:T(8,128)(2,1)S(1)}, u32[]{:S(2)}, u32[]{:S(2)}) collective-permute-start(bf16[160,4224]{1,0:T(8,128)(2,1)S(1)} %get-tuple-element.110.refs_0_), channel_id=1, source_target_pairs={{0,1},{1,0},{2,3},{3,2},{4,5},{5,4},{6,7},{7,6},{8,9},{9,8},{10,11... | collective-permute-start | bytes 4055048 | tf_op jit(solution)/shard_map/gate_up/ppermute | solution.py:572
  69.1 3.2 %collective-permute-start.16 = (bf16[160,4096]{1,0:T(8,128)(2,1)S(1)}, bf16[160,4096]{1,0:T(8,128)(2,1)S(1)}, u32[]{:S(2)}, u32[]{:S(2)}) collective-permute-start(bf16[160,4096]{1,0:T(8,128)(2,1)S(1)} %get-tuple-element.109.refs_0_), channel_id=1, source_target_pairs={{0,1},{1,0},{2,3},{3,2},{4,5},{5,4},{6,7},{7,6},{8,9},{9,8},{10,11... | collective-permute-start | bytes 3932168 | tf_op jit(solution)/shard_map/gate_up/ppermute | solution.py:572
  72.3 26.4 %copy-start = (f32[64,2]{0,1:T(2,128)S(1)}, f32[64,2]{0,1:T(2,128)}, u32[]{:S(2)}) copy-start(f32[64,2]{0,1:T(2,128)} %param.26) | copy-start | bytes 1540
  73.7 10.3 %collective-permute-start.19 = (bf16[80,1024]{1,0:T(8,128)(2,1)S(1)}, bf16[80,1024]{1,0:T(8,128)(2,1)S(1)}, u32[]{:S(2)}, u32[]{:S(2)}) collective-permute-start(bf16[80,1024]{1,0:T(8,128)(2,1)S(1)} %get-tuple-element.117), channel_id=1, source_target_pairs={{0,2},{2,0},{1,3},{3,1},{4,6},{6,4},{5,7},{7,5},{8,10},{10,8},{9,1... | collective-permute-start | bytes 491528 | tf_op jit(solution)/shard_map/sum_experts/ppermute | solution.py:699
  75.3 8.8 %collective-permute-start.18 = (bf16[80,1024]{1,0:T(8,128)(2,1)S(1)}, bf16[80,1024]{1,0:T(8,128)(2,1)S(1)}, u32[]{:S(2)}, u32[]{:S(2)}) collective-permute-start(bf16[80,1024]{1,0:T(8,128)(2,1)S(1)} %get-tuple-element.118), channel_id=1, source_target_pairs={{0,2},{2,0},{1,3},{3,1},{4,6},{6,4},{5,7},{7,5},{8,10},{10,8},{9,1... | collective-permute-start | bytes 491528 | tf_op jit(solution)/shard_map/sum_experts/ppermute | solution.py:701
  76.7 13.4 %collective-permute-start.21 = (bf16[64,1024]{1,0:T(8,128)(2,1)S(1)}, bf16[64,1024]{1,0:T(8,128)(2,1)S(1)}, u32[]{:S(2)}, u32[]{:S(2)}) collective-permute-start(bf16[64,1024]{1,0:T(8,128)(2,1)S(1)} %get-tuple-element.126), channel_id=1, source_target_pairs={{0,8},{6,14},{9,1},{15,7},{16,24},{22,30},{25,17},{31,23}} | collective-permute-start | bytes 393224 | tf_op jit(solution)/shard_map/reply/stream_home/ppermute | solution.py:563
  82.7 8.8 %collective-permute-start.22 = (bf16[64,1024]{1,0:T(8,128)(2,1)S(1)}, bf16[64,1024]{1,0:T(8,128)(2,1)S(1)}, u32[]{:S(2)}, u32[]{:S(2)}) collective-permute-start(bf16[64,1024]{1,0:T(8,128)(2,1)S(1)} %get-tuple-element.128), channel_id=1, source_target_pairs={{0,12},{6,10},{9,5},{15,3},{16,28},{22,26},{25,21},{31,19}} | collective-permute-start | bytes 393224 | tf_op jit(solution)/shard_map/reply/stream_home/ppermute | solution.py:563
  84.2 14.6 %collective-permute-start.20 = (bf16[64,1024]{1,0:T(8,128)(2,1)S(1)}, bf16[64,1024]{1,0:T(8,128)(2,1)S(1)}, u32[]{:S(2)}, u32[]{:S(2)}) collective-permute-start(bf16[64,1024]{1,0:T(8,128)(2,1)S(1)} %get-tuple-element.124), channel_id=1, source_target_pairs={{0,4},{6,2},{9,13},{15,11},{16,20},{22,18},{25,29},{31,27}} | collective-permute-start | bytes 393224 | tf_op jit(solution)/shard_map/reply/stream_home/ppermute | solution.py:563
  87.9 4.7 %collective-permute-start.23 = (bf16[40,1024]{1,0:T(8,128)(2,1)S(1)}, bf16[40,1024]{1,0:T(8,128)(2,1)S(1)}, u32[]{:S(2)}, u32[]{:S(2)}) collective-permute-start(bf16[40,1024]{1,0:T(8,128)(2,1)S(1)} %get-tuple-element.123), channel_id=1, source_target_pairs={{0,4},{1,5},{2,6},{3,7},{4,0},{5,1},{6,2},{7,3},{8,12},{9,13},{10,... | collective-permute-start | bytes 245768 | tf_op jit(solution)/shard_map/reply/ppermute | solution.py:563
  88.0 7.3 %collective-permute-start.25 = (bf16[40,1024]{1,0:T(8,128)(2,1)S(1)}, bf16[40,1024]{1,0:T(8,128)(2,1)S(1)}, u32[]{:S(2)}, u32[]{:S(2)}) collective-permute-start(bf16[40,1024]{1,0:T(8,128)(2,1)S(1)} %get-tuple-element.130), channel_id=1, source_target_pairs={{0,12},{1,13},{2,14},{3,15},{4,8},{5,9},{6,10},{7,11},{8,4},{9,5},... | collective-permute-start | bytes 245768 | tf_op jit(solution)/shard_map/reply/ppermute | solution.py:563
  90.1 8.6 %collective-permute-start.24 = (bf16[40,1024]{1,0:T(8,128)(2,1)S(1)}, bf16[40,1024]{1,0:T(8,128)(2,1)S(1)}, u32[]{:S(2)}, u32[]{:S(2)}) collective-permute-start(bf16[40,1024]{1,0:T(8,128)(2,1)S(1)} %get-tuple-element.120), channel_id=1, source_target_pairs={{0,8},{1,9},{2,10},{3,11},{4,12},{5,13},{6,14},{7,15},{8,0},{9,1},... | collective-permute-start | bytes 245768 | tf_op jit(solution)/shard_map/reply/ppermute | solution.py:563

commit v4 on v3

--- a/solution.py
+++ b/solution.py
@@ -152,8 +152,27 @@
         store_ref[pl.ds(k, rows, stride=count), :] = value[:, k * 128 : (k + 1) * 128]
 
 
+def slots_of(ids, lanes):
+    count = ids.shape[1]
+    ids = ids.astype(f32)
+    first, second = ids[0:1, :], ids[1:2, :]
+    expert = lax.broadcasted_iota(jnp.int32, (8, count), 0).astype(f32)
+    member = (jnp.where(expert == first, 1.0, 0.0) + jnp.where(expert == second, 1.0, 0.0)).astype(bf16)
+    before = lax.broadcasted_iota(jnp.int32, (count, count), 0)
+    token = lax.broadcasted_iota(jnp.int32, (count, count), 1)
+    rank = jnp.dot(member, jnp.where(before < token, 1.0, 0.0).astype(bf16), preferred_element_type=f32)
+    slot = [
+        which * CAP + jnp.sum(jnp.where(expert == which, rank, 0.0), axis=0, keepdims=True) for which in (first, second)
+    ]
+    both = jnp.where(expert == 0, slot[0], jnp.where(expert == 1, slot[1], 0.0))
+    row = lax.broadcasted_iota(jnp.int32, (count, lanes), 0)
+    lane = lax.broadcasted_iota(jnp.int32, (count, lanes), 1)
+    repeat = (row == lane) | (row + count == lane)
+    return jnp.dot(both.astype(bf16), jnp.where(repeat, 1.0, 0.0).astype(bf16), preferred_element_type=f32)
+
+
 def scan_kernel(
-    b_ref, c_ref, dt_ref, conv_ref, z_ref, alog_ref, skip_ref,
+    b_ref, c_ref, dt_ref, conv_ref, z_ref, alog_ref, skip_ref, ids_ref,
     base_ref, cum_ref, silu_ref, rate_ref, pack_ref, step_s, in_s, z_s, alog_s,
 ):
     tokens, width = dt_ref.shape
@@ -187,13 +206,15 @@
     state, cum = lax.fori_loop(0, tokens, advance, ((zero,) * states, zero), unroll=2)
     z = z_s[...]
     silu_ref[...] = z / (1.0 + jnp.exp(-z))
-    pack_ref[...] = jnp.concatenate(list(state) + [cum, zero], axis=0).astype(bf16)
-
-
-def spread_kernel(c_ref, base_ref, cum_ref, silu_ref, rate_ref, out_ref, weight_ref):
+    pack_ref[...] = jnp.concatenate(list(state) + [cum, slots_of(ids_ref[...], 128)], axis=0).astype(bf16)
+
+
+def spread_kernel(c_ref, base_ref, cum_ref, silu_ref, rate_ref, resid_ref, out_ref, weight_ref, near_ref, sem):
     states = c_ref.shape[0]
     g = rate_ref.shape[0] // states
     tokens = base_ref.shape[0] // g
+    copy = pltpu.make_async_copy(resid_ref, near_ref, sem)
+    copy.start()
     out_ref[...] = base_ref[...] * silu_ref[...]
 
     def one(t, _):
@@ -206,6 +227,7 @@
         return 0
 
     lax.fori_loop(0, tokens, one, 0, unroll=2)
+    copy.wait()
 
 
 def correct_kernel(one_ref, two_ref, three_ref, base_ref, weight_ref, rate_ref, out_ref, gated_s):
@@ -242,49 +264,43 @@
         out_ref[:, k * 128 : (k + 1) * 128] = gated_s[pl.ds(k, tokens, stride=g), :].astype(bf16)
 
 
-def route_kernel(ids_ref, lanes_ref, cols_ref):
-    count = cols_ref.shape[0]
-    ids = ids_ref[...].astype(f32)
-    first, second = ids[0:1, :], ids[1:2, :]
-    expert = lax.broadcasted_iota(jnp.int32, (8, count), 0).astype(f32)
-    member = (jnp.where(expert == first, 1.0, 0.0) + jnp.where(expert == second, 1.0, 0.0)).astype(bf16)
-    before = lax.broadcasted_iota(jnp.int32, (count, count), 0)
-    token = lax.broadcasted_iota(jnp.int32, (count, count), 1)
-    rank = jnp.dot(member, jnp.where(before < token, 1.0, 0.0).astype(bf16), preferred_element_type=f32)
-    slot = [
-        which * CAP + jnp.sum(jnp.where(expert == which, rank, 0.0), axis=0, keepdims=True) for which in (first, second)
-    ]
-    both = jnp.where(expert == 0, slot[0], jnp.where(expert == 1, slot[1], 0.0))
-    lanes_ref[...] = both
-    same = lax.broadcasted_iota(jnp.int32, (8, 128), 0) == lax.broadcasted_iota(jnp.int32, (8, 128), 1)
-    cols_ref[...] = lax.dot_general(
-        both.astype(bf16), jnp.where(same, 1.0, 0.0).astype(bf16), (((0,), (0,)), ((), ())), preferred_element_type=f32
-    ).astype(bf16)
-
-
-def pack_kernel(own_ref, peer_ref, resid_ref, slots_ref, m0_ref, m1_ref, m2_ref, m3_ref):
+def pack_kernel(own_ref, peer_ref, resid_ref, m0_ref, m1_ref, m2_ref, m3_ref):
     ctx, exp = lax.axis_index("ctx"), lax.axis_index("exp")
     width = own_ref.shape[1]
-    part = m0_ref.shape[1] - 2 * width - 128
+    part = m0_ref.shape[1] - 2 * width
     for p, ref in enumerate((m0_ref, m1_ref, m2_ref, m3_ref)):
         ref[:, :width] = own_ref[...]
         ref[:, width : 2 * width] = peer_ref[...]
         begin = pl.multiple_of((ctx ^ p) * 2 * part + exp * part, 128)
-        ref[:, 2 * width : 2 * width + part] = resid_ref[:, pl.ds(begin, part)]
-        ref[:, 2 * width + part :] = slots_ref[...]
-
-
-def hold_out_kernel(own_ref, peer_ref, after_ref, out_ref, sems):
-    half = own_ref.shape[0]
-    copies = [
-        pltpu.make_async_copy(ref, out_ref.at[pl.ds(k * half, half)], sems.at[k]) for k, ref in enumerate((own_ref, peer_ref))
-    ]
+        ref[:, 2 * width :] = resid_ref[:, pl.ds(begin, part)]
+
+
+def part_copy(source_ref, begin, held_ref, place, sem, rows=None):
+    height, cols = source_ref.shape[0], held_ref.shape[1]
+    first, count = rows or (0, height)
+    return pltpu.make_async_copy(
+        source_ref.at[pl.ds(first, count), pl.ds(begin, cols)], held_ref.at[pl.ds(place * height + first, count)], sem
+    )
+
+
+def wait_all(copies):
     for copy in copies:
         copy.start()
     for copy in copies:
         copy.wait()
 
 
+def hold_out_kernel(own_ref, peer_ref, gate_ref, after_ref, out_ref, held_ref, sems):
+    half = own_ref.shape[0]
+    wait_all([
+        *(
+            pltpu.make_async_copy(ref, out_ref.at[pl.ds(k * half, half)], sems.at[k])
+            for k, ref in enumerate((own_ref, peer_ref))
+        ),
+        part_copy(gate_ref, 0, held_ref, 0, sems.at[2], (0, gate_ref.shape[0] // 2)),
+    ])
+
+
 def after_kernel(earlier_ref, token_ref):
     token_ref[...] = jnp.zeros_like(token_ref)
 
@@ -295,7 +311,7 @@
     scratch[pl.ds(pl.multiple_of((1 - odd) * rows, rows), rows), :] = second
 
 
-def project_kernel(first_ref, second_ref, w_ref, after_ref, out_ref, slots_ref, rows_s):
+def project_kernel(first_ref, second_ref, after_ref, out_ref, w_ref, held_ref, rows_s):
     place_pair(rows_s, lax.axis_index("ctx") % 2, first_ref[...], second_ref[...])
     exp = lax.axis_index("exp")
     depth = w_ref.shape[0]
@@ -305,11 +321,10 @@
     for side in range(2):
         value = jnp.dot(feats, w_ref[:, side * part : (side + 1) * part], preferred_element_type=f32)
         out_ref[:, side * part : (side + 1) * part] = (value + jnp.where(exp == side, resid, 0.0)).astype(bf16)
-    slots_ref[...] = rows_s[:, depth + part :]
 
 
 def select_kernel(
-    own_ref, peer_ref, slots_ref, after_ref, stream_first_ref, stream_second_ref, d0_ref, d1_ref, d2_ref, d3_ref, rows_s
+    own_ref, peer_ref, first_ref, second_ref, after_ref, stream_first_ref, stream_second_ref, d0_ref, d1_ref, d2_ref, d3_ref, rows_s
 ):
     ctx = lax.axis_index("ctx")
     odd = ctx % 2
@@ -318,7 +333,10 @@
     stream_first_ref[...] = rows_s[pl.ds(pl.multiple_of(odd * block, block), block), :]
     stream_second_ref[...] = rows_s[pl.ds(pl.multiple_of((1 - odd) * block, block), block), :]
     feats = rows_s[...]
-    slots = slots_ref[...].astype(f32).T
+    top = first_ref.shape[0] - 16
+    first, second = first_ref[top:, :].astype(f32), second_ref[top:, :].astype(f32)
+    lane = lax.broadcasted_iota(jnp.int32, first.shape, 1)
+    slots = jnp.where((lane >= block) == (odd == 0), second, first)
     count = d0_ref.shape[0]
     row = lax.broadcasted_iota(jnp.int32, (count, 2 * block), 0)
     lane = lax.broadcasted_iota(jnp.int32, (count, 2 * block), 1)
@@ -327,38 +345,19 @@
     want = jnp.where(late, row - CAP, row).astype(f32)
     for p, ref in enumerate((d0_ref, d1_ref, d2_ref, d3_ref)):
         base = ((ctx ^ p) * CAP).astype(f32)
-        hit = mine & ((slots[0:1, :] == want + base) | (slots[1:2, :] == want + base))
+        hit = mine & ((slots[8:9, :] == want + base) | (slots[9:10, :] == want + base))
         pick = jnp.where(hit, 1.0, 0.0).astype(bf16)
         ref[...] = jnp.dot(pick, feats, preferred_element_type=f32).astype(bf16)
 
 
-def part_copy(source_ref, begin, held_ref, place, sem, rows=None):
-    height, cols = source_ref.shape[0], held_ref.shape[1]
-    first, count = rows or (0, height)
-    return pltpu.make_async_copy(
-        source_ref.at[pl.ds(first, count), pl.ds(begin, cols)], held_ref.at[pl.ds(place * height + first, count)], sem
-    )
-
-
-def wait_all(copies):
-    for copy in copies:
-        copy.start()
-    for copy in copies:
-        copy.wait()
-
-
 def hold_early_kernel(gate_ref, up_ref, after_ref, token_ref, held_ref, sems):
     token_ref[...] = jnp.zeros_like(token_ref)
-    rows = up_ref.shape[0] // 2
-    wait_all([part_copy(gate_ref, 0, held_ref, 0, sems.at[0]), part_copy(up_ref, 0, held_ref, 1, sems.at[1], (0, rows))])
-
-
-def hold_late_kernel(gate_ref, up_ref, after_ref, held_second_ref, held_ref, sems):
-    rows = up_ref.shape[0] // 2
-    wait_all([
-        part_copy(up_ref, 0, held_ref, 1, sems.at[0], (rows, rows)),
-        part_copy(gate_ref, held_ref.shape[1], held_second_ref, 0, sems.at[1]),
-    ])
+    rows = gate_ref.shape[0] // 2
+    wait_all([part_copy(gate_ref, 0, held_ref, 0, sems.at[0], (rows, rows)), part_copy(up_ref, 0, held_ref, 1, sems.at[1])])
+
+
+def hold_late_kernel(gate_ref, after_ref, held_second_ref, sem):
+    wait_all([part_copy(gate_ref, held_second_ref.shape[1], held_second_ref, 0, sem)])
 
 
 def gate_up(feats, held_ref, out_ref):
@@ -413,7 +412,8 @@
 
 
 def second_half_kernel(feats_ref, wd_ref, out_ref, down_ref, held_ref, sem):
-    copy = pltpu.make_async_copy(wd_ref, down_ref, sem)
+    rows = wd_ref.shape[0] // 2
+    copy = pltpu.make_async_copy(wd_ref.at[pl.ds(0, rows)], down_ref.at[pl.ds(0, rows)], sem)
     copy.start()
     gate_up(feats_ref[...], held_ref, out_ref)
     copy.wait()
@@ -433,13 +433,17 @@
     return (gate / (1.0 + jnp.exp(-gate)) * up).astype(bf16)
 
 
-def down_first_kernel(features, own_ref, peer_ref, held_ref, out_ref, scale_ref):
+def down_first_kernel(features, own_ref, peer_ref, wd_ref, out_ref, scale_ref, held_ref, sem):
+    rows = wd_ref.shape[0] // 2
+    copy = pltpu.make_async_copy(wd_ref.at[pl.ds(rows, rows)], held_ref.at[pl.ds(rows, rows)], sem)
+    copy.start()
     scale_ref[...] = scale_of(own_ref, peer_ref, features)
     hidden = hidden_of(own_ref, peer_ref, scale_ref[:, 0:1])
     depth = hidden.shape[1]
     block = min(512, out_ref.shape[1])
     for n in range(0, out_ref.shape[1], block):
         out_ref[:, n : n + block] = jnp.dot(hidden, held_ref[:depth, n : n + block], preferred_element_type=f32)
+    copy.wait()
 
 
 def down_piece(hidden, held_ref, acc_ref, near_ref, far_ref, sum_s, piece):
@@ -452,14 +456,12 @@
     far_ref[...] = sum_s[pl.ds(pl.multiple_of((1 - pair) * count, count), count), :].astype(bf16)
 
 
-def down_theirs_kernel(
-    own_ref, peer_ref, scale_ref, held_ref, acc_ref, near_ref, far_ref, hidden_ref, sum_s
-):
+def down_theirs_kernel(own_ref, peer_ref, scale_ref, acc_ref, near_ref, far_ref, hidden_ref, held_ref, sum_s):
     hidden_ref[...] = hidden_of(own_ref, peer_ref, scale_ref[:, 0:1])
     down_piece(hidden_ref[...], held_ref, acc_ref, near_ref, far_ref, sum_s, 1 - lax.axis_index("exp"))
 
 
-def down_mine_kernel(hidden_ref, held_ref, acc_ref, near_ref, far_ref, sum_s):
+def down_mine_kernel(hidden_ref, acc_ref, near_ref, far_ref, held_ref, sum_s):
     down_piece(hidden_ref[...], held_ref, acc_ref, near_ref, far_ref, sum_s, lax.axis_index("exp"))
 
 
@@ -472,7 +474,7 @@
 
 
 def finish_kernel(
-    s0_ref, s1_ref, s2_ref, s3_ref, slots_ref, weights_ref, r0_ref, r1_ref, r2_ref, r3_ref, out_ref
+    s0_ref, s1_ref, s2_ref, s3_ref, pack_ref, weights_ref, r0_ref, r1_ref, r2_ref, r3_ref, out_ref
 ):
     ctx = lax.axis_index("ctx")
     apart = ctx ^ (lax.axis_index("tp") * lax.axis_size("exp") + lax.axis_index("exp"))
@@ -480,6 +482,7 @@
     stream = s0_ref[...]
     for p, ref in ((1, s1_ref), (2, s2_ref), (3, s3_ref)):
         stream = jnp.where(apart == p, ref[...], stream)
+    slots = pack_ref[pack_ref.shape[0] - 16 :, :].astype(f32)[8:10, :tokens]
     total = stream.astype(f32)
     over_rows = (((0,), (0,)), ((), ()))
     want = lax.broadcasted_iota(jnp.int32, (r0_ref.shape[0], tokens), 0).astype(f32)
@@ -487,7 +490,7 @@
         base = ((ctx ^ p) * CAP).astype(f32)
         weight = jnp.zeros(want.shape, f32)
         for k in range(2):
-            weight = weight + jnp.where(slots_ref[k : k + 1, :] == want + base, weights_ref[k : k + 1, :], 0.0)
+            weight = weight + jnp.where(slots[k : k + 1, :] == want + base, weights_ref[k : k + 1, :], 0.0)
         high = weight.astype(bf16)
         low = (weight - high.astype(f32)).astype(bf16)
         rows = ref[...]
@@ -571,102 +574,98 @@
     def swap_tp(x):
         return lax.ppermute(x, "tp", [(i, tp_count - 1 - i) for i in range(tp_count)])
 
-    peer_weight = swap_tp(out_weight)
     with jax.named_scope("scan"):
         flat = shape(tokens * g, 128, f32)
         b_rows, c_rows = b_proj.T, c_proj.T
         base, cum, silu_z, rate, pack = call(
             scan_kernel,
             (flat, flat, flat, shape(states * g, 128, f32), shape((states + 2) * g, 128, bf16)),
-            [SM, SM] + [VM] * 5,
+            [SM, SM] + [VM] * 6,
             [pltpu.VMEM((tokens * g, 128), f32)] * 3 + [pltpu.VMEM((states * g, 128), f32)],
-            tuple(in_hbm(v) for v in (b_rows, c_rows, dt_raw, conv_out, gate_z, a_log, d_skip.reshape(g, 128))),
-        )
+            tuple(in_hbm(v) for v in (b_rows, c_rows, dt_raw, conv_out, gate_z, a_log, d_skip.reshape(g, 128), route_ids.T)),
+        )
+    peer_weight, _ = lax.optimization_barrier((out_weight, pack))
+    peer_weight = swap_tp(peer_weight)
     with jax.named_scope("relay"):
         entered = [
             permute(pack, [(number(c, x, t), number(c ^ p, x, t)) for c, x in chips for t in range(tp_count)])
             for p in away
         ]
     with jax.named_scope("spread"):
-        base, spread = call(
-            spread_kernel, (flat, shape(tokens * states * g, 128, f32)), [SM] + [VM] * 4, (),
-            (in_hbm(c_rows), base, cum, silu_z, rate), us=2.0,
+        base, spread, resid = call(
+            spread_kernel, (flat, shape(tokens * states * g, 128, f32), pltpu.VMEM(resid.shape, bf16)), [SM] + [VM] * 4 + [HB],
+            [pltpu.SemaphoreType.DMA], (in_hbm(c_rows), base, cum, silu_z, rate, in_hbm(resid)), us=2.0,
         )
     with jax.named_scope("correct"):
         gated = call(
             correct_kernel, shape(tokens, channels, bf16), [VM] * 6, [pltpu.VMEM((tokens * g, 128), f32)],
             (*entered, base, spread, rate),
         )
-    gated, route_ids = lax.optimization_barrier((gated, route_ids))
     with jax.named_scope("gather_gated"):
         peer_gated = swap_tp(gated)
     gain = norm_gain[None, :]
-    with jax.named_scope("route"):
-        slot_lanes, slot_cols = call(
-            route_kernel, (shape(8, tokens, f32), shape(tokens, 128, bf16)), [VM], (), (in_hbm(route_ids.T),)
-        )
     with jax.named_scope("gather_gated"):
-        message = shape(tokens, 2 * channels + block_cols // 2 + 128, bf16)
+        message = shape(tokens, 2 * channels + block_cols // 2, bf16)
         messages = call(
-            pack_kernel, (message,) * 4, [VM] * 4, (), (gated, peer_gated, in_hbm(resid), slot_cols)
+            pack_kernel, (message,) * 4, [VM] * 3, (), (gated, peer_gated, in_vmem(resid))
         )
         blocks = [messages[0]] + [to_owner(messages[p], p) for p in away]
 
     token_kind = shape(8, 128, f32)
-    with jax.named_scope("hold_out_weight"):
-        held_out = call(
-            hold_out_kernel, pltpu.VMEM((2 * out_weight.shape[0], block_cols), bf16), [HB, AN, AN],
-            [pltpu.SemaphoreType.DMA((2,))], (in_hbm(out_weight), peer_weight, messages[0]),
-        )
     slots_total = EXPERTS * CAP
     part_width = w_gate.shape[1] // 2
     wg, wu, wd = (in_hbm(v) for v in (w_gate, w_up, w_down))
     dma = pltpu.SemaphoreType.DMA
     held_kind = pltpu.VMEM((2 * half_width, part_width), bf16)
+    with jax.named_scope("hold_out_weight"):
+        held_out, held = call(
+            hold_out_kernel, (pltpu.VMEM((2 * out_weight.shape[0], block_cols), bf16), held_kind), [HB, AN, HB, AN],
+            [dma((3,))], (in_hbm(out_weight), peer_weight, wg, messages[0]),
+        )
 
     def project(first, second, token, keep):
         with jax.named_scope("project"):
             return call(
-                project_kernel, (shape(2 * tokens, block_cols, bf16), shape(2 * tokens, 128, bf16)), [VM] * 3 + [AN],
-                [pltpu.VMEM((2 * tokens, message.shape[1]), bf16)], (first, second, in_vmem(held_out), token), keep=keep,
+                project_kernel, (shape(2 * tokens, block_cols, bf16),), [VM] * 2 + [AN],
+                [pltpu.VMEM((2 * tokens, message.shape[1]), bf16)], (first, second, token), keep=keep, show=True,
             )
 
     def sum_exp(own):
         with jax.named_scope("sum_exp"):
             return permute(own, [(number(c, x, owner(c)), number(c, 1 - x, owner(c))) for c, x in chips])
 
-    def select(own, peer, slots, token, keep):
+    def select(own, peer, first, second, token, keep):
         with jax.named_scope("select"):
             block = shape(tokens, block_cols, bf16)
             routed = shape(2 * CAP, block_cols, bf16)
             return call(
-                select_kernel, (block, block) + (routed,) * 4, [VM] * 3 + [AN], [pltpu.VMEM((2 * tokens, block_cols), bf16)],
-                (own, peer, slots, token), keep=keep,
+                select_kernel, (block, block) + (routed,) * 4, [VM] * 4 + [AN], [pltpu.VMEM((2 * tokens, block_cols), bf16)],
+                (own, peer, first, second, token), keep=keep,
             )
 
     def dispatch(out):
         with jax.named_scope("dispatch"):
             return [out[0]] + [from_owner(out[p], p) for p in away]
 
-    own, slots, held_out = project(blocks[0], blocks[1], slot_lanes, (held_out,))
+    own, held_out, held = project(blocks[0], blocks[1], pack, (held_out, held))
     peer = sum_exp(own)
     with jax.named_scope("hold_weights"):
         token, held = call(
-            hold_early_kernel, (token_kind, held_kind), [HB, HB, AN], [dma((2,))], (wg, wu, own), us=HOLD
-        )
-    first, second, *out, held_out, held = select(own, peer, slots, token, (held_out, held))
+            hold_early_kernel, (token_kind,), [HB, HB, AN], [dma((2,))], (wg, wu, own), us=HOLD, keep=(held,), show=True
+        )
+    first, second, *out, held_out, held = select(own, peer, pack, entered[0], token, (held_out, held))
     streams = [first, second]
     sent = [dispatch(out)]
     token = call(after_kernel, token_kind, [AN], (), (out[0],), us=ORDER)
-    own, slots, held = project(blocks[2], blocks[3], token, (held,))
+    own, _, held = project(blocks[2], blocks[3], token, (held_out, held))
     peer = sum_exp(own)
     token = call(after_kernel, token_kind, [AN], (), (own,), us=ORDER)
-    first, second, *out, held = select(own, peer, slots, token, (held,))
+    first, second, *out, held = select(own, peer, entered[1], entered[2], token, (held,))
     streams += [first, second]
     sent.append(dispatch(out))
     with jax.named_scope("hold_weights"):
         held_second, held = call(
-            hold_late_kernel, (held_kind,), [HB, HB, AN], [dma((2,))], (wg, wu, out[0]), us=HOLD, keep=(held,), show=True
+            hold_late_kernel, (held_kind,), [HB, AN], [dma], (wg, out[0]), us=HOLD, keep=(held,)
         )
     with jax.named_scope("gate_up"):
         first, feats, held, held_second = call(
@@ -682,24 +681,25 @@
         )
         peer_second = swap_tp(second)
     with jax.named_scope("down"):
-        held = in_vmem(held)
-        acc, scale = call(
+        acc, scale, held = call(
             functools.partial(down_first_kernel, model_width),
-            (shape(slots_total, half_width, f32), shape(slots_total, 128, f32)), [VM] * 3, (),
-            (first, peer_first, held),
+            (shape(slots_total, half_width, f32), shape(slots_total, 128, f32)), [VM] * 2 + [HB], [dma],
+            (first, peer_first, wd), keep=(held,), show=True,
         )
         piece = shape(slots_total // 2, piece_width, bf16)
         total = pltpu.VMEM((slots_total, piece_width), f32)
-        theirs_near, theirs_far, hidden = call(
+        theirs_near, theirs_far, hidden, held = call(
             down_theirs_kernel, (piece, piece, shape(slots_total, part_width, bf16)),
-            [VM] * 5, [total], (second, peer_second, scale, held, acc),
+            [VM] * 4, [total], (second, peer_second, scale, acc), keep=(held,), show=True,
         )
     with jax.named_scope("sum_experts"):
         swap = [(0, 1), (1, 0)]
         peer_far = lax.ppermute(theirs_far, "exp", swap)
         theirs_near, _ = lax.optimization_barrier((theirs_near, theirs_far))
         peer_near = lax.ppermute(theirs_near, "exp", swap)
-        mine_near, mine_far = call(down_mine_kernel, (piece, piece), [VM] * 3, [total], (hidden, held, acc))
+        mine_near, mine_far, _ = call(
+            down_mine_kernel, (piece, piece), [VM] * 2, [total], (hidden, acc), keep=(held,), show=True
+        )
     def reply(own, peer):
         small = shape(CAP, piece_width, bf16)
         return call(
@@ -728,7 +728,7 @@
     with jax.named_scope("finish"):
         return call(
             finish_kernel, shape(tokens, piece_width, bf16), [VM] * 10, (),
-            (streams[0], *home, slot_lanes, route_weight.T, *replies),
+            (streams[0], *home, pack, route_weight.T, *replies),
         )
 
 

time: 101 us -> 96.8 us (0.958)
  Pallas kernels: 36.5 us -> 33.7 us
  waiting for transfers between devices: 16 us -> 14 us
  starting transfers between devices: 46.6 us -> 48 us
    pallas_call x22 -> x21, Pallas kernels: 36.5 us -> 33.7 us  [call(): pl.pallas_call(body_kernel, out_shape=outs + tuple((pltpu.VMEM(x.shape, x...]
    ppermute x20, waiting for transfers between devices: 15.1 us -> 12.7 us  [permute(): return lax.ppermute(x, AXES, pairs)]
    ppermute x20, starting transfers between devices: 43.3 us -> 44.8 us  [permute(): return lax.ppermute(x, AXES, pairs)]
  transfers between devices with their start and end apart: 26 -> 26, of which waited for: 9 -> 9; matrix products, arithmetic and copies ran while one was open for 0% -> 0% of each run, Pallas kernels for 30% -> 25%
where the time goes in v4:
time: 96.8 us; the launch traced here: 96.1 us
  starting transfers between devices  48 us (50%)
  Pallas kernels  33.7 us (35%)
  waiting for transfers between devices  14 us (14%)
    ppermute x20, starting transfers between devices, permute(): return lax.ppermute(x, AXES, pairs)  44.8 us
    pallas_call x21, Pallas kernels, call(): pl.pallas_call(body_kernel, out_shape=outs + tuple((pltpu.VMEM(x.shape, x...  33.7 us
    ppermute x20, waiting for transfers between devices, permute(): return lax.ppermute(x, AXES, pairs)  12.7 us
  transfers between devices with their start and end apart: 26, of which 9 were waited for; matrix products, arithmetic and copies ran while one was open for 0% of the time, Pallas kernels for 25%

profile of v4, /device:TPU:0, one launch (start us, length us, event | category | flops | bytes accessed | tf_op | source)
XLA Modules:
  0.0 96.1 jit_solution(14057650197192796321)
XLA Ops:
  0.0 3.3 %scan.1 = (f32[512,128]{1,0:T(8,128)S(1)}, f32[512,128]{1,0:T(8,128)S(1)}, f32[512,128]{1,0:T(8,128)S(1)}, f32[128,128]{1,0:T(8,128)S(1)}, bf16[144,128]{1,0:T(8,128)(2,1)S(1)}) custom-call(f32[16,64]{1,0:T(8,128)} %bitcast.8, f32[16,64]{1,0:T(8,128)} %bitcast.9, f32[64,1024]{1,0:T(8,128)} %refs_2_.3, bf16[64,1024]{1,0:T(8,128)(2,1)} %refs_3_.1, ...), custom_call_target="tpu_custom_call" | custom-call | tf_op jit(solution)/shard_map/scan/pallas_call | solution.py:517
  3.3 0.5 collective-permute-start.5
  3.7 4.6 %collective-permute-start.2 = (bf16[144,128]{1,0:T(8,128)(2,1)S(1)}, bf16[144,128]{1,0:T(8,128)(2,1)S(1)}, u32[]{:S(2)}, u32[]{:S(2)}) collective-permute-start(bf16[144,128]{1,0:T(8,128)(2,1)S(1)} %get-tuple-element.69.refs_2_.refs_4_), channel_id=1, source_target_pairs={{0,12},{1,13},{2,14},{3,15},{4,8},{5,9},{6,10},{7,11},{8,4},{9,5},... | collective-permute-start | bytes 110600 | tf_op jit(solution)/shard_map/relay/ppermute | solution.py:566
  8.4 0.7 collective-permute-start
  9.1 1.9 %spread.1 = (f32[512,128]{1,0:T(8,128)S(1)}, f32[8192,128]{1,0:T(8,128)S(1)}, bf16[64,4096]{1,0:T(8,128)(2,1)S(1)}) custom-call(f32[16,64]{1,0:T(8,128)} %bitcast.10, f32[512,128]{1,0:T(8,128)S(1)} %get-tuple-element.70.refs_1_, f32[512,128]{1,0:T(8,128)S(1)} %get-tuple-element.71.refs_2_, f32[512,128]{1,0:T(8,128)S(1)} %get-tuple-element.72.refs_3_, ...), custom_call_target="tpu_custom_call" | custom-call | flops 2000000000 | tf_op jit(solution)/shard_map/spread/pallas_call | solution.py:517
  11.0 2.2 %collective-permute-done.1.refs_1_.refs_2_ = bf16[144,128]{1,0:T(8,128)(2,1)S(1)} collective-permute-done((bf16[144,128]{1,0:T(8,128)(2,1)S(1)}, bf16[144,128]{1,0:T(8,128)(2,1)S(1)}, u32[]{:S(2)}, u32[]{:S(2)}) %collective-permute-start.1) | collective-permute-done | bytes 36896 | tf_op jit(solution)/shard_map/relay/ppermute | solution.py:566
  13.2 0.5 correct.1.refs_0_
  13.8 1.3 %collective-permute-done.3.refs_1_ = bf16[64,1024]{1,0:T(8,128)(2,1)S(1)} collective-permute-done((bf16[64,1024]{1,0:T(8,128)(2,1)S(1)}, bf16[64,1024]{1,0:T(8,128)(2,1)S(1)}, u32[]{:S(2)}, u32[]{:S(2)}) %collective-permute-start.3) | collective-permute-done | bytes 131104 | tf_op jit(solution)/shard_map/gather_gated/ppermute | solution.py:575
  15.2 0.1 gather_gated.1
  15.2 2.5 %collective-permute-start.4 = (bf16[64,2560]{1,0:T(8,128)(2,1)S(1)}, bf16[64,2560]{1,0:T(8,128)(2,1)S(1)}, u32[]{:S(2)}, u32[]{:S(2)}) collective-permute-start(bf16[64,2560]{1,0:T(8,128)(2,1)S(1)} %get-tuple-element.78), channel_id=1, source_target_pairs={{4,0},{6,2},{0,4},{2,6},{13,9},{15,11},{9,13},{11,15},{20,16},{22,... | collective-permute-start | bytes 983048 | tf_op jit(solution)/shard_map/gather_gated/ppermute | solution.py:566
  17.8 1.3 %collective-permute-start.10 = (bf16[64,2560]{1,0:T(8,128)(2,1)S(1)}, bf16[64,2560]{1,0:T(8,128)(2,1)S(1)}, u32[]{:S(2)}, u32[]{:S(2)}) collective-permute-start(bf16[64,2560]{1,0:T(8,128)(2,1)S(1)} %get-tuple-element.93), channel_id=1, source_target_pairs={{8,0},{10,2},{12,4},{14,6},{1,9},{3,11},{5,13},{7,15},{24,16},{26,... | collective-permute-start | bytes 983048 | tf_op jit(solution)/shard_map/gather_gated/ppermute | solution.py:566
  19.1 1.3 %collective-permute-start.11 = (bf16[64,2560]{1,0:T(8,128)(2,1)S(1)}, bf16[64,2560]{1,0:T(8,128)(2,1)S(1)}, u32[]{:S(2)}, u32[]{:S(2)}) collective-permute-start(bf16[64,2560]{1,0:T(8,128)(2,1)S(1)} %get-tuple-element.94), channel_id=1, source_target_pairs={{12,0},{14,2},{8,4},{10,6},{5,9},{7,11},{1,13},{3,15},{28,16},{30,... | collective-permute-start | bytes 983048 | tf_op jit(solution)/shard_map/gather_gated/ppermute | solution.py:566
  20.4 2.9 %hold_out_weight.1 = (bf16[2048,1024]{1,0:T(8,128)(2,1)S(1)}, bf16[4096,2048]{1,0:T(8,128)(2,1)S(1)}) custom-call(bf16[1024,1024]{1,0:T(8,128)(2,1)} %refs_0_.3, bf16[1024,1024]{1,0:T(8,128)(2,1)S(1)} %collective-permute-done.5.refs_1_, bf16[2048,4096]{1,0:T(8,128)(2,1)} %refs_0_.5, bf16[64,2560]{1,0:T(8,128)(2,1)S(1)} %get-tuple-element.77.refs_3_.refs_0_), custom_call_target="tpu_custom_call" | custom-call | tf_op jit(solution)/shard_map/hold_out_weight/pallas_call | solution.py:517
  23.3 0.9 collective-permute-done.4.refs_1_
  24.2 0.8 project.2
  25.0 3.4 %collective-permute-start.6 = (bf16[128,1024]{1,0:T(8,128)(2,1)S(1)}, bf16[128,1024]{1,0:T(8,128)(2,1)S(1)}, u32[]{:S(2)}, u32[]{:S(2)}) collective-permute-start(bf16[128,1024]{1,0:T(8,128)(2,1)S(1)} %get-tuple-element.82.refs_2_.refs_0_), channel_id=1, source_target_pairs={{0,2},{2,0},{4,6},{6,4},{9,11},{11,9},{13,15},{15,13},{16,18},{18,... | collective-permute-start | bytes 786440 | tf_op jit(solution)/shard_map/sum_exp/ppermute | solution.py:566
  28.4 4.7 %hold_weights.2 = (f32[8,128]{1,0:T(8,128)S(1)}, bf16[4096,2048]{1,0:T(8,128)(2,1)S(1)}) custom-call(bf16[2048,4096]{1,0:T(8,128)(2,1)} %refs_0_.5, bf16[2048,4096]{1,0:T(8,128)(2,1)} %refs_9_.1, bf16[128,1024]{1,0:T(8,128)(2,1)S(1)} %get-tuple-element.82.refs_2_.refs_0_, ...), custom_call_target="tpu_custom_call", output_to_operand_aliasing={{1}: (3, {})} | custom-call | flops 3000000000 | tf_op jit(solution)/shard_map/hold_weights/pallas_call | solution.py:517
  33.1 0.2 collective-permute-done.6.refs_1_
  33.3 0.4 select.2
  33.7 3.4 %collective-permute-start.7 = (bf16[80,1024]{1,0:T(8,128)(2,1)S(1)}, bf16[80,1024]{1,0:T(8,128)(2,1)S(1)}, u32[]{:S(2)}, u32[]{:S(2)}) collective-permute-start(bf16[80,1024]{1,0:T(8,128)(2,1)S(1)} %get-tuple-element.90), channel_id=1, source_target_pairs={{0,4},{2,6},{4,0},{6,2},{9,13},{11,15},{13,9},{15,11},{16,20},{18,... | collective-permute-start | bytes 491528 | tf_op jit(solution)/shard_map/dispatch/ppermute | solution.py:566
  37.2 0.8 project.3
  38.0 3.3 %collective-permute-start.12 = (bf16[128,1024]{1,0:T(8,128)(2,1)S(1)}, bf16[128,1024]{1,0:T(8,128)(2,1)S(1)}, u32[]{:S(2)}, u32[]{:S(2)}) collective-permute-start(bf16[128,1024]{1,0:T(8,128)(2,1)S(1)} %get-tuple-element.97.refs_0_), channel_id=1, source_target_pairs={{0,2},{2,0},{4,6},{6,4},{9,11},{11,9},{13,15},{15,13},{16,18},{18,... | collective-permute-start | bytes 786440 | tf_op jit(solution)/shard_map/sum_exp/ppermute | solution.py:566
  41.4 1.3 %collective-permute-start.8 = (bf16[80,1024]{1,0:T(8,128)(2,1)S(1)}, bf16[80,1024]{1,0:T(8,128)(2,1)S(1)}, u32[]{:S(2)}, u32[]{:S(2)}) collective-permute-start(bf16[80,1024]{1,0:T(8,128)(2,1)S(1)} %get-tuple-element.91), channel_id=1, source_target_pairs={{0,8},{2,10},{4,12},{6,14},{9,1},{11,3},{13,5},{15,7},{16,24},{18,... | collective-permute-start | bytes 491528 | tf_op jit(solution)/shard_map/dispatch/ppermute | solution.py:566
  42.7 1.3 %collective-permute-start.9 = (bf16[80,1024]{1,0:T(8,128)(2,1)S(1)}, bf16[80,1024]{1,0:T(8,128)(2,1)S(1)}, u32[]{:S(2)}, u32[]{:S(2)}) collective-permute-start(bf16[80,1024]{1,0:T(8,128)(2,1)S(1)} %get-tuple-element.92), channel_id=1, source_target_pairs={{0,12},{2,14},{4,8},{6,10},{9,5},{11,7},{13,1},{15,3},{16,28},{18,... | collective-permute-start | bytes 491528 | tf_op jit(solution)/shard_map/dispatch/ppermute | solution.py:566
  44.0 2.3 %collective-permute-done.12.refs_1_ = bf16[128,1024]{1,0:T(8,128)(2,1)S(1)} collective-permute-done((bf16[128,1024]{1,0:T(8,128)(2,1)S(1)}, bf16[128,1024]{1,0:T(8,128)(2,1)S(1)}, u32[]{:S(2)}, u32[]{:S(2)}) %collective-permute-start.12) | collective-permute-done | bytes 262176 | tf_op jit(solution)/shard_map/sum_exp/ppermute | solution.py:566
  46.3 0.4 select.3
  46.7 3.4 %collective-permute-start.13 = (bf16[80,1024]{1,0:T(8,128)(2,1)S(1)}, bf16[80,1024]{1,0:T(8,128)(2,1)S(1)}, u32[]{:S(2)}, u32[]{:S(2)}) collective-permute-start(bf16[80,1024]{1,0:T(8,128)(2,1)S(1)} %get-tuple-element.100), channel_id=1, source_target_pairs={{0,4},{2,6},{4,0},{6,2},{9,13},{11,15},{13,9},{15,11},{16,20},{18,... | collective-permute-start | bytes 491528 | tf_op jit(solution)/shard_map/dispatch/ppermute | solution.py:566
  50.1 1.3 %collective-permute-start.14 = (bf16[80,1024]{1,0:T(8,128)(2,1)S(1)}, bf16[80,1024]{1,0:T(8,128)(2,1)S(1)}, u32[]{:S(2)}, u32[]{:S(2)}) collective-permute-start(bf16[80,1024]{1,0:T(8,128)(2,1)S(1)} %get-tuple-element.101), channel_id=1, source_target_pairs={{0,8},{2,10},{4,12},{6,14},{9,1},{11,3},{13,5},{15,7},{16,24},{18,... | collective-permute-start | bytes 491528 | tf_op jit(solution)/shard_map/dispatch/ppermute | solution.py:566
  51.5 1.3 %collective-permute-start.15 = (bf16[80,1024]{1,0:T(8,128)(2,1)S(1)}, bf16[80,1024]{1,0:T(8,128)(2,1)S(1)}, u32[]{:S(2)}, u32[]{:S(2)}) collective-permute-start(bf16[80,1024]{1,0:T(8,128)(2,1)S(1)} %get-tuple-element.102), channel_id=1, source_target_pairs={{0,12},{2,14},{4,8},{6,10},{9,5},{11,7},{13,1},{15,3},{16,28},{18,... | collective-permute-start | bytes 491528 | tf_op jit(solution)/shard_map/dispatch/ppermute | solution.py:566
  52.8 3.4 %hold_weights.3 = (bf16[4096,2048]{1,0:T(8,128)(2,1)S(1)}, bf16[4096,2048]{1,0:T(8,128)(2,1)S(1)}) custom-call(bf16[2048,4096]{1,0:T(8,128)(2,1)} %refs_0_.5, bf16[80,1024]{1,0:T(8,128)(2,1)S(1)} %get-tuple-element.99.refs_1_.refs_4_, bf16[4096,2048]{1,0:T(8,128)(2,1)S(1)} %get-tuple-element.103.refs_2_), custom_call_target="tpu_custom_call", output_to_operand_aliasing={{1}: (2, {})} | custom-call | flops 3000000000 | tf_op jit(solution)/shard_map/hold_weights/pallas_call | solution.py:517
  56.2 0.3 collective-permute-done.15.refs_7_
  56.5 4.1 %gate_up.2 = (bf16[160,4224]{1,0:T(8,128)(2,1)S(1)}, bf16[160,2048]{1,0:T(8,128)(2,1)S(1)}, bf16[4096,2048]{1,0:T(8,128)(2,1)S(1)}, bf16[4096,2048]{1,0:T(8,128)(2,1)S(1)}) custom-call(bf16[80,1024]{1,0:T(8,128)(2,1)S(1)} %get-tuple-element.89.refs_0_, ...), custom_call_target="tpu_custom_call", output_to_operand_aliasing={{2}: (10, {}), {3}: (11, {})} | custom-call | tf_op jit(solution)/shard_map/gate_up/pallas_call | solution.py:517
  60.7 3.4 %gate_up.3 = (bf16[160,4096]{1,0:T(8,128)(2,1)S(1)}, bf16[4096,2048]{1,0:T(8,128)(2,1)S(1)}, bf16[4096,2048]{1,0:T(8,128)(2,1)S(1)}) custom-call(bf16[160,2048]{1,0:T(8,128)(2,1)S(1)} %get-tuple-element.106.refs_0_, bf16[4096,2048]{1,0:T(8,128)(2,1)} %refs_2_.5, ...), custom_call_target="tpu_custom_call", output_to_operand_aliasing={{1}: (2, {}), {2}: (3, {})} | custom-call | tf_op jit(solution)/shard_map/gate_up/pallas_call | solution.py:517
  64.1 0.6 collective-permute-start.16
  64.7 3.4 %down.2 = (f32[160,2048]{1,0:T(8,128)S(1)}, f32[160,128]{1,0:T(8,128)S(1)}, bf16[4096,2048]{1,0:T(8,128)(2,1)S(1)}) custom-call(bf16[160,4224]{1,0:T(8,128)(2,1)S(1)} %get-tuple-element.110.refs_0_, bf16[160,4224]{1,0:T(8,128)(2,1)S(1)} %collective-permute-done.17.refs_1_, bf16[4096,2048]{1,0:T(8,128)(2,1)} %refs_2_.5, ...), custom_call_target="tpu_custom_call", output_to_operand_aliasing={{2}: (3, {})} | custom-call | tf_op jit(solution)/shard_map/down/pallas_call | solution.py:517
  68.1 1.4 %down.3 = (bf16[80,1024]{1,0:T(8,128)(2,1)S(1)}, bf16[80,1024]{1,0:T(8,128)(2,1)S(1)}, bf16[160,2048]{1,0:T(8,128)(2,1)S(1)}, bf16[4096,2048]{1,0:T(8,128)(2,1)S(1)}) custom-call(bf16[160,4096]{1,0:T(8,128)(2,1)S(1)} %get-tuple-element.109.refs_0_, bf16[160,4096]{1,0:T(8,128)(2,1)S(1)} %collective-permute-done.16.refs_1_, ...), custom_call_target="tpu_custom_call", output_to_operand_aliasing={{3}: (4, {})} | custom-call | tf_op jit(solution)/shard_map/down/pallas_call | solution.py:517
  69.5 1.6 %collective-permute-start.19 = (bf16[80,1024]{1,0:T(8,128)(2,1)S(1)}, bf16[80,1024]{1,0:T(8,128)(2,1)S(1)}, u32[]{:S(2)}, u32[]{:S(2)}) collective-permute-start(bf16[80,1024]{1,0:T(8,128)(2,1)S(1)} %get-tuple-element.119), channel_id=1, source_target_pairs={{0,2},{2,0},{1,3},{3,1},{4,6},{6,4},{5,7},{7,5},{8,10},{10,8},{9,1... | collective-permute-start | bytes 491528 | tf_op jit(solution)/shard_map/sum_experts/ppermute | solution.py:697
  71.1 0.5 collective-permute-start.18
  71.6 0.9 sum_experts.1
  72.5 7.3 %collective-permute-start.21 = (bf16[64,1024]{1,0:T(8,128)(2,1)S(1)}, bf16[64,1024]{1,0:T(8,128)(2,1)S(1)}, u32[]{:S(2)}, u32[]{:S(2)}) collective-permute-start(bf16[64,1024]{1,0:T(8,128)(2,1)S(1)} %get-tuple-element.128), channel_id=1, source_target_pairs={{0,8},{6,14},{9,1},{15,7},{16,24},{22,30},{25,17},{31,23}} | collective-permute-start | bytes 393224 | tf_op jit(solution)/shard_map/reply/stream_home/ppermute | solution.py:566
  79.8 1.3 %collective-permute-start.22 = (bf16[64,1024]{1,0:T(8,128)(2,1)S(1)}, bf16[64,1024]{1,0:T(8,128)(2,1)S(1)}, u32[]{:S(2)}, u32[]{:S(2)}) collective-permute-start(bf16[64,1024]{1,0:T(8,128)(2,1)S(1)} %get-tuple-element.130), channel_id=1, source_target_pairs={{0,12},{6,10},{9,5},{15,3},{16,28},{22,26},{25,21},{31,19}} | collective-permute-start | bytes 393224 | tf_op jit(solution)/shard_map/reply/stream_home/ppermute | solution.py:566
  81.3 3.4 %collective-permute-start.20 = (bf16[64,1024]{1,0:T(8,128)(2,1)S(1)}, bf16[64,1024]{1,0:T(8,128)(2,1)S(1)}, u32[]{:S(2)}, u32[]{:S(2)}) collective-permute-start(bf16[64,1024]{1,0:T(8,128)(2,1)S(1)} %get-tuple-element.126), channel_id=1, source_target_pairs={{0,4},{6,2},{9,13},{15,11},{16,20},{22,18},{25,29},{31,27}} | collective-permute-start | bytes 393224 | tf_op jit(solution)/shard_map/reply/stream_home/ppermute | solution.py:566
  84.8 2.1 %collective-permute-start.25 = (bf16[40,1024]{1,0:T(8,128)(2,1)S(1)}, bf16[40,1024]{1,0:T(8,128)(2,1)S(1)}, u32[]{:S(2)}, u32[]{:S(2)}) collective-permute-start(bf16[40,1024]{1,0:T(8,128)(2,1)S(1)} %get-tuple-element.132), channel_id=1, source_target_pairs={{0,12},{1,13},{2,14},{3,15},{4,8},{5,9},{6,10},{7,11},{8,4},{9,5},... | collective-permute-start | bytes 245768 | tf_op jit(solution)/shard_map/reply/ppermute | solution.py:566
  86.9 1.4 %collective-permute-start.24 = (bf16[40,1024]{1,0:T(8,128)(2,1)S(1)}, bf16[40,1024]{1,0:T(8,128)(2,1)S(1)}, u32[]{:S(2)}, u32[]{:S(2)}) collective-permute-start(bf16[40,1024]{1,0:T(8,128)(2,1)S(1)} %get-tuple-element.122), channel_id=1, source_target_pairs={{0,8},{1,9},{2,10},{3,11},{4,12},{5,13},{6,14},{7,15},{8,0},{9,1},... | collective-permute-start | bytes 245768 | tf_op jit(solution)/shard_map/reply/ppermute | solution.py:566
  88.3 1.8 %collective-permute-done.23.refs_7_ = bf16[40,1024]{1,0:T(8,128)(2,1)S(1)} collective-permute-done((bf16[40,1024]{1,0:T(8,128)(2,1)S(1)}, bf16[40,1024]{1,0:T(8,128)(2,1)S(1)}, u32[]{:S(2)}, u32[]{:S(2)}) %collective-permute-start.23) | collective-permute-done | bytes 81952 | tf_op jit(solution)/shard_map/reply/ppermute | solution.py:566
  90.1 1.7 %collective-permute-done.25.refs_9_ = bf16[40,1024]{1,0:T(8,128)(2,1)S(1)} collective-permute-done((bf16[40,1024]{1,0:T(8,128)(2,1)S(1)}, bf16[40,1024]{1,0:T(8,128)(2,1)S(1)}, u32[]{:S(2)}, u32[]{:S(2)}) %collective-permute-start.25) | collective-permute-done | bytes 81952 | tf_op jit(solution)/shard_map/reply/ppermute | solution.py:566
  91.8 3.1 %collective-permute-done.24.refs_8_ = bf16[40,1024]{1,0:T(8,128)(2,1)S(1)} collective-permute-done((bf16[40,1024]{1,0:T(8,128)(2,1)S(1)}, bf16[40,1024]{1,0:T(8,128)(2,1)S(1)}, u32[]{:S(2)}, u32[]{:S(2)}) %collective-permute-start.24) | collective-permute-done | bytes 81952 | tf_op jit(solution)/shard_map/reply/ppermute | solution.py:566
  95.0 1.1 %finish.1 = bf16[64,1024]{1,0:T(8,128)(2,1)} custom-call(bf16[64,1024]{1,0:T(8,128)(2,1)S(1)} %get-tuple-element.87.refs_0_, bf16[64,1024]{1,0:T(8,128)(2,1)S(1)} %collective-permute-done.20.refs_1_, bf16[64,1024]{1,0:T(8,128)(2,1)S(1)} %collective-permute-done.21.refs_2_, bf16[64,1024]{1,0:T(8,128)(2,1)S(1)} %collective-permute-done.22.refs_3_, ...), custom_call_target="tpu_custom_call" | custom-call | tf_op jit(solution)/shard_map/finish/pallas_call | solution.py:517
  (27 shorter events, 0.4 us)
Async XLA Ops:
  3.3 17.1 %collective-permute-start.5 = (bf16[1024,1024]{1,0:T(8,128)(2,1)}, bf16[1024,1024]{1,0:T(8,128)(2,1)S(1)}, u32[]{:S(2)}, u32[]{:S(2)}) collective-permute-start(bf16[1024,1024]{1,0:T(8,128)(2,1)} %refs_0_.3), channel_id=1, source_target_pairs={{0,1},{1,0},{2,3},{3,2},{4,5},{5,4},{6,7},{7,6},{8,9},{9,8},{10,11... | collective-permute-start | bytes 6291464 | tf_op jit(solution)/shard_map/ppermute | solution.py:575
  3.7 7.3 %collective-permute-start.2 = (bf16[144,128]{1,0:T(8,128)(2,1)S(1)}, bf16[144,128]{1,0:T(8,128)(2,1)S(1)}, u32[]{:S(2)}, u32[]{:S(2)}) collective-permute-start(bf16[144,128]{1,0:T(8,128)(2,1)S(1)} %get-tuple-element.69.refs_2_.refs_4_), channel_id=1, source_target_pairs={{0,12},{1,13},{2,14},{3,15},{4,8},{5,9},{6,10},{7,11},{8,4},{9,5},... | collective-permute-start | bytes 110600 | tf_op jit(solution)/shard_map/relay/ppermute | solution.py:566
  8.4 4.9 %collective-permute-start.1 = (bf16[144,128]{1,0:T(8,128)(2,1)S(1)}, bf16[144,128]{1,0:T(8,128)(2,1)S(1)}, u32[]{:S(2)}, u32[]{:S(2)}) collective-permute-start(bf16[144,128]{1,0:T(8,128)(2,1)S(1)} %get-tuple-element.69.refs_2_.refs_4_), channel_id=1, source_target_pairs={{0,8},{1,9},{2,10},{3,11},{4,12},{5,13},{6,14},{7,15},{8,0},{9,1},... | collective-permute-start | bytes 110600 | tf_op jit(solution)/shard_map/relay/ppermute | solution.py:566
  8.4 4.9 %collective-permute-start = (bf16[144,128]{1,0:T(8,128)(2,1)S(1)}, bf16[144,128]{1,0:T(8,128)(2,1)S(1)}, u32[]{:S(2)}, u32[]{:S(2)}) collective-permute-start(bf16[144,128]{1,0:T(8,128)(2,1)S(1)} %get-tuple-element.69.refs_2_.refs_4_), channel_id=1, source_target_pairs={{0,4},{1,5},{2,6},{3,7},{4,0},{5,1},{6,2},{7,3},{8,12},{9,13},{10,... | collective-permute-start | bytes 110600 | tf_op jit(solution)/shard_map/relay/ppermute | solution.py:566
  13.7 1.4 %collective-permute-start.3 = (bf16[64,1024]{1,0:T(8,128)(2,1)S(1)}, bf16[64,1024]{1,0:T(8,128)(2,1)S(1)}, u32[]{:S(2)}, u32[]{:S(2)}) collective-permute-start(bf16[64,1024]{1,0:T(8,128)(2,1)S(1)} %correct.1.refs_0_), channel_id=1, source_target_pairs={{0,1},{1,0},{2,3},{3,2},{4,5},{5,4},{6,7},{7,6},{8,9},{9,8},{10,11... | collective-permute-start | bytes 393224 | tf_op jit(solution)/shard_map/gather_gated/ppermute | solution.py:575
  15.2 9.0 %collective-permute-start.4 = (bf16[64,2560]{1,0:T(8,128)(2,1)S(1)}, bf16[64,2560]{1,0:T(8,128)(2,1)S(1)}, u32[]{:S(2)}, u32[]{:S(2)}) collective-permute-start(bf16[64,2560]{1,0:T(8,128)(2,1)S(1)} %get-tuple-element.78), channel_id=1, source_target_pairs={{4,0},{6,2},{0,4},{2,6},{13,9},{15,11},{9,13},{11,15},{20,16},{22,... | collective-permute-start | bytes 983048 | tf_op jit(solution)/shard_map/gather_gated/ppermute | solution.py:566
  17.8 19.4 %collective-permute-start.10 = (bf16[64,2560]{1,0:T(8,128)(2,1)S(1)}, bf16[64,2560]{1,0:T(8,128)(2,1)S(1)}, u32[]{:S(2)}, u32[]{:S(2)}) collective-permute-start(bf16[64,2560]{1,0:T(8,128)(2,1)S(1)} %get-tuple-element.93), channel_id=1, source_target_pairs={{8,0},{10,2},{12,4},{14,6},{1,9},{3,11},{5,13},{7,15},{24,16},{26,... | collective-permute-start | bytes 983048 | tf_op jit(solution)/shard_map/gather_gated/ppermute | solution.py:566
  19.1 18.1 %collective-permute-start.11 = (bf16[64,2560]{1,0:T(8,128)(2,1)S(1)}, bf16[64,2560]{1,0:T(8,128)(2,1)S(1)}, u32[]{:S(2)}, u32[]{:S(2)}) collective-permute-start(bf16[64,2560]{1,0:T(8,128)(2,1)S(1)} %get-tuple-element.94), channel_id=1, source_target_pairs={{12,0},{14,2},{8,4},{10,6},{5,9},{7,11},{1,13},{3,15},{28,16},{30,... | collective-permute-start | bytes 983048 | tf_op jit(solution)/shard_map/gather_gated/ppermute | solution.py:566
  25.0 8.3 %collective-permute-start.6 = (bf16[128,1024]{1,0:T(8,128)(2,1)S(1)}, bf16[128,1024]{1,0:T(8,128)(2,1)S(1)}, u32[]{:S(2)}, u32[]{:S(2)}) collective-permute-start(bf16[128,1024]{1,0:T(8,128)(2,1)S(1)} %get-tuple-element.82.refs_2_.refs_0_), channel_id=1, source_target_pairs={{0,2},{2,0},{4,6},{6,4},{9,11},{11,9},{13,15},{15,13},{16,18},{18,... | collective-permute-start | bytes 786440 | tf_op jit(solution)/shard_map/sum_exp/ppermute | solution.py:566
  33.7 17.7 %collective-permute-start.7 = (bf16[80,1024]{1,0:T(8,128)(2,1)S(1)}, bf16[80,1024]{1,0:T(8,128)(2,1)S(1)}, u32[]{:S(2)}, u32[]{:S(2)}) collective-permute-start(bf16[80,1024]{1,0:T(8,128)(2,1)S(1)} %get-tuple-element.90), channel_id=1, source_target_pairs={{0,4},{2,6},{4,0},{6,2},{9,13},{11,15},{13,9},{15,11},{16,20},{18,... | collective-permute-start | bytes 491528 | tf_op jit(solution)/shard_map/dispatch/ppermute | solution.py:566
  38.0 8.3 %collective-permute-start.12 = (bf16[128,1024]{1,0:T(8,128)(2,1)S(1)}, bf16[128,1024]{1,0:T(8,128)(2,1)S(1)}, u32[]{:S(2)}, u32[]{:S(2)}) collective-permute-start(bf16[128,1024]{1,0:T(8,128)(2,1)S(1)} %get-tuple-element.97.refs_0_), channel_id=1, source_target_pairs={{0,2},{2,0},{4,6},{6,4},{9,11},{11,9},{13,15},{15,13},{16,18},{18,... | collective-permute-start | bytes 786440 | tf_op jit(solution)/shard_map/sum_exp/ppermute | solution.py:566
  41.4 14.8 %collective-permute-start.8 = (bf16[80,1024]{1,0:T(8,128)(2,1)S(1)}, bf16[80,1024]{1,0:T(8,128)(2,1)S(1)}, u32[]{:S(2)}, u32[]{:S(2)}) collective-permute-start(bf16[80,1024]{1,0:T(8,128)(2,1)S(1)} %get-tuple-element.91), channel_id=1, source_target_pairs={{0,8},{2,10},{4,12},{6,14},{9,1},{11,3},{13,5},{15,7},{16,24},{18,... | collective-permute-start | bytes 491528 | tf_op jit(solution)/shard_map/dispatch/ppermute | solution.py:566
  42.7 13.5 %collective-permute-start.9 = (bf16[80,1024]{1,0:T(8,128)(2,1)S(1)}, bf16[80,1024]{1,0:T(8,128)(2,1)S(1)}, u32[]{:S(2)}, u32[]{:S(2)}) collective-permute-start(bf16[80,1024]{1,0:T(8,128)(2,1)S(1)} %get-tuple-element.92), channel_id=1, source_target_pairs={{0,12},{2,14},{4,8},{6,10},{9,5},{11,7},{13,1},{15,3},{16,28},{18,... | collective-permute-start | bytes 491528 | tf_op jit(solution)/shard_map/dispatch/ppermute | solution.py:566
  46.7 9.5 %collective-permute-start.13 = (bf16[80,1024]{1,0:T(8,128)(2,1)S(1)}, bf16[80,1024]{1,0:T(8,128)(2,1)S(1)}, u32[]{:S(2)}, u32[]{:S(2)}) collective-permute-start(bf16[80,1024]{1,0:T(8,128)(2,1)S(1)} %get-tuple-element.100), channel_id=1, source_target_pairs={{0,4},{2,6},{4,0},{6,2},{9,13},{11,15},{13,9},{15,11},{16,20},{18,... | collective-permute-start | bytes 491528 | tf_op jit(solution)/shard_map/dispatch/ppermute | solution.py:566
  50.1 6.1 %collective-permute-start.14 = (bf16[80,1024]{1,0:T(8,128)(2,1)S(1)}, bf16[80,1024]{1,0:T(8,128)(2,1)S(1)}, u32[]{:S(2)}, u32[]{:S(2)}) collective-permute-start(bf16[80,1024]{1,0:T(8,128)(2,1)S(1)} %get-tuple-element.101), channel_id=1, source_target_pairs={{0,8},{2,10},{4,12},{6,14},{9,1},{11,3},{13,5},{15,7},{16,24},{18,... | collective-permute-start | bytes 491528 | tf_op jit(solution)/shard_map/dispatch/ppermute | solution.py:566
  51.5 5.1 %collective-permute-start.15 = (bf16[80,1024]{1,0:T(8,128)(2,1)S(1)}, bf16[80,1024]{1,0:T(8,128)(2,1)S(1)}, u32[]{:S(2)}, u32[]{:S(2)}) collective-permute-start(bf16[80,1024]{1,0:T(8,128)(2,1)S(1)} %get-tuple-element.102), channel_id=1, source_target_pairs={{0,12},{2,14},{4,8},{6,10},{9,5},{11,7},{13,1},{15,3},{16,28},{18,... | collective-permute-start | bytes 491528 | tf_op jit(solution)/shard_map/dispatch/ppermute | solution.py:566
  60.7 4.0 %collective-permute-start.17 = (bf16[160,4224]{1,0:T(8,128)(2,1)S(1)}, bf16[160,4224]{1,0:T(8,128)(2,1)S(1)}, u32[]{:S(2)}, u32[]{:S(2)}) collective-permute-start(bf16[160,4224]{1,0:T(8,128)(2,1)S(1)} %get-tuple-element.110.refs_0_), channel_id=1, source_target_pairs={{0,1},{1,0},{2,3},{3,2},{4,5},{5,4},{6,7},{7,6},{8,9},{9,8},{10,11... | collective-permute-start | bytes 4055048 | tf_op jit(solution)/shard_map/gate_up/ppermute | solution.py:575
  64.1 4.0 %collective-permute-start.16 = (bf16[160,4096]{1,0:T(8,128)(2,1)S(1)}, bf16[160,4096]{1,0:T(8,128)(2,1)S(1)}, u32[]{:S(2)}, u32[]{:S(2)}) collective-permute-start(bf16[160,4096]{1,0:T(8,128)(2,1)S(1)} %get-tuple-element.109.refs_0_), channel_id=1, source_target_pairs={{0,1},{1,0},{2,3},{3,2},{4,5},{5,4},{6,7},{7,6},{8,9},{9,8},{10,11... | collective-permute-start | bytes 3932168 | tf_op jit(solution)/shard_map/gate_up/ppermute | solution.py:575
  68.1 26.8 %copy-start = (f32[64,2]{0,1:T(2,128)S(1)}, f32[64,2]{0,1:T(2,128)}, u32[]{:S(2)}) copy-start(f32[64,2]{0,1:T(2,128)} %param.26) | copy-start | bytes 1540
  69.5 11.6 %collective-permute-start.19 = (bf16[80,1024]{1,0:T(8,128)(2,1)S(1)}, bf16[80,1024]{1,0:T(8,128)(2,1)S(1)}, u32[]{:S(2)}, u32[]{:S(2)}) collective-permute-start(bf16[80,1024]{1,0:T(8,128)(2,1)S(1)} %get-tuple-element.119), channel_id=1, source_target_pairs={{0,2},{2,0},{1,3},{3,1},{4,6},{6,4},{5,7},{7,5},{8,10},{10,8},{9,1... | collective-permute-start | bytes 491528 | tf_op jit(solution)/shard_map/sum_experts/ppermute | solution.py:697
  71.1 10.2 %collective-permute-start.18 = (bf16[80,1024]{1,0:T(8,128)(2,1)S(1)}, bf16[80,1024]{1,0:T(8,128)(2,1)S(1)}, u32[]{:S(2)}, u32[]{:S(2)}) collective-permute-start(bf16[80,1024]{1,0:T(8,128)(2,1)S(1)} %get-tuple-element.120), channel_id=1, source_target_pairs={{0,2},{2,0},{1,3},{3,1},{4,6},{6,4},{5,7},{7,5},{8,10},{10,8},{9,1... | collective-permute-start | bytes 491528 | tf_op jit(solution)/shard_map/sum_experts/ppermute | solution.py:699
  72.5 14.4 %collective-permute-start.21 = (bf16[64,1024]{1,0:T(8,128)(2,1)S(1)}, bf16[64,1024]{1,0:T(8,128)(2,1)S(1)}, u32[]{:S(2)}, u32[]{:S(2)}) collective-permute-start(bf16[64,1024]{1,0:T(8,128)(2,1)S(1)} %get-tuple-element.128), channel_id=1, source_target_pairs={{0,8},{6,14},{9,1},{15,7},{16,24},{22,30},{25,17},{31,23}} | collective-permute-start | bytes 393224 | tf_op jit(solution)/shard_map/reply/stream_home/ppermute | solution.py:566
  79.8 8.4 %collective-permute-start.22 = (bf16[64,1024]{1,0:T(8,128)(2,1)S(1)}, bf16[64,1024]{1,0:T(8,128)(2,1)S(1)}, u32[]{:S(2)}, u32[]{:S(2)}) collective-permute-start(bf16[64,1024]{1,0:T(8,128)(2,1)S(1)} %get-tuple-element.130), channel_id=1, source_target_pairs={{0,12},{6,10},{9,5},{15,3},{16,28},{22,26},{25,21},{31,19}} | collective-permute-start | bytes 393224 | tf_op jit(solution)/shard_map/reply/stream_home/ppermute | solution.py:566
  81.3 13.6 %collective-permute-start.20 = (bf16[64,1024]{1,0:T(8,128)(2,1)S(1)}, bf16[64,1024]{1,0:T(8,128)(2,1)S(1)}, u32[]{:S(2)}, u32[]{:S(2)}) collective-permute-start(bf16[64,1024]{1,0:T(8,128)(2,1)S(1)} %get-tuple-element.126), channel_id=1, source_target_pairs={{0,4},{6,2},{9,13},{15,11},{16,20},{22,18},{25,29},{31,27}} | collective-permute-start | bytes 393224 | tf_op jit(solution)/shard_map/reply/stream_home/ppermute | solution.py:566
  84.7 5.4 %collective-permute-start.23 = (bf16[40,1024]{1,0:T(8,128)(2,1)S(1)}, bf16[40,1024]{1,0:T(8,128)(2,1)S(1)}, u32[]{:S(2)}, u32[]{:S(2)}) collective-permute-start(bf16[40,1024]{1,0:T(8,128)(2,1)S(1)} %get-tuple-element.125), channel_id=1, source_target_pairs={{0,4},{1,5},{2,6},{3,7},{4,0},{5,1},{6,2},{7,3},{8,12},{9,13},{10,... | collective-permute-start | bytes 245768 | tf_op jit(solution)/shard_map/reply/ppermute | solution.py:566
  84.8 7.0 %collective-permute-start.25 = (bf16[40,1024]{1,0:T(8,128)(2,1)S(1)}, bf16[40,1024]{1,0:T(8,128)(2,1)S(1)}, u32[]{:S(2)}, u32[]{:S(2)}) collective-permute-start(bf16[40,1024]{1,0:T(8,128)(2,1)S(1)} %get-tuple-element.132), channel_id=1, source_target_pairs={{0,12},{1,13},{2,14},{3,15},{4,8},{5,9},{6,10},{7,11},{8,4},{9,5},... | collective-permute-start | bytes 245768 | tf_op jit(solution)/shard_map/reply/ppermute | solution.py:566
  86.9 8.1 %collective-permute-start.24 = (bf16[40,1024]{1,0:T(8,128)(2,1)S(1)}, bf16[40,1024]{1,0:T(8,128)(2,1)S(1)}, u32[]{:S(2)}, u32[]{:S(2)}) collective-permute-start(bf16[40,1024]{1,0:T(8,128)(2,1)S(1)} %get-tuple-element.122), channel_id=1, source_target_pairs={{0,8},{1,9},{2,10},{3,11},{4,12},{5,13},{6,14},{7,15},{8,0},{9,1},... | collective-permute-start | bytes 245768 | tf_op jit(solution)/shard_map/reply/ppermute | solution.py:566

commit v5 on v4

--- a/solution.py
+++ b/solution.py
@@ -372,7 +372,7 @@
 
 
 def first_half_kernel(
-    a0_ref, a1_ref, a2_ref, a3_ref, b0_ref, b1_ref, b2_ref, b3_ref, gain_ref, wu_ref,
+    a0_ref, a2_ref, a3_ref, a1_ref, b0_ref, b2_ref, b3_ref, b1_ref, gain_ref, wu_ref,
     out_ref, feats_ref, held_ref, held_second_ref, squares_s, sem,
 ):
     begin = held_ref.shape[1]
@@ -446,31 +446,28 @@
     copy.wait()
 
 
-def down_piece(hidden, held_ref, acc_ref, near_ref, far_ref, sum_s, piece):
+def down_piece(hidden, held_ref, acc_ref, out_ref, piece):
     depth = hidden.shape[1]
-    count, width = near_ref.shape
+    width = out_ref.shape[1]
     cols = pl.ds(pl.multiple_of(piece * width, width), width)
-    sum_s[...] = acc_ref[:, cols] + jnp.dot(hidden, held_ref[depth:, cols], preferred_element_type=f32)
-    pair = lax.axis_index("ctx") // 2
-    near_ref[...] = sum_s[pl.ds(pl.multiple_of(pair * count, count), count), :].astype(bf16)
-    far_ref[...] = sum_s[pl.ds(pl.multiple_of((1 - pair) * count, count), count), :].astype(bf16)
-
-
-def down_theirs_kernel(own_ref, peer_ref, scale_ref, acc_ref, near_ref, far_ref, hidden_ref, held_ref, sum_s):
+    out_ref[...] = (acc_ref[:, cols] + jnp.dot(hidden, held_ref[depth:, cols], preferred_element_type=f32)).astype(bf16)
+
+
+def down_theirs_kernel(own_ref, peer_ref, scale_ref, acc_ref, out_ref, hidden_ref, held_ref):
     hidden_ref[...] = hidden_of(own_ref, peer_ref, scale_ref[:, 0:1])
-    down_piece(hidden_ref[...], held_ref, acc_ref, near_ref, far_ref, sum_s, 1 - lax.axis_index("exp"))
-
-
-def down_mine_kernel(hidden_ref, acc_ref, near_ref, far_ref, held_ref, sum_s):
-    down_piece(hidden_ref[...], held_ref, acc_ref, near_ref, far_ref, sum_s, lax.axis_index("exp"))
-
-
-def reply_kernel(own_ref, peer_ref, first_ref, second_ref, sum_s):
-    odd = lax.axis_index("ctx") % 2
+    down_piece(hidden_ref[...], held_ref, acc_ref, out_ref, 1 - lax.axis_index("exp"))
+
+
+def down_mine_kernel(hidden_ref, acc_ref, out_ref, held_ref):
+    down_piece(hidden_ref[...], held_ref, acc_ref, out_ref, lax.axis_index("exp"))
+
+
+def reply_kernel(own_ref, peer_ref, r0_ref, r1_ref, r2_ref, r3_ref, sum_s):
+    ctx = lax.axis_index("ctx")
     sum_s[...] = own_ref[...].astype(f32) + peer_ref[...].astype(f32)
-    count = first_ref.shape[0]
-    for place, ref in ((odd, first_ref), (1 - odd, second_ref)):
-        ref[...] = sum_s[pl.ds(pl.multiple_of(place * count, 8), count), :].astype(bf16)
+    count = r0_ref.shape[0]
+    for p, ref in enumerate((r0_ref, r1_ref, r2_ref, r3_ref)):
+        ref[...] = sum_s[pl.ds(pl.multiple_of((ctx ^ p) * count, 8), count), :].astype(bf16)
 
 
 def finish_kernel(
@@ -643,9 +640,10 @@
                 (own, peer, first, second, token), keep=keep,
             )
 
-    def dispatch(out):
+    def dispatch(out, order):
         with jax.named_scope("dispatch"):
-            return [out[0]] + [from_owner(out[p], p) for p in away]
+            arrived = {p: from_owner(out[p], p) for p in order}
+            return [out[0]] + [arrived[p] for p in away]
 
     own, held_out, held = project(blocks[0], blocks[1], pack, (held_out, held))
     peer = sum_exp(own)
@@ -655,14 +653,14 @@
         )
     first, second, *out, held_out, held = select(own, peer, pack, entered[0], token, (held_out, held))
     streams = [first, second]
-    sent = [dispatch(out)]
-    token = call(after_kernel, token_kind, [AN], (), (out[0],), us=ORDER)
+    sent = [dispatch(out, (1,2,3))]
+    token = call(after_kernel, token_kind, [AN], (), (out[0],), us=5.0)
     own, _, held = project(blocks[2], blocks[3], token, (held_out, held))
     peer = sum_exp(own)
-    token = call(after_kernel, token_kind, [AN], (), (own,), us=ORDER)
+    token = call(after_kernel, token_kind, [AN], (), (own,), us=5.0)
     first, second, *out, held = select(own, peer, entered[1], entered[2], token, (held,))
     streams += [first, second]
-    sent.append(dispatch(out))
+    sent.append(dispatch(out, (2, 3, 1)))
     with jax.named_scope("hold_weights"):
         held_second, held = call(
             hold_late_kernel, (held_kind,), [HB, AN], [dma], (wg, out[0]), us=HOLD, keep=(held,)
@@ -672,7 +670,7 @@
             first_half_kernel,
             (shape(slots_total, 2 * part_width + 128, bf16), shape(slots_total, half_width, bf16)),
             [VM] * 9 + [HB], [pltpu.VMEM((slots_total, 128), f32), dma],
-            (*sent[0], *sent[1], in_hbm(gain), wu), keep=(held, held_second), show=True,
+            (*(sent[k][p] for k in range(2) for p in (0, 2, 3, 1)), in_hbm(gain), wu), keep=(held, held_second), show=True,
         )
         peer_first = swap_tp(first)
         second, held, _ = call(
@@ -686,28 +684,14 @@
             (shape(slots_total, half_width, f32), shape(slots_total, 128, f32)), [VM] * 2 + [HB], [dma],
             (first, peer_first, wd), keep=(held,), show=True,
         )
-        piece = shape(slots_total // 2, piece_width, bf16)
-        total = pltpu.VMEM((slots_total, piece_width), f32)
-        theirs_near, theirs_far, hidden, held = call(
-            down_theirs_kernel, (piece, piece, shape(slots_total, part_width, bf16)),
-            [VM] * 4, [total], (second, peer_second, scale, acc), keep=(held,), show=True,
+        piece = shape(slots_total, piece_width, bf16)
+        theirs, hidden, held = call(
+            down_theirs_kernel, (piece, shape(slots_total, part_width, bf16)), [VM] * 4, (),
+            (second, peer_second, scale, acc), keep=(held,), show=True,
         )
     with jax.named_scope("sum_experts"):
-        swap = [(0, 1), (1, 0)]
-        peer_far = lax.ppermute(theirs_far, "exp", swap)
-        theirs_near, _ = lax.optimization_barrier((theirs_near, theirs_far))
-        peer_near = lax.ppermute(theirs_near, "exp", swap)
-        mine_near, mine_far, _ = call(
-            down_mine_kernel, (piece, piece), [VM] * 2, [total], (hidden, acc), keep=(held,), show=True
-        )
-    def reply(own, peer):
-        small = shape(CAP, piece_width, bf16)
-        return call(
-            reply_kernel, (small, small), [VM] * 2, [pltpu.VMEM((slots_total // 2, piece_width), f32)], (own, peer)
-        )
-
-    def send(x, p):
-        return permute(x, [(number(c, x_at, t), number(c ^ p, x_at, t)) for c, x_at in chips for t in range(tp_count)])
+        peer = lax.ppermute(theirs, "exp", [(0, 1), (1, 0)])
+        mine, _ = call(down_mine_kernel, (piece,), [VM] * 2, (), (hidden, acc), keep=(held,), show=True)
 
     def send_home(p, after):
         stream, _ = lax.optimization_barrier((streams[p], after))
@@ -717,14 +701,17 @@
                 [(number(c, c % exp_count, owner(c)), number(c ^ p, c % exp_count, owner(c))) for c in range(ctx_count)],
             )
 
+    def send(x, p):
+        with jax.named_scope("reply"):
+            return permute(x, [(number(c, x_at, t), number(c ^ p, x_at, t)) for c, x_at in chips for t in range(tp_count)])
+
+    home = [send_home(p, mine) for p in away]
     with jax.named_scope("reply"):
-        far_home = [send_home(p, mine_far) for p in (2, 3)]
-        r2, r3 = reply(mine_far, peer_far)
-        far = [send(r2, 2), send(r3, 3)]
-        mine_near, peer_near, _ = lax.optimization_barrier((mine_near, peer_near, r2))
-        r0, r1 = reply(mine_near, peer_near)
-        replies = [r0, send(r1, 1), *far]
-        home = [send_home(1, r1), *far_home]
+        small = shape(CAP, piece_width, bf16)
+        replies = call(
+            reply_kernel, (small,) * 4, [VM] * 2, [pltpu.VMEM((slots_total, piece_width), f32)], (mine, peer)
+        )
+    replies = [replies[0]] + [send(replies[p], p) for p in away]
     with jax.named_scope("finish"):
         return call(
             finish_kernel, shape(tokens, piece_width, bf16), [VM] * 10, (),

time: 96.8 us -> 91.5 us (0.945)
  starting transfers between devices: 48 us -> 44.9 us
  waiting for transfers between devices: 14 us -> 12 us
    ppermute x20, waiting for transfers between devices: 12.7 us -> 9.5 us  [permute(): return lax.ppermute(x, AXES, pairs)]
    ppermute x20, starting transfers between devices: 44.8 us -> 42.4 us  [permute(): return lax.ppermute(x, AXES, pairs)]
    ppermute x2 -> x1, waiting for transfers between devices: 0.01 us -> 1.12 us  [fast_body(): peer = lax.ppermute(theirs, 'exp', [(0, 1), (1, 0)])]
    ppermute x2 -> x1, starting transfers between devices: 2.09 us -> 1.34 us  [fast_body(): peer = lax.ppermute(theirs, 'exp', [(0, 1), (1, 0)])]
    pallas_call x21 -> x20, Pallas kernels: 33.7 us -> 33.6 us  [call(): pl.pallas_call(body_kernel, out_shape=outs + tuple((pltpu.VMEM(x.shape, x...]
  transfers between devices with their start and end apart: 26 -> 25, of which waited for: 9 -> 8; matrix products, arithmetic and copies ran while one was open for 0% -> 0% of each run, Pallas kernels for 25% -> 26%
where the time goes in v5:
time: 91.5 us; the launch traced here: 90.8 us
  starting transfers between devices  44.9 us (49%)
  Pallas kernels  33.6 us (37%)
  waiting for transfers between devices  12 us (13%)
    ppermute x20, starting transfers between devices, permute(): return lax.ppermute(x, AXES, pairs)  42.4 us
    pallas_call x20, Pallas kernels, call(): pl.pallas_call(body_kernel, out_shape=outs + tuple((pltpu.VMEM(x.shape, x...  33.6 us
    ppermute x20, waiting for transfers between devices, permute(): return lax.ppermute(x, AXES, pairs)  9.5 us
  transfers between devices with their start and end apart: 25, of which 8 were waited for; matrix products, arithmetic and copies ran while one was open for 0% of the time, Pallas kernels for 26%

profile of v5, /device:TPU:0, one launch (start us, length us, event | category | flops | bytes accessed | tf_op | source)
XLA Modules:
  0.0 90.8 jit_solution(14199851104642329965)
XLA Ops:
  0.0 3.3 %scan.1 = (f32[512,128]{1,0:T(8,128)S(1)}, f32[512,128]{1,0:T(8,128)S(1)}, f32[512,128]{1,0:T(8,128)S(1)}, f32[128,128]{1,0:T(8,128)S(1)}, bf16[144,128]{1,0:T(8,128)(2,1)S(1)}) custom-call(f32[16,64]{1,0:T(8,128)} %bitcast.8, f32[16,64]{1,0:T(8,128)} %bitcast.9, f32[64,1024]{1,0:T(8,128)} %refs_2_.3, bf16[64,1024]{1,0:T(8,128)(2,1)} %refs_3_.1, ...), custom_call_target="tpu_custom_call" | custom-call | tf_op jit(solution)/shard_map/scan/pallas_call | solution.py:514
  3.3 0.5 collective-permute-start.5
  3.7 4.6 %collective-permute-start.2 = (bf16[144,128]{1,0:T(8,128)(2,1)S(1)}, bf16[144,128]{1,0:T(8,128)(2,1)S(1)}, u32[]{:S(2)}, u32[]{:S(2)}) collective-permute-start(bf16[144,128]{1,0:T(8,128)(2,1)S(1)} %get-tuple-element.64.refs_2_.refs_4_), channel_id=1, source_target_pairs={{0,12},{1,13},{2,14},{3,15},{4,8},{5,9},{6,10},{7,11},{8,4},{9,5},... | collective-permute-start | bytes 110600 | tf_op jit(solution)/shard_map/relay/ppermute | solution.py:563
  8.4 0.7 collective-permute-start
  9.1 1.9 %spread.1 = (f32[512,128]{1,0:T(8,128)S(1)}, f32[8192,128]{1,0:T(8,128)S(1)}, bf16[64,4096]{1,0:T(8,128)(2,1)S(1)}) custom-call(f32[16,64]{1,0:T(8,128)} %bitcast.10, f32[512,128]{1,0:T(8,128)S(1)} %get-tuple-element.65.refs_1_, f32[512,128]{1,0:T(8,128)S(1)} %get-tuple-element.66.refs_2_, f32[512,128]{1,0:T(8,128)S(1)} %get-tuple-element.67.refs_3_, ...), custom_call_target="tpu_custom_call" | custom-call | flops 2000000000 | tf_op jit(solution)/shard_map/spread/pallas_call | solution.py:514
  11.0 2.2 %collective-permute-done.1.refs_1_.refs_2_ = bf16[144,128]{1,0:T(8,128)(2,1)S(1)} collective-permute-done((bf16[144,128]{1,0:T(8,128)(2,1)S(1)}, bf16[144,128]{1,0:T(8,128)(2,1)S(1)}, u32[]{:S(2)}, u32[]{:S(2)}) %collective-permute-start.1) | collective-permute-done | bytes 36896 | tf_op jit(solution)/shard_map/relay/ppermute | solution.py:563
  13.2 0.5 correct.1.refs_0_
  13.8 1.3 %collective-permute-done.3.refs_1_ = bf16[64,1024]{1,0:T(8,128)(2,1)S(1)} collective-permute-done((bf16[64,1024]{1,0:T(8,128)(2,1)S(1)}, bf16[64,1024]{1,0:T(8,128)(2,1)S(1)}, u32[]{:S(2)}, u32[]{:S(2)}) %collective-permute-start.3) | collective-permute-done | bytes 131104 | tf_op jit(solution)/shard_map/gather_gated/ppermute | solution.py:572
  15.2 0.1 gather_gated.1
  15.2 2.5 %collective-permute-start.4 = (bf16[64,2560]{1,0:T(8,128)(2,1)S(1)}, bf16[64,2560]{1,0:T(8,128)(2,1)S(1)}, u32[]{:S(2)}, u32[]{:S(2)}) collective-permute-start(bf16[64,2560]{1,0:T(8,128)(2,1)S(1)} %get-tuple-element.73), channel_id=1, source_target_pairs={{4,0},{6,2},{0,4},{2,6},{13,9},{15,11},{9,13},{11,15},{20,16},{22,... | collective-permute-start | bytes 983048 | tf_op jit(solution)/shard_map/gather_gated/ppermute | solution.py:563
  17.8 1.3 %collective-permute-start.10 = (bf16[64,2560]{1,0:T(8,128)(2,1)S(1)}, bf16[64,2560]{1,0:T(8,128)(2,1)S(1)}, u32[]{:S(2)}, u32[]{:S(2)}) collective-permute-start(bf16[64,2560]{1,0:T(8,128)(2,1)S(1)} %get-tuple-element.88), channel_id=1, source_target_pairs={{8,0},{10,2},{12,4},{14,6},{1,9},{3,11},{5,13},{7,15},{24,16},{26,... | collective-permute-start | bytes 983048 | tf_op jit(solution)/shard_map/gather_gated/ppermute | solution.py:563
  19.1 1.3 %collective-permute-start.11 = (bf16[64,2560]{1,0:T(8,128)(2,1)S(1)}, bf16[64,2560]{1,0:T(8,128)(2,1)S(1)}, u32[]{:S(2)}, u32[]{:S(2)}) collective-permute-start(bf16[64,2560]{1,0:T(8,128)(2,1)S(1)} %get-tuple-element.89), channel_id=1, source_target_pairs={{12,0},{14,2},{8,4},{10,6},{5,9},{7,11},{1,13},{3,15},{28,16},{30,... | collective-permute-start | bytes 983048 | tf_op jit(solution)/shard_map/gather_gated/ppermute | solution.py:563
  20.4 2.9 %hold_out_weight.1 = (bf16[2048,1024]{1,0:T(8,128)(2,1)S(1)}, bf16[4096,2048]{1,0:T(8,128)(2,1)S(1)}) custom-call(bf16[1024,1024]{1,0:T(8,128)(2,1)} %refs_0_.3, bf16[1024,1024]{1,0:T(8,128)(2,1)S(1)} %collective-permute-done.5.refs_1_, bf16[2048,4096]{1,0:T(8,128)(2,1)} %refs_0_.5, bf16[64,2560]{1,0:T(8,128)(2,1)S(1)} %get-tuple-element.72.refs_3_.refs_0_), custom_call_target="tpu_custom_call" | custom-call | tf_op jit(solution)/shard_map/hold_out_weight/pallas_call | solution.py:514
  23.3 0.9 %collective-permute-done.4.refs_1_ = bf16[64,2560]{1,0:T(8,128)(2,1)S(1)} collective-permute-done((bf16[64,2560]{1,0:T(8,128)(2,1)S(1)}, bf16[64,2560]{1,0:T(8,128)(2,1)S(1)}, u32[]{:S(2)}, u32[]{:S(2)}) %collective-permute-start.4) | collective-permute-done | bytes 327712 | tf_op jit(solution)/shard_map/gather_gated/ppermute | solution.py:563
  24.2 0.8 project.2
  25.0 3.4 %collective-permute-start.6 = (bf16[128,1024]{1,0:T(8,128)(2,1)S(1)}, bf16[128,1024]{1,0:T(8,128)(2,1)S(1)}, u32[]{:S(2)}, u32[]{:S(2)}) collective-permute-start(bf16[128,1024]{1,0:T(8,128)(2,1)S(1)} %get-tuple-element.77.refs_2_.refs_0_), channel_id=1, source_target_pairs={{0,2},{2,0},{4,6},{6,4},{9,11},{11,9},{13,15},{15,13},{16,18},{18,... | collective-permute-start | bytes 786440 | tf_op jit(solution)/shard_map/sum_exp/ppermute | solution.py:563
  28.4 4.7 %hold_weights.2 = (f32[8,128]{1,0:T(8,128)S(1)}, bf16[4096,2048]{1,0:T(8,128)(2,1)S(1)}) custom-call(bf16[2048,4096]{1,0:T(8,128)(2,1)} %refs_0_.5, bf16[2048,4096]{1,0:T(8,128)(2,1)} %refs_9_.1, bf16[128,1024]{1,0:T(8,128)(2,1)S(1)} %get-tuple-element.77.refs_2_.refs_0_, ...), custom_call_target="tpu_custom_call", output_to_operand_aliasing={{1}: (3, {})} | custom-call | flops 3000000000 | tf_op jit(solution)/shard_map/hold_weights/pallas_call | solution.py:514
  33.1 0.2 collective-permute-done.6.refs_1_
  33.3 0.4 select.2
  33.7 1.7 %collective-permute-start.7 = (bf16[80,1024]{1,0:T(8,128)(2,1)S(1)}, bf16[80,1024]{1,0:T(8,128)(2,1)S(1)}, u32[]{:S(2)}, u32[]{:S(2)}) collective-permute-start(bf16[80,1024]{1,0:T(8,128)(2,1)S(1)} %get-tuple-element.85), channel_id=1, source_target_pairs={{0,8},{2,10},{4,12},{6,14},{9,1},{11,3},{13,5},{15,7},{16,24},{18,... | collective-permute-start | bytes 491528 | tf_op jit(solution)/shard_map/dispatch/ppermute | solution.py:563
  35.4 0.8 project.3
  36.2 3.4 %collective-permute-start.12 = (bf16[128,1024]{1,0:T(8,128)(2,1)S(1)}, bf16[128,1024]{1,0:T(8,128)(2,1)S(1)}, u32[]{:S(2)}, u32[]{:S(2)}) collective-permute-start(bf16[128,1024]{1,0:T(8,128)(2,1)S(1)} %get-tuple-element.92.refs_0_), channel_id=1, source_target_pairs={{0,2},{2,0},{4,6},{6,4},{9,11},{11,9},{13,15},{15,13},{16,18},{18,... | collective-permute-start | bytes 786440 | tf_op jit(solution)/shard_map/sum_exp/ppermute | solution.py:563
  39.7 1.3 %collective-permute-start.8 = (bf16[80,1024]{1,0:T(8,128)(2,1)S(1)}, bf16[80,1024]{1,0:T(8,128)(2,1)S(1)}, u32[]{:S(2)}, u32[]{:S(2)}) collective-permute-start(bf16[80,1024]{1,0:T(8,128)(2,1)S(1)} %get-tuple-element.86), channel_id=1, source_target_pairs={{0,12},{2,14},{4,8},{6,10},{9,5},{11,7},{13,1},{15,3},{16,28},{18,... | collective-permute-start | bytes 491528 | tf_op jit(solution)/shard_map/dispatch/ppermute | solution.py:563
  41.0 5.2 %collective-permute-start.9 = (bf16[80,1024]{1,0:T(8,128)(2,1)S(1)}, bf16[80,1024]{1,0:T(8,128)(2,1)S(1)}, u32[]{:S(2)}, u32[]{:S(2)}) collective-permute-start(bf16[80,1024]{1,0:T(8,128)(2,1)S(1)} %get-tuple-element.87), channel_id=1, source_target_pairs={{0,4},{2,6},{4,0},{6,2},{9,13},{11,15},{13,9},{15,11},{16,20},{18,... | collective-permute-start | bytes 491528 | tf_op jit(solution)/shard_map/dispatch/ppermute | solution.py:563
  46.2 0.4 select.3
  46.6 1.3 %collective-permute-start.13 = (bf16[80,1024]{1,0:T(8,128)(2,1)S(1)}, bf16[80,1024]{1,0:T(8,128)(2,1)S(1)}, u32[]{:S(2)}, u32[]{:S(2)}) collective-permute-start(bf16[80,1024]{1,0:T(8,128)(2,1)S(1)} %get-tuple-element.95), channel_id=1, source_target_pairs={{0,8},{2,10},{4,12},{6,14},{9,1},{11,3},{13,5},{15,7},{16,24},{18,... | collective-permute-start | bytes 491528 | tf_op jit(solution)/shard_map/dispatch/ppermute | solution.py:563
  47.9 1.3 %collective-permute-start.14 = (bf16[80,1024]{1,0:T(8,128)(2,1)S(1)}, bf16[80,1024]{1,0:T(8,128)(2,1)S(1)}, u32[]{:S(2)}, u32[]{:S(2)}) collective-permute-start(bf16[80,1024]{1,0:T(8,128)(2,1)S(1)} %get-tuple-element.96), channel_id=1, source_target_pairs={{0,12},{2,14},{4,8},{6,10},{9,5},{11,7},{13,1},{15,3},{16,28},{18,... | collective-permute-start | bytes 491528 | tf_op jit(solution)/shard_map/dispatch/ppermute | solution.py:563
  49.2 3.5 %collective-permute-start.15 = (bf16[80,1024]{1,0:T(8,128)(2,1)S(1)}, bf16[80,1024]{1,0:T(8,128)(2,1)S(1)}, u32[]{:S(2)}, u32[]{:S(2)}) collective-permute-start(bf16[80,1024]{1,0:T(8,128)(2,1)S(1)} %get-tuple-element.97), channel_id=1, source_target_pairs={{0,4},{2,6},{4,0},{6,2},{9,13},{11,15},{13,9},{15,11},{16,20},{18,... | collective-permute-start | bytes 491528 | tf_op jit(solution)/shard_map/dispatch/ppermute | solution.py:563
  52.8 3.4 %hold_weights.3 = (bf16[4096,2048]{1,0:T(8,128)(2,1)S(1)}, bf16[4096,2048]{1,0:T(8,128)(2,1)S(1)}) custom-call(bf16[2048,4096]{1,0:T(8,128)(2,1)} %refs_0_.5, bf16[80,1024]{1,0:T(8,128)(2,1)S(1)} %get-tuple-element.94.refs_1_.refs_4_, bf16[4096,2048]{1,0:T(8,128)(2,1)S(1)} %get-tuple-element.98.refs_2_), custom_call_target="tpu_custom_call", output_to_operand_aliasing={{1}: (2, {})} | custom-call | flops 3000000000 | tf_op jit(solution)/shard_map/hold_weights/pallas_call | solution.py:514
  56.2 0.2 collective-permute-done.15.refs_7_
  56.5 4.1 %gate_up.2 = (bf16[160,4224]{1,0:T(8,128)(2,1)S(1)}, bf16[160,2048]{1,0:T(8,128)(2,1)S(1)}, bf16[4096,2048]{1,0:T(8,128)(2,1)S(1)}, bf16[4096,2048]{1,0:T(8,128)(2,1)S(1)}) custom-call(bf16[80,1024]{1,0:T(8,128)(2,1)S(1)} %get-tuple-element.84.refs_0_, ...), custom_call_target="tpu_custom_call", output_to_operand_aliasing={{2}: (10, {}), {3}: (11, {})} | custom-call | tf_op jit(solution)/shard_map/gate_up/pallas_call | solution.py:514
  60.7 3.4 %gate_up.3 = (bf16[160,4096]{1,0:T(8,128)(2,1)S(1)}, bf16[4096,2048]{1,0:T(8,128)(2,1)S(1)}, bf16[4096,2048]{1,0:T(8,128)(2,1)S(1)}) custom-call(bf16[160,2048]{1,0:T(8,128)(2,1)S(1)} %get-tuple-element.101.refs_0_, bf16[4096,2048]{1,0:T(8,128)(2,1)} %refs_2_.5, ...), custom_call_target="tpu_custom_call", output_to_operand_aliasing={{1}: (2, {}), {2}: (3, {})} | custom-call | tf_op jit(solution)/shard_map/gate_up/pallas_call | solution.py:514
  64.1 0.6 collective-permute-start.16
  64.6 3.4 %down.2 = (f32[160,2048]{1,0:T(8,128)S(1)}, f32[160,128]{1,0:T(8,128)S(1)}, bf16[4096,2048]{1,0:T(8,128)(2,1)S(1)}) custom-call(bf16[160,4224]{1,0:T(8,128)(2,1)S(1)} %get-tuple-element.105.refs_0_, bf16[160,4224]{1,0:T(8,128)(2,1)S(1)} %collective-permute-done.17.refs_1_, bf16[4096,2048]{1,0:T(8,128)(2,1)} %refs_2_.5, ...), custom_call_target="tpu_custom_call", output_to_operand_aliasing={{2}: (3, {})} | custom-call | tf_op jit(solution)/shard_map/down/pallas_call | solution.py:514
  68.1 1.3 %down.3 = (bf16[160,1024]{1,0:T(8,128)(2,1)S(1)}, bf16[160,2048]{1,0:T(8,128)(2,1)S(1)}, bf16[4096,2048]{1,0:T(8,128)(2,1)S(1)}) custom-call(bf16[160,4096]{1,0:T(8,128)(2,1)S(1)} %get-tuple-element.104.refs_0_, bf16[160,4096]{1,0:T(8,128)(2,1)S(1)} %collective-permute-done.16.refs_1_, ...), custom_call_target="tpu_custom_call", output_to_operand_aliasing={{2}: (4, {})} | custom-call | tf_op jit(solution)/shard_map/down/pallas_call | solution.py:514
  69.4 1.3 %collective-permute-start.21 = (bf16[160,1024]{1,0:T(8,128)(2,1)S(1)}, bf16[160,1024]{1,0:T(8,128)(2,1)S(1)}, u32[]{:S(2)}, u32[]{:S(2)}) collective-permute-start(bf16[160,1024]{1,0:T(8,128)(2,1)S(1)} %get-tuple-element.118), channel_id=1, source_target_pairs={{0,2},{2,0},{1,3},{3,1},{4,6},{6,4},{5,7},{7,5},{8,10},{10,8},{9,1... | collective-permute-start | bytes 983048 | tf_op jit(solution)/shard_map/sum_experts/ppermute | solution.py:693
  70.7 0.9 sum_experts.1
  71.6 3.7 %collective-permute-start.18 = (bf16[64,1024]{1,0:T(8,128)(2,1)S(1)}, bf16[64,1024]{1,0:T(8,128)(2,1)S(1)}, u32[]{:S(2)}, u32[]{:S(2)}) collective-permute-start(bf16[64,1024]{1,0:T(8,128)(2,1)S(1)} %get-tuple-element.113), channel_id=1, source_target_pairs={{0,4},{6,2},{9,13},{15,11},{16,20},{22,18},{25,29},{31,27}} | collective-permute-start | bytes 393224 | tf_op jit(solution)/shard_map/stream_home/ppermute | solution.py:563
  75.4 1.3 %collective-permute-start.19 = (bf16[64,1024]{1,0:T(8,128)(2,1)S(1)}, bf16[64,1024]{1,0:T(8,128)(2,1)S(1)}, u32[]{:S(2)}, u32[]{:S(2)}) collective-permute-start(bf16[64,1024]{1,0:T(8,128)(2,1)S(1)} %get-tuple-element.115), channel_id=1, source_target_pairs={{0,8},{6,14},{9,1},{15,7},{16,24},{22,30},{25,17},{31,23}} | collective-permute-start | bytes 393224 | tf_op jit(solution)/shard_map/stream_home/ppermute | solution.py:563
  76.7 1.3 %collective-permute-start.20 = (bf16[64,1024]{1,0:T(8,128)(2,1)S(1)}, bf16[64,1024]{1,0:T(8,128)(2,1)S(1)}, u32[]{:S(2)}, u32[]{:S(2)}) collective-permute-start(bf16[64,1024]{1,0:T(8,128)(2,1)S(1)} %get-tuple-element.117), channel_id=1, source_target_pairs={{0,12},{6,10},{9,5},{15,3},{16,28},{22,26},{25,21},{31,19}} | collective-permute-start | bytes 393224 | tf_op jit(solution)/shard_map/stream_home/ppermute | solution.py:563
  78.0 1.1 %collective-permute-done.21.refs_1_ = bf16[160,1024]{1,0:T(8,128)(2,1)S(1)} collective-permute-done((bf16[160,1024]{1,0:T(8,128)(2,1)S(1)}, bf16[160,1024]{1,0:T(8,128)(2,1)S(1)}, u32[]{:S(2)}, u32[]{:S(2)}) %collective-permute-start.21) | collective-permute-done | bytes 327712 | tf_op jit(solution)/shard_map/sum_experts/ppermute | solution.py:693
  79.1 0.1 reply.1
  79.2 1.7 %collective-permute-start.22 = (bf16[40,1024]{1,0:T(8,128)(2,1)S(1)}, bf16[40,1024]{1,0:T(8,128)(2,1)S(1)}, u32[]{:S(2)}, u32[]{:S(2)}) collective-permute-start(bf16[40,1024]{1,0:T(8,128)(2,1)S(1)} %get-tuple-element.120), channel_id=1, source_target_pairs={{0,4},{1,5},{2,6},{3,7},{4,0},{5,1},{6,2},{7,3},{8,12},{9,13},{10,... | collective-permute-start | bytes 245768 | tf_op jit(solution)/shard_map/reply/ppermute | solution.py:563
  80.9 2.1 %collective-permute-start.23 = (bf16[40,1024]{1,0:T(8,128)(2,1)S(1)}, bf16[40,1024]{1,0:T(8,128)(2,1)S(1)}, u32[]{:S(2)}, u32[]{:S(2)}) collective-permute-start(bf16[40,1024]{1,0:T(8,128)(2,1)S(1)} %get-tuple-element.121), channel_id=1, source_target_pairs={{0,8},{1,9},{2,10},{3,11},{4,12},{5,13},{6,14},{7,15},{8,0},{9,1},... | collective-permute-start | bytes 245768 | tf_op jit(solution)/shard_map/reply/ppermute | solution.py:563
  83.1 0.7 collective-permute-start.24
  83.8 0.9 collective-permute-done.22.refs_7_
  84.6 5.0 %collective-permute-done.23.refs_8_ = bf16[40,1024]{1,0:T(8,128)(2,1)S(1)} collective-permute-done((bf16[40,1024]{1,0:T(8,128)(2,1)S(1)}, bf16[40,1024]{1,0:T(8,128)(2,1)S(1)}, u32[]{:S(2)}, u32[]{:S(2)}) %collective-permute-start.23) | collective-permute-done | bytes 81952 | tf_op jit(solution)/shard_map/reply/ppermute | solution.py:563
  89.7 1.1 %finish.1 = bf16[64,1024]{1,0:T(8,128)(2,1)} custom-call(bf16[64,1024]{1,0:T(8,128)(2,1)S(1)} %get-tuple-element.82.refs_0_, bf16[64,1024]{1,0:T(8,128)(2,1)S(1)} %collective-permute-done.18.refs_1_, bf16[64,1024]{1,0:T(8,128)(2,1)S(1)} %collective-permute-done.19.refs_2_, bf16[64,1024]{1,0:T(8,128)(2,1)S(1)} %collective-permute-done.20.refs_3_, ...), custom_call_target="tpu_custom_call" | custom-call | tf_op jit(solution)/shard_map/finish/pallas_call | solution.py:514
  (24 shorter events, 0.2 us)
Async XLA Ops:
  3.3 17.1 %collective-permute-start.5 = (bf16[1024,1024]{1,0:T(8,128)(2,1)}, bf16[1024,1024]{1,0:T(8,128)(2,1)S(1)}, u32[]{:S(2)}, u32[]{:S(2)}) collective-permute-start(bf16[1024,1024]{1,0:T(8,128)(2,1)} %refs_0_.3), channel_id=1, source_target_pairs={{0,1},{1,0},{2,3},{3,2},{4,5},{5,4},{6,7},{7,6},{8,9},{9,8},{10,11... | collective-permute-start | bytes 6291464 | tf_op jit(solution)/shard_map/ppermute | solution.py:572
  3.7 7.3 %collective-permute-start.2 = (bf16[144,128]{1,0:T(8,128)(2,1)S(1)}, bf16[144,128]{1,0:T(8,128)(2,1)S(1)}, u32[]{:S(2)}, u32[]{:S(2)}) collective-permute-start(bf16[144,128]{1,0:T(8,128)(2,1)S(1)} %get-tuple-element.64.refs_2_.refs_4_), channel_id=1, source_target_pairs={{0,12},{1,13},{2,14},{3,15},{4,8},{5,9},{6,10},{7,11},{8,4},{9,5},... | collective-permute-start | bytes 110600 | tf_op jit(solution)/shard_map/relay/ppermute | solution.py:563
  8.4 4.9 %collective-permute-start.1 = (bf16[144,128]{1,0:T(8,128)(2,1)S(1)}, bf16[144,128]{1,0:T(8,128)(2,1)S(1)}, u32[]{:S(2)}, u32[]{:S(2)}) collective-permute-start(bf16[144,128]{1,0:T(8,128)(2,1)S(1)} %get-tuple-element.64.refs_2_.refs_4_), channel_id=1, source_target_pairs={{0,8},{1,9},{2,10},{3,11},{4,12},{5,13},{6,14},{7,15},{8,0},{9,1},... | collective-permute-start | bytes 110600 | tf_op jit(solution)/shard_map/relay/ppermute | solution.py:563
  8.4 4.9 %collective-permute-start = (bf16[144,128]{1,0:T(8,128)(2,1)S(1)}, bf16[144,128]{1,0:T(8,128)(2,1)S(1)}, u32[]{:S(2)}, u32[]{:S(2)}) collective-permute-start(bf16[144,128]{1,0:T(8,128)(2,1)S(1)} %get-tuple-element.64.refs_2_.refs_4_), channel_id=1, source_target_pairs={{0,4},{1,5},{2,6},{3,7},{4,0},{5,1},{6,2},{7,3},{8,12},{9,13},{10,... | collective-permute-start | bytes 110600 | tf_op jit(solution)/shard_map/relay/ppermute | solution.py:563
  13.7 1.4 %collective-permute-start.3 = (bf16[64,1024]{1,0:T(8,128)(2,1)S(1)}, bf16[64,1024]{1,0:T(8,128)(2,1)S(1)}, u32[]{:S(2)}, u32[]{:S(2)}) collective-permute-start(bf16[64,1024]{1,0:T(8,128)(2,1)S(1)} %correct.1.refs_0_), channel_id=1, source_target_pairs={{0,1},{1,0},{2,3},{3,2},{4,5},{5,4},{6,7},{7,6},{8,9},{9,8},{10,11... | collective-permute-start | bytes 393224 | tf_op jit(solution)/shard_map/gather_gated/ppermute | solution.py:572
  15.2 9.0 %collective-permute-start.4 = (bf16[64,2560]{1,0:T(8,128)(2,1)S(1)}, bf16[64,2560]{1,0:T(8,128)(2,1)S(1)}, u32[]{:S(2)}, u32[]{:S(2)}) collective-permute-start(bf16[64,2560]{1,0:T(8,128)(2,1)S(1)} %get-tuple-element.73), channel_id=1, source_target_pairs={{4,0},{6,2},{0,4},{2,6},{13,9},{15,11},{9,13},{11,15},{20,16},{22,... | collective-permute-start | bytes 983048 | tf_op jit(solution)/shard_map/gather_gated/ppermute | solution.py:563
  17.8 17.6 %collective-permute-start.10 = (bf16[64,2560]{1,0:T(8,128)(2,1)S(1)}, bf16[64,2560]{1,0:T(8,128)(2,1)S(1)}, u32[]{:S(2)}, u32[]{:S(2)}) collective-permute-start(bf16[64,2560]{1,0:T(8,128)(2,1)S(1)} %get-tuple-element.88), channel_id=1, source_target_pairs={{8,0},{10,2},{12,4},{14,6},{1,9},{3,11},{5,13},{7,15},{24,16},{26,... | collective-permute-start | bytes 983048 | tf_op jit(solution)/shard_map/gather_gated/ppermute | solution.py:563
  19.1 16.4 %collective-permute-start.11 = (bf16[64,2560]{1,0:T(8,128)(2,1)S(1)}, bf16[64,2560]{1,0:T(8,128)(2,1)S(1)}, u32[]{:S(2)}, u32[]{:S(2)}) collective-permute-start(bf16[64,2560]{1,0:T(8,128)(2,1)S(1)} %get-tuple-element.89), channel_id=1, source_target_pairs={{12,0},{14,2},{8,4},{10,6},{5,9},{7,11},{1,13},{3,15},{28,16},{30,... | collective-permute-start | bytes 983048 | tf_op jit(solution)/shard_map/gather_gated/ppermute | solution.py:563
  25.0 8.3 %collective-permute-start.6 = (bf16[128,1024]{1,0:T(8,128)(2,1)S(1)}, bf16[128,1024]{1,0:T(8,128)(2,1)S(1)}, u32[]{:S(2)}, u32[]{:S(2)}) collective-permute-start(bf16[128,1024]{1,0:T(8,128)(2,1)S(1)} %get-tuple-element.77.refs_2_.refs_0_), channel_id=1, source_target_pairs={{0,2},{2,0},{4,6},{6,4},{9,11},{11,9},{13,15},{15,13},{16,18},{18,... | collective-permute-start | bytes 786440 | tf_op jit(solution)/shard_map/sum_exp/ppermute | solution.py:563
  33.7 15.5 %collective-permute-start.7 = (bf16[80,1024]{1,0:T(8,128)(2,1)S(1)}, bf16[80,1024]{1,0:T(8,128)(2,1)S(1)}, u32[]{:S(2)}, u32[]{:S(2)}) collective-permute-start(bf16[80,1024]{1,0:T(8,128)(2,1)S(1)} %get-tuple-element.85), channel_id=1, source_target_pairs={{0,8},{2,10},{4,12},{6,14},{9,1},{11,3},{13,5},{15,7},{16,24},{18,... | collective-permute-start | bytes 491528 | tf_op jit(solution)/shard_map/dispatch/ppermute | solution.py:563
  36.2 9.9 %collective-permute-start.12 = (bf16[128,1024]{1,0:T(8,128)(2,1)S(1)}, bf16[128,1024]{1,0:T(8,128)(2,1)S(1)}, u32[]{:S(2)}, u32[]{:S(2)}) collective-permute-start(bf16[128,1024]{1,0:T(8,128)(2,1)S(1)} %get-tuple-element.92.refs_0_), channel_id=1, source_target_pairs={{0,2},{2,0},{4,6},{6,4},{9,11},{11,9},{13,15},{15,13},{16,18},{18,... | collective-permute-start | bytes 786440 | tf_op jit(solution)/shard_map/sum_exp/ppermute | solution.py:563
  39.7 16.5 %collective-permute-start.8 = (bf16[80,1024]{1,0:T(8,128)(2,1)S(1)}, bf16[80,1024]{1,0:T(8,128)(2,1)S(1)}, u32[]{:S(2)}, u32[]{:S(2)}) collective-permute-start(bf16[80,1024]{1,0:T(8,128)(2,1)S(1)} %get-tuple-element.86), channel_id=1, source_target_pairs={{0,12},{2,14},{4,8},{6,10},{9,5},{11,7},{13,1},{15,3},{16,28},{18,... | collective-permute-start | bytes 491528 | tf_op jit(solution)/shard_map/dispatch/ppermute | solution.py:563
  41.0 15.2 %collective-permute-start.9 = (bf16[80,1024]{1,0:T(8,128)(2,1)S(1)}, bf16[80,1024]{1,0:T(8,128)(2,1)S(1)}, u32[]{:S(2)}, u32[]{:S(2)}) collective-permute-start(bf16[80,1024]{1,0:T(8,128)(2,1)S(1)} %get-tuple-element.87), channel_id=1, source_target_pairs={{0,4},{2,6},{4,0},{6,2},{9,13},{11,15},{13,9},{15,11},{16,20},{18,... | collective-permute-start | bytes 491528 | tf_op jit(solution)/shard_map/dispatch/ppermute | solution.py:563
  46.6 9.6 %collective-permute-start.13 = (bf16[80,1024]{1,0:T(8,128)(2,1)S(1)}, bf16[80,1024]{1,0:T(8,128)(2,1)S(1)}, u32[]{:S(2)}, u32[]{:S(2)}) collective-permute-start(bf16[80,1024]{1,0:T(8,128)(2,1)S(1)} %get-tuple-element.95), channel_id=1, source_target_pairs={{0,8},{2,10},{4,12},{6,14},{9,1},{11,3},{13,5},{15,7},{16,24},{18,... | collective-permute-start | bytes 491528 | tf_op jit(solution)/shard_map/dispatch/ppermute | solution.py:563
  47.9 8.3 %collective-permute-start.14 = (bf16[80,1024]{1,0:T(8,128)(2,1)S(1)}, bf16[80,1024]{1,0:T(8,128)(2,1)S(1)}, u32[]{:S(2)}, u32[]{:S(2)}) collective-permute-start(bf16[80,1024]{1,0:T(8,128)(2,1)S(1)} %get-tuple-element.96), channel_id=1, source_target_pairs={{0,12},{2,14},{4,8},{6,10},{9,5},{11,7},{13,1},{15,3},{16,28},{18,... | collective-permute-start | bytes 491528 | tf_op jit(solution)/shard_map/dispatch/ppermute | solution.py:563
  49.2 7.2 %collective-permute-start.15 = (bf16[80,1024]{1,0:T(8,128)(2,1)S(1)}, bf16[80,1024]{1,0:T(8,128)(2,1)S(1)}, u32[]{:S(2)}, u32[]{:S(2)}) collective-permute-start(bf16[80,1024]{1,0:T(8,128)(2,1)S(1)} %get-tuple-element.97), channel_id=1, source_target_pairs={{0,4},{2,6},{4,0},{6,2},{9,13},{11,15},{13,9},{15,11},{16,20},{18,... | collective-permute-start | bytes 491528 | tf_op jit(solution)/shard_map/dispatch/ppermute | solution.py:563
  60.6 4.0 %collective-permute-start.17 = (bf16[160,4224]{1,0:T(8,128)(2,1)S(1)}, bf16[160,4224]{1,0:T(8,128)(2,1)S(1)}, u32[]{:S(2)}, u32[]{:S(2)}) collective-permute-start(bf16[160,4224]{1,0:T(8,128)(2,1)S(1)} %get-tuple-element.105.refs_0_), channel_id=1, source_target_pairs={{0,1},{1,0},{2,3},{3,2},{4,5},{5,4},{6,7},{7,6},{8,9},{9,8},{10,11... | collective-permute-start | bytes 4055048 | tf_op jit(solution)/shard_map/gate_up/ppermute | solution.py:572
  64.1 4.0 %collective-permute-start.16 = (bf16[160,4096]{1,0:T(8,128)(2,1)S(1)}, bf16[160,4096]{1,0:T(8,128)(2,1)S(1)}, u32[]{:S(2)}, u32[]{:S(2)}) collective-permute-start(bf16[160,4096]{1,0:T(8,128)(2,1)S(1)} %get-tuple-element.104.refs_0_), channel_id=1, source_target_pairs={{0,1},{1,0},{2,3},{3,2},{4,5},{5,4},{6,7},{7,6},{8,9},{9,8},{10,11... | collective-permute-start | bytes 3932168 | tf_op jit(solution)/shard_map/gate_up/ppermute | solution.py:572
  68.0 21.6 %copy-start = (f32[64,2]{0,1:T(2,128)S(1)}, f32[64,2]{0,1:T(2,128)}, u32[]{:S(2)}) copy-start(f32[64,2]{0,1:T(2,128)} %param.26) | copy-start | bytes 1540
  69.4 9.7 %collective-permute-start.21 = (bf16[160,1024]{1,0:T(8,128)(2,1)S(1)}, bf16[160,1024]{1,0:T(8,128)(2,1)S(1)}, u32[]{:S(2)}, u32[]{:S(2)}) collective-permute-start(bf16[160,1024]{1,0:T(8,128)(2,1)S(1)} %get-tuple-element.118), channel_id=1, source_target_pairs={{0,2},{2,0},{1,3},{3,1},{4,6},{6,4},{5,7},{7,5},{8,10},{10,8},{9,1... | collective-permute-start | bytes 983048 | tf_op jit(solution)/shard_map/sum_experts/ppermute | solution.py:693
  71.6 11.4 %collective-permute-start.18 = (bf16[64,1024]{1,0:T(8,128)(2,1)S(1)}, bf16[64,1024]{1,0:T(8,128)(2,1)S(1)}, u32[]{:S(2)}, u32[]{:S(2)}) collective-permute-start(bf16[64,1024]{1,0:T(8,128)(2,1)S(1)} %get-tuple-element.113), channel_id=1, source_target_pairs={{0,4},{6,2},{9,13},{15,11},{16,20},{22,18},{25,29},{31,27}} | collective-permute-start | bytes 393224 | tf_op jit(solution)/shard_map/stream_home/ppermute | solution.py:563
  75.4 8.4 %collective-permute-start.19 = (bf16[64,1024]{1,0:T(8,128)(2,1)S(1)}, bf16[64,1024]{1,0:T(8,128)(2,1)S(1)}, u32[]{:S(2)}, u32[]{:S(2)}) collective-permute-start(bf16[64,1024]{1,0:T(8,128)(2,1)S(1)} %get-tuple-element.115), channel_id=1, source_target_pairs={{0,8},{6,14},{9,1},{15,7},{16,24},{22,30},{25,17},{31,23}} | collective-permute-start | bytes 393224 | tf_op jit(solution)/shard_map/stream_home/ppermute | solution.py:563
  76.7 7.1 %collective-permute-start.20 = (bf16[64,1024]{1,0:T(8,128)(2,1)S(1)}, bf16[64,1024]{1,0:T(8,128)(2,1)S(1)}, u32[]{:S(2)}, u32[]{:S(2)}) collective-permute-start(bf16[64,1024]{1,0:T(8,128)(2,1)S(1)} %get-tuple-element.117), channel_id=1, source_target_pairs={{0,12},{6,10},{9,5},{15,3},{16,28},{22,26},{25,21},{31,19}} | collective-permute-start | bytes 393224 | tf_op jit(solution)/shard_map/stream_home/ppermute | solution.py:563
  79.2 5.4 %collective-permute-start.22 = (bf16[40,1024]{1,0:T(8,128)(2,1)S(1)}, bf16[40,1024]{1,0:T(8,128)(2,1)S(1)}, u32[]{:S(2)}, u32[]{:S(2)}) collective-permute-start(bf16[40,1024]{1,0:T(8,128)(2,1)S(1)} %get-tuple-element.120), channel_id=1, source_target_pairs={{0,4},{1,5},{2,6},{3,7},{4,0},{5,1},{6,2},{7,3},{8,12},{9,13},{10,... | collective-permute-start | bytes 245768 | tf_op jit(solution)/shard_map/reply/ppermute | solution.py:563
  80.9 8.7 %collective-permute-start.23 = (bf16[40,1024]{1,0:T(8,128)(2,1)S(1)}, bf16[40,1024]{1,0:T(8,128)(2,1)S(1)}, u32[]{:S(2)}, u32[]{:S(2)}) collective-permute-start(bf16[40,1024]{1,0:T(8,128)(2,1)S(1)} %get-tuple-element.121), channel_id=1, source_target_pairs={{0,8},{1,9},{2,10},{3,11},{4,12},{5,13},{6,14},{7,15},{8,0},{9,1},... | collective-permute-start | bytes 245768 | tf_op jit(solution)/shard_map/reply/ppermute | solution.py:563
  83.1 6.6 %collective-permute-start.24 = (bf16[40,1024]{1,0:T(8,128)(2,1)S(1)}, bf16[40,1024]{1,0:T(8,128)(2,1)S(1)}, u32[]{:S(2)}, u32[]{:S(2)}) collective-permute-start(bf16[40,1024]{1,0:T(8,128)(2,1)S(1)} %get-tuple-element.122), channel_id=1, source_target_pairs={{0,12},{1,13},{2,14},{3,15},{4,8},{5,9},{6,10},{7,11},{8,4},{9,5},... | collective-permute-start | bytes 245768 | tf_op jit(solution)/shard_map/reply/ppermute | solution.py:563

commit v6 on v5

--- a/solution.py
+++ b/solution.py
@@ -230,7 +230,7 @@
     copy.wait()
 
 
-def correct_kernel(one_ref, two_ref, three_ref, base_ref, weight_ref, rate_ref, out_ref, gated_s):
+def correct_kernel(one_ref, three_ref, two_ref, base_ref, weight_ref, rate_ref, out_ref, gated_s):
     tokens, width = out_ref.shape
     g = width // 128
     states = rate_ref.shape[0] // g
@@ -471,7 +471,7 @@
 
 
 def finish_kernel(
-    s0_ref, s1_ref, s2_ref, s3_ref, pack_ref, weights_ref, r0_ref, r1_ref, r2_ref, r3_ref, out_ref
+    s0_ref, s2_ref, s3_ref, s1_ref, pack_ref, weights_ref, r0_ref, r2_ref, r3_ref, r1_ref, out_ref
 ):
     ctx = lax.axis_index("ctx")
     apart = ctx ^ (lax.axis_index("tp") * lax.axis_size("exp") + lax.axis_index("exp"))
@@ -596,7 +596,7 @@
     with jax.named_scope("correct"):
         gated = call(
             correct_kernel, shape(tokens, channels, bf16), [VM] * 6, [pltpu.VMEM((tokens * g, 128), f32)],
-            (*entered, base, spread, rate),
+            (entered[0], entered[2], entered[1], base, spread, rate),
         )
     with jax.named_scope("gather_gated"):
         peer_gated = swap_tp(gated)
@@ -715,7 +715,7 @@
     with jax.named_scope("finish"):
         return call(
             finish_kernel, shape(tokens, piece_width, bf16), [VM] * 10, (),
-            (streams[0], *home, pack, route_weight.T, *replies),
+            (streams[0], home[1], home[2], home[0], pack, route_weight.T, *(replies[p] for p in (0, 2, 3, 1))),
         )
 
 

time: 91.5 us -> 90.2 us (0.986)
  starting transfers between devices: 44.9 us -> 43.1 us
    ppermute x20, starting transfers between devices: 42.4 us -> 40.6 us  [permute(): return lax.ppermute(x, AXES, pairs)]
    ppermute x20, waiting for transfers between devices: 9.5 us -> 11.1 us  [permute(): return lax.ppermute(x, AXES, pairs)]
    ppermute x1, waiting for transfers between devices: 1.12 us -> 0.04 us  [fast_body(): peer = lax.ppermute(theirs, 'exp', [(0, 1), (1, 0)])]
where the time goes in v6:
time: 90.2 us; the launch traced here: 89.5 us
  starting transfers between devices  43.1 us (48%)
  Pallas kernels  33.6 us (37%)
  waiting for transfers between devices  12.5 us (14%)
    ppermute x20, starting transfers between devices, permute(): return lax.ppermute(x, AXES, pairs)  40.6 us
    pallas_call x20, Pallas kernels, call(): pl.pallas_call(body_kernel, out_shape=outs + tuple((pltpu.VMEM(x.shape, x...  33.6 us
    ppermute x20, waiting for transfers between devices, permute(): return lax.ppermute(x, AXES, pairs)  11.1 us
  transfers between devices with their start and end apart: 25, of which 8 were waited for; matrix products, arithmetic and copies ran while one was open for 0% of the time, Pallas kernels for 26%

profile of v6, /device:TPU:0, one launch (start us, length us, event | category | flops | bytes accessed | tf_op | source)
XLA Modules:
  0.0 89.5 jit_solution(5456687735516382977)
XLA Ops:
  0.0 3.3 %scan.1 = (f32[512,128]{1,0:T(8,128)S(1)}, f32[512,128]{1,0:T(8,128)S(1)}, f32[512,128]{1,0:T(8,128)S(1)}, f32[128,128]{1,0:T(8,128)S(1)}, bf16[144,128]{1,0:T(8,128)(2,1)S(1)}) custom-call(f32[16,64]{1,0:T(8,128)} %bitcast.8, f32[16,64]{1,0:T(8,128)} %bitcast.9, f32[64,1024]{1,0:T(8,128)} %refs_2_.3, bf16[64,1024]{1,0:T(8,128)(2,1)} %refs_3_.1, ...), custom_call_target="tpu_custom_call" | custom-call | tf_op jit(solution)/shard_map/scan/pallas_call | solution.py:514
  3.3 0.5 collective-permute-start.5
  3.7 3.6 %collective-permute-start.2 = (bf16[144,128]{1,0:T(8,128)(2,1)S(1)}, bf16[144,128]{1,0:T(8,128)(2,1)S(1)}, u32[]{:S(2)}, u32[]{:S(2)}) collective-permute-start(bf16[144,128]{1,0:T(8,128)(2,1)S(1)} %get-tuple-element.64.refs_2_.refs_4_), channel_id=1, source_target_pairs={{0,8},{1,9},{2,10},{3,11},{4,12},{5,13},{6,14},{7,15},{8,0},{9,1},... | collective-permute-start | bytes 110600 | tf_op jit(solution)/shard_map/relay/ppermute | solution.py:563
  7.4 1.3 %collective-permute-start.1 = (bf16[144,128]{1,0:T(8,128)(2,1)S(1)}, bf16[144,128]{1,0:T(8,128)(2,1)S(1)}, u32[]{:S(2)}, u32[]{:S(2)}) collective-permute-start(bf16[144,128]{1,0:T(8,128)(2,1)S(1)} %get-tuple-element.64.refs_2_.refs_4_), channel_id=1, source_target_pairs={{0,12},{1,13},{2,14},{3,15},{4,8},{5,9},{6,10},{7,11},{8,4},{9,5},... | collective-permute-start | bytes 110600 | tf_op jit(solution)/shard_map/relay/ppermute | solution.py:563
  8.7 0.2 collective-permute-start
  8.9 1.9 %spread.1 = (f32[512,128]{1,0:T(8,128)S(1)}, f32[8192,128]{1,0:T(8,128)S(1)}, bf16[64,4096]{1,0:T(8,128)(2,1)S(1)}) custom-call(f32[16,64]{1,0:T(8,128)} %bitcast.10, f32[512,128]{1,0:T(8,128)S(1)} %get-tuple-element.65.refs_1_, f32[512,128]{1,0:T(8,128)S(1)} %get-tuple-element.66.refs_2_, f32[512,128]{1,0:T(8,128)S(1)} %get-tuple-element.67.refs_3_, ...), custom_call_target="tpu_custom_call" | custom-call | flops 2000000000 | tf_op jit(solution)/shard_map/spread/pallas_call | solution.py:514
  10.9 2.3 %collective-permute-done.1.refs_1_.refs_3_ = bf16[144,128]{1,0:T(8,128)(2,1)S(1)} collective-permute-done((bf16[144,128]{1,0:T(8,128)(2,1)S(1)}, bf16[144,128]{1,0:T(8,128)(2,1)S(1)}, u32[]{:S(2)}, u32[]{:S(2)}) %collective-permute-start.1) | collective-permute-done | bytes 36896 | tf_op jit(solution)/shard_map/relay/ppermute | solution.py:563
  13.2 0.5 correct.1.refs_0_
  13.7 1.3 %collective-permute-done.3.refs_1_ = bf16[64,1024]{1,0:T(8,128)(2,1)S(1)} collective-permute-done((bf16[64,1024]{1,0:T(8,128)(2,1)S(1)}, bf16[64,1024]{1,0:T(8,128)(2,1)S(1)}, u32[]{:S(2)}, u32[]{:S(2)}) %collective-permute-start.3) | collective-permute-done | bytes 131104 | tf_op jit(solution)/shard_map/gather_gated/ppermute | solution.py:572
  15.1 0.1 gather_gated.1
  15.2 2.0 %collective-permute-start.4 = (bf16[64,2560]{1,0:T(8,128)(2,1)S(1)}, bf16[64,2560]{1,0:T(8,128)(2,1)S(1)}, u32[]{:S(2)}, u32[]{:S(2)}) collective-permute-start(bf16[64,2560]{1,0:T(8,128)(2,1)S(1)} %get-tuple-element.73), channel_id=1, source_target_pairs={{4,0},{6,2},{0,4},{2,6},{13,9},{15,11},{9,13},{11,15},{20,16},{22,... | collective-permute-start | bytes 983048 | tf_op jit(solution)/shard_map/gather_gated/ppermute | solution.py:563
  17.2 1.3 %collective-permute-start.7 = (bf16[64,2560]{1,0:T(8,128)(2,1)S(1)}, bf16[64,2560]{1,0:T(8,128)(2,1)S(1)}, u32[]{:S(2)}, u32[]{:S(2)}) collective-permute-start(bf16[64,2560]{1,0:T(8,128)(2,1)S(1)} %get-tuple-element.83), channel_id=1, source_target_pairs={{8,0},{10,2},{12,4},{14,6},{1,9},{3,11},{5,13},{7,15},{24,16},{26,... | collective-permute-start | bytes 983048 | tf_op jit(solution)/shard_map/gather_gated/ppermute | solution.py:563
  18.5 1.3 %collective-permute-start.8 = (bf16[64,2560]{1,0:T(8,128)(2,1)S(1)}, bf16[64,2560]{1,0:T(8,128)(2,1)S(1)}, u32[]{:S(2)}, u32[]{:S(2)}) collective-permute-start(bf16[64,2560]{1,0:T(8,128)(2,1)S(1)} %get-tuple-element.84), channel_id=1, source_target_pairs={{12,0},{14,2},{8,4},{10,6},{5,9},{7,11},{1,13},{3,15},{28,16},{30,... | collective-permute-start | bytes 983048 | tf_op jit(solution)/shard_map/gather_gated/ppermute | solution.py:563
  19.8 2.9 %hold_out_weight.1 = (bf16[2048,1024]{1,0:T(8,128)(2,1)S(1)}, bf16[4096,2048]{1,0:T(8,128)(2,1)S(1)}) custom-call(bf16[1024,1024]{1,0:T(8,128)(2,1)} %refs_0_.3, bf16[1024,1024]{1,0:T(8,128)(2,1)S(1)} %collective-permute-done.5.refs_1_, bf16[2048,4096]{1,0:T(8,128)(2,1)} %refs_0_.5, bf16[64,2560]{1,0:T(8,128)(2,1)S(1)} %get-tuple-element.72.refs_3_.refs_0_), custom_call_target="tpu_custom_call" | custom-call | tf_op jit(solution)/shard_map/hold_out_weight/pallas_call | solution.py:514
  22.7 2.8 %collective-permute-done.4.refs_1_ = bf16[64,2560]{1,0:T(8,128)(2,1)S(1)} collective-permute-done((bf16[64,2560]{1,0:T(8,128)(2,1)S(1)}, bf16[64,2560]{1,0:T(8,128)(2,1)S(1)}, u32[]{:S(2)}, u32[]{:S(2)}) %collective-permute-start.4) | collective-permute-done | bytes 327712 | tf_op jit(solution)/shard_map/gather_gated/ppermute | solution.py:563
  25.5 0.8 project.2
  26.3 3.4 %collective-permute-start.6 = (bf16[128,1024]{1,0:T(8,128)(2,1)S(1)}, bf16[128,1024]{1,0:T(8,128)(2,1)S(1)}, u32[]{:S(2)}, u32[]{:S(2)}) collective-permute-start(bf16[128,1024]{1,0:T(8,128)(2,1)S(1)} %get-tuple-element.77.refs_2_.refs_0_), channel_id=1, source_target_pairs={{0,2},{2,0},{4,6},{6,4},{9,11},{11,9},{13,15},{15,13},{16,18},{18,... | collective-permute-start | bytes 786440 | tf_op jit(solution)/shard_map/sum_exp/ppermute | solution.py:563
  29.7 4.7 %hold_weights.2 = (f32[8,128]{1,0:T(8,128)S(1)}, bf16[4096,2048]{1,0:T(8,128)(2,1)S(1)}) custom-call(bf16[2048,4096]{1,0:T(8,128)(2,1)} %refs_0_.5, bf16[2048,4096]{1,0:T(8,128)(2,1)} %refs_9_.1, bf16[128,1024]{1,0:T(8,128)(2,1)S(1)} %get-tuple-element.77.refs_2_.refs_0_, ...), custom_call_target="tpu_custom_call", output_to_operand_aliasing={{1}: (3, {})} | custom-call | flops 3000000000 | tf_op jit(solution)/shard_map/hold_weights/pallas_call | solution.py:514
  34.4 0.2 collective-permute-done.6.refs_1_
  34.6 0.4 select.2
  35.0 1.3 %collective-permute-start.10 = (bf16[80,1024]{1,0:T(8,128)(2,1)S(1)}, bf16[80,1024]{1,0:T(8,128)(2,1)S(1)}, u32[]{:S(2)}, u32[]{:S(2)}) collective-permute-start(bf16[80,1024]{1,0:T(8,128)(2,1)S(1)} %get-tuple-element.91), channel_id=1, source_target_pairs={{0,8},{2,10},{4,12},{6,14},{9,1},{11,3},{13,5},{15,7},{16,24},{18,... | collective-permute-start | bytes 491528 | tf_op jit(solution)/shard_map/dispatch/ppermute | solution.py:563
  36.3 0.8 project.3
  37.2 3.4 %collective-permute-start.9 = (bf16[128,1024]{1,0:T(8,128)(2,1)S(1)}, bf16[128,1024]{1,0:T(8,128)(2,1)S(1)}, u32[]{:S(2)}, u32[]{:S(2)}) collective-permute-start(bf16[128,1024]{1,0:T(8,128)(2,1)S(1)} %get-tuple-element.88.refs_0_), channel_id=1, source_target_pairs={{0,2},{2,0},{4,6},{6,4},{9,11},{11,9},{13,15},{15,13},{16,18},{18,... | collective-permute-start | bytes 786440 | tf_op jit(solution)/shard_map/sum_exp/ppermute | solution.py:563
  40.6 1.3 %collective-permute-start.11 = (bf16[80,1024]{1,0:T(8,128)(2,1)S(1)}, bf16[80,1024]{1,0:T(8,128)(2,1)S(1)}, u32[]{:S(2)}, u32[]{:S(2)}) collective-permute-start(bf16[80,1024]{1,0:T(8,128)(2,1)S(1)} %get-tuple-element.92), channel_id=1, source_target_pairs={{0,12},{2,14},{4,8},{6,10},{9,5},{11,7},{13,1},{15,3},{16,28},{18,... | collective-permute-start | bytes 491528 | tf_op jit(solution)/shard_map/dispatch/ppermute | solution.py:563
  41.9 3.8 %collective-permute-start.12 = (bf16[80,1024]{1,0:T(8,128)(2,1)S(1)}, bf16[80,1024]{1,0:T(8,128)(2,1)S(1)}, u32[]{:S(2)}, u32[]{:S(2)}) collective-permute-start(bf16[80,1024]{1,0:T(8,128)(2,1)S(1)} %get-tuple-element.93), channel_id=1, source_target_pairs={{0,4},{2,6},{4,0},{6,2},{9,13},{11,15},{13,9},{15,11},{16,20},{18,... | collective-permute-start | bytes 491528 | tf_op jit(solution)/shard_map/dispatch/ppermute | solution.py:563
  45.7 0.4 select.3
  46.1 1.3 %collective-permute-start.13 = (bf16[80,1024]{1,0:T(8,128)(2,1)S(1)}, bf16[80,1024]{1,0:T(8,128)(2,1)S(1)}, u32[]{:S(2)}, u32[]{:S(2)}) collective-permute-start(bf16[80,1024]{1,0:T(8,128)(2,1)S(1)} %get-tuple-element.95), channel_id=1, source_target_pairs={{0,8},{2,10},{4,12},{6,14},{9,1},{11,3},{13,5},{15,7},{16,24},{18,... | collective-permute-start | bytes 491528 | tf_op jit(solution)/shard_map/dispatch/ppermute | solution.py:563
  47.4 1.3 %collective-permute-start.14 = (bf16[80,1024]{1,0:T(8,128)(2,1)S(1)}, bf16[80,1024]{1,0:T(8,128)(2,1)S(1)}, u32[]{:S(2)}, u32[]{:S(2)}) collective-permute-start(bf16[80,1024]{1,0:T(8,128)(2,1)S(1)} %get-tuple-element.96), channel_id=1, source_target_pairs={{0,12},{2,14},{4,8},{6,10},{9,5},{11,7},{13,1},{15,3},{16,28},{18,... | collective-permute-start | bytes 491528 | tf_op jit(solution)/shard_map/dispatch/ppermute | solution.py:563
  48.8 3.5 %collective-permute-start.15 = (bf16[80,1024]{1,0:T(8,128)(2,1)S(1)}, bf16[80,1024]{1,0:T(8,128)(2,1)S(1)}, u32[]{:S(2)}, u32[]{:S(2)}) collective-permute-start(bf16[80,1024]{1,0:T(8,128)(2,1)S(1)} %get-tuple-element.97), channel_id=1, source_target_pairs={{0,4},{2,6},{4,0},{6,2},{9,13},{11,15},{13,9},{15,11},{16,20},{18,... | collective-permute-start | bytes 491528 | tf_op jit(solution)/shard_map/dispatch/ppermute | solution.py:563
  52.3 3.4 %hold_weights.3 = (bf16[4096,2048]{1,0:T(8,128)(2,1)S(1)}, bf16[4096,2048]{1,0:T(8,128)(2,1)S(1)}) custom-call(bf16[2048,4096]{1,0:T(8,128)(2,1)} %refs_0_.5, bf16[80,1024]{1,0:T(8,128)(2,1)S(1)} %get-tuple-element.94.refs_1_.refs_4_, bf16[4096,2048]{1,0:T(8,128)(2,1)S(1)} %get-tuple-element.98.refs_2_), custom_call_target="tpu_custom_call", output_to_operand_aliasing={{1}: (2, {})} | custom-call | flops 3000000000 | tf_op jit(solution)/shard_map/hold_weights/pallas_call | solution.py:514
  55.7 0.2 collective-permute-done.15.refs_7_
  56.0 4.1 %gate_up.2 = (bf16[160,4224]{1,0:T(8,128)(2,1)S(1)}, bf16[160,2048]{1,0:T(8,128)(2,1)S(1)}, bf16[4096,2048]{1,0:T(8,128)(2,1)S(1)}, bf16[4096,2048]{1,0:T(8,128)(2,1)S(1)}) custom-call(bf16[80,1024]{1,0:T(8,128)(2,1)S(1)} %get-tuple-element.85.refs_0_, ...), custom_call_target="tpu_custom_call", output_to_operand_aliasing={{2}: (10, {}), {3}: (11, {})} | custom-call | tf_op jit(solution)/shard_map/gate_up/pallas_call | solution.py:514
  60.2 3.4 %gate_up.3 = (bf16[160,4096]{1,0:T(8,128)(2,1)S(1)}, bf16[4096,2048]{1,0:T(8,128)(2,1)S(1)}, bf16[4096,2048]{1,0:T(8,128)(2,1)S(1)}) custom-call(bf16[160,2048]{1,0:T(8,128)(2,1)S(1)} %get-tuple-element.101.refs_0_, bf16[4096,2048]{1,0:T(8,128)(2,1)} %refs_2_.5, ...), custom_call_target="tpu_custom_call", output_to_operand_aliasing={{1}: (2, {}), {2}: (3, {})} | custom-call | tf_op jit(solution)/shard_map/gate_up/pallas_call | solution.py:514
  63.6 0.6 collective-permute-start.16
  64.1 3.4 %down.2 = (f32[160,2048]{1,0:T(8,128)S(1)}, f32[160,128]{1,0:T(8,128)S(1)}, bf16[4096,2048]{1,0:T(8,128)(2,1)S(1)}) custom-call(bf16[160,4224]{1,0:T(8,128)(2,1)S(1)} %get-tuple-element.105.refs_0_, bf16[160,4224]{1,0:T(8,128)(2,1)S(1)} %collective-permute-done.17.refs_1_, bf16[4096,2048]{1,0:T(8,128)(2,1)} %refs_2_.5, ...), custom_call_target="tpu_custom_call", output_to_operand_aliasing={{2}: (3, {})} | custom-call | tf_op jit(solution)/shard_map/down/pallas_call | solution.py:514
  67.6 1.3 %down.3 = (bf16[160,1024]{1,0:T(8,128)(2,1)S(1)}, bf16[160,2048]{1,0:T(8,128)(2,1)S(1)}, bf16[4096,2048]{1,0:T(8,128)(2,1)S(1)}) custom-call(bf16[160,4096]{1,0:T(8,128)(2,1)S(1)} %get-tuple-element.104.refs_0_, bf16[160,4096]{1,0:T(8,128)(2,1)S(1)} %collective-permute-done.16.refs_1_, ...), custom_call_target="tpu_custom_call", output_to_operand_aliasing={{2}: (4, {})} | custom-call | tf_op jit(solution)/shard_map/down/pallas_call | solution.py:514
  68.9 1.3 %collective-permute-start.21 = (bf16[160,1024]{1,0:T(8,128)(2,1)S(1)}, bf16[160,1024]{1,0:T(8,128)(2,1)S(1)}, u32[]{:S(2)}, u32[]{:S(2)}) collective-permute-start(bf16[160,1024]{1,0:T(8,128)(2,1)S(1)} %get-tuple-element.118), channel_id=1, source_target_pairs={{0,2},{2,0},{1,3},{3,1},{4,6},{6,4},{5,7},{7,5},{8,10},{10,8},{9,1... | collective-permute-start | bytes 983048 | tf_op jit(solution)/shard_map/sum_experts/ppermute | solution.py:693
  70.3 0.9 sum_experts.1
  71.1 4.8 %collective-permute-start.18 = (bf16[64,1024]{1,0:T(8,128)(2,1)S(1)}, bf16[64,1024]{1,0:T(8,128)(2,1)S(1)}, u32[]{:S(2)}, u32[]{:S(2)}) collective-permute-start(bf16[64,1024]{1,0:T(8,128)(2,1)S(1)} %get-tuple-element.113), channel_id=1, source_target_pairs={{0,8},{6,14},{9,1},{15,7},{16,24},{22,30},{25,17},{31,23}} | collective-permute-start | bytes 393224 | tf_op jit(solution)/shard_map/stream_home/ppermute | solution.py:563
  76.0 1.3 %collective-permute-start.19 = (bf16[64,1024]{1,0:T(8,128)(2,1)S(1)}, bf16[64,1024]{1,0:T(8,128)(2,1)S(1)}, u32[]{:S(2)}, u32[]{:S(2)}) collective-permute-start(bf16[64,1024]{1,0:T(8,128)(2,1)S(1)} %get-tuple-element.115), channel_id=1, source_target_pairs={{0,12},{6,10},{9,5},{15,3},{16,28},{22,26},{25,21},{31,19}} | collective-permute-start | bytes 393224 | tf_op jit(solution)/shard_map/stream_home/ppermute | solution.py:563
  77.3 1.3 %collective-permute-start.20 = (bf16[64,1024]{1,0:T(8,128)(2,1)S(1)}, bf16[64,1024]{1,0:T(8,128)(2,1)S(1)}, u32[]{:S(2)}, u32[]{:S(2)}) collective-permute-start(bf16[64,1024]{1,0:T(8,128)(2,1)S(1)} %get-tuple-element.117), channel_id=1, source_target_pairs={{0,4},{6,2},{9,13},{15,11},{16,20},{22,18},{25,29},{31,27}} | collective-permute-start | bytes 393224 | tf_op jit(solution)/shard_map/stream_home/ppermute | solution.py:563
  78.6 0.1 reply.1
  78.8 3.1 %collective-permute-start.22 = (bf16[40,1024]{1,0:T(8,128)(2,1)S(1)}, bf16[40,1024]{1,0:T(8,128)(2,1)S(1)}, u32[]{:S(2)}, u32[]{:S(2)}) collective-permute-start(bf16[40,1024]{1,0:T(8,128)(2,1)S(1)} %get-tuple-element.120), channel_id=1, source_target_pairs={{0,8},{1,9},{2,10},{3,11},{4,12},{5,13},{6,14},{7,15},{8,0},{9,1},... | collective-permute-start | bytes 245768 | tf_op jit(solution)/shard_map/reply/ppermute | solution.py:563
  81.8 1.0 %collective-permute-start.23 = (bf16[40,1024]{1,0:T(8,128)(2,1)S(1)}, bf16[40,1024]{1,0:T(8,128)(2,1)S(1)}, u32[]{:S(2)}, u32[]{:S(2)}) collective-permute-start(bf16[40,1024]{1,0:T(8,128)(2,1)S(1)} %get-tuple-element.121), channel_id=1, source_target_pairs={{0,12},{1,13},{2,14},{3,15},{4,8},{5,9},{6,10},{7,11},{8,4},{9,5},... | collective-permute-start | bytes 245768 | tf_op jit(solution)/shard_map/reply/ppermute | solution.py:563
  82.8 4.1 %collective-permute-done.22.refs_7_ = bf16[40,1024]{1,0:T(8,128)(2,1)S(1)} collective-permute-done((bf16[40,1024]{1,0:T(8,128)(2,1)S(1)}, bf16[40,1024]{1,0:T(8,128)(2,1)S(1)}, u32[]{:S(2)}, u32[]{:S(2)}) %collective-permute-start.22) | collective-permute-done | bytes 81952 | tf_op jit(solution)/shard_map/reply/ppermute | solution.py:563
  86.9 1.3 %collective-permute-done.23.refs_8_ = bf16[40,1024]{1,0:T(8,128)(2,1)S(1)} collective-permute-done((bf16[40,1024]{1,0:T(8,128)(2,1)S(1)}, bf16[40,1024]{1,0:T(8,128)(2,1)S(1)}, u32[]{:S(2)}, u32[]{:S(2)}) %collective-permute-start.23) | collective-permute-done | bytes 81952 | tf_op jit(solution)/shard_map/reply/ppermute | solution.py:563
  88.2 0.2 collective-permute-done.24.refs_9_
  88.4 1.1 %finish.1 = bf16[64,1024]{1,0:T(8,128)(2,1)} custom-call(bf16[64,1024]{1,0:T(8,128)(2,1)S(1)} %get-tuple-element.82.refs_0_, bf16[64,1024]{1,0:T(8,128)(2,1)S(1)} %collective-permute-done.18.refs_1_, bf16[64,1024]{1,0:T(8,128)(2,1)S(1)} %collective-permute-done.19.refs_2_, bf16[64,1024]{1,0:T(8,128)(2,1)S(1)} %collective-permute-done.20.refs_3_, ...), custom_call_target="tpu_custom_call" | custom-call | tf_op jit(solution)/shard_map/finish/pallas_call | solution.py:514
  (24 shorter events, 0.2 us)
Async XLA Ops:
  3.3 16.5 %collective-permute-start.5 = (bf16[1024,1024]{1,0:T(8,128)(2,1)}, bf16[1024,1024]{1,0:T(8,128)(2,1)S(1)}, u32[]{:S(2)}, u32[]{:S(2)}) collective-permute-start(bf16[1024,1024]{1,0:T(8,128)(2,1)} %refs_0_.3), channel_id=1, source_target_pairs={{0,1},{1,0},{2,3},{3,2},{4,5},{5,4},{6,7},{7,6},{8,9},{9,8},{10,11... | collective-permute-start | bytes 6291464 | tf_op jit(solution)/shard_map/ppermute | solution.py:572
  3.7 7.2 %collective-permute-start.2 = (bf16[144,128]{1,0:T(8,128)(2,1)S(1)}, bf16[144,128]{1,0:T(8,128)(2,1)S(1)}, u32[]{:S(2)}, u32[]{:S(2)}) collective-permute-start(bf16[144,128]{1,0:T(8,128)(2,1)S(1)} %get-tuple-element.64.refs_2_.refs_4_), channel_id=1, source_target_pairs={{0,8},{1,9},{2,10},{3,11},{4,12},{5,13},{6,14},{7,15},{8,0},{9,1},... | collective-permute-start | bytes 110600 | tf_op jit(solution)/shard_map/relay/ppermute | solution.py:563
  7.4 5.8 %collective-permute-start.1 = (bf16[144,128]{1,0:T(8,128)(2,1)S(1)}, bf16[144,128]{1,0:T(8,128)(2,1)S(1)}, u32[]{:S(2)}, u32[]{:S(2)}) collective-permute-start(bf16[144,128]{1,0:T(8,128)(2,1)S(1)} %get-tuple-element.64.refs_2_.refs_4_), channel_id=1, source_target_pairs={{0,12},{1,13},{2,14},{3,15},{4,8},{5,9},{6,10},{7,11},{8,4},{9,5},... | collective-permute-start | bytes 110600 | tf_op jit(solution)/shard_map/relay/ppermute | solution.py:563
  8.7 4.4 %collective-permute-start = (bf16[144,128]{1,0:T(8,128)(2,1)S(1)}, bf16[144,128]{1,0:T(8,128)(2,1)S(1)}, u32[]{:S(2)}, u32[]{:S(2)}) collective-permute-start(bf16[144,128]{1,0:T(8,128)(2,1)S(1)} %get-tuple-element.64.refs_2_.refs_4_), channel_id=1, source_target_pairs={{0,4},{1,5},{2,6},{3,7},{4,0},{5,1},{6,2},{7,3},{8,12},{9,13},{10,... | collective-permute-start | bytes 110600 | tf_op jit(solution)/shard_map/relay/ppermute | solution.py:563
  13.7 1.4 %collective-permute-start.3 = (bf16[64,1024]{1,0:T(8,128)(2,1)S(1)}, bf16[64,1024]{1,0:T(8,128)(2,1)S(1)}, u32[]{:S(2)}, u32[]{:S(2)}) collective-permute-start(bf16[64,1024]{1,0:T(8,128)(2,1)S(1)} %correct.1.refs_0_), channel_id=1, source_target_pairs={{0,1},{1,0},{2,3},{3,2},{4,5},{5,4},{6,7},{7,6},{8,9},{9,8},{10,11... | collective-permute-start | bytes 393224 | tf_op jit(solution)/shard_map/gather_gated/ppermute | solution.py:572
  15.2 10.3 %collective-permute-start.4 = (bf16[64,2560]{1,0:T(8,128)(2,1)S(1)}, bf16[64,2560]{1,0:T(8,128)(2,1)S(1)}, u32[]{:S(2)}, u32[]{:S(2)}) collective-permute-start(bf16[64,2560]{1,0:T(8,128)(2,1)S(1)} %get-tuple-element.73), channel_id=1, source_target_pairs={{4,0},{6,2},{0,4},{2,6},{13,9},{15,11},{9,13},{11,15},{20,16},{22,... | collective-permute-start | bytes 983048 | tf_op jit(solution)/shard_map/gather_gated/ppermute | solution.py:563
  17.2 19.1 %collective-permute-start.7 = (bf16[64,2560]{1,0:T(8,128)(2,1)S(1)}, bf16[64,2560]{1,0:T(8,128)(2,1)S(1)}, u32[]{:S(2)}, u32[]{:S(2)}) collective-permute-start(bf16[64,2560]{1,0:T(8,128)(2,1)S(1)} %get-tuple-element.83), channel_id=1, source_target_pairs={{8,0},{10,2},{12,4},{14,6},{1,9},{3,11},{5,13},{7,15},{24,16},{26,... | collective-permute-start | bytes 983048 | tf_op jit(solution)/shard_map/gather_gated/ppermute | solution.py:563
  18.5 17.8 %collective-permute-start.8 = (bf16[64,2560]{1,0:T(8,128)(2,1)S(1)}, bf16[64,2560]{1,0:T(8,128)(2,1)S(1)}, u32[]{:S(2)}, u32[]{:S(2)}) collective-permute-start(bf16[64,2560]{1,0:T(8,128)(2,1)S(1)} %get-tuple-element.84), channel_id=1, source_target_pairs={{12,0},{14,2},{8,4},{10,6},{5,9},{7,11},{1,13},{3,15},{28,16},{30,... | collective-permute-start | bytes 983048 | tf_op jit(solution)/shard_map/gather_gated/ppermute | solution.py:563
  26.3 8.3 %collective-permute-start.6 = (bf16[128,1024]{1,0:T(8,128)(2,1)S(1)}, bf16[128,1024]{1,0:T(8,128)(2,1)S(1)}, u32[]{:S(2)}, u32[]{:S(2)}) collective-permute-start(bf16[128,1024]{1,0:T(8,128)(2,1)S(1)} %get-tuple-element.77.refs_2_.refs_0_), channel_id=1, source_target_pairs={{0,2},{2,0},{4,6},{6,4},{9,11},{11,9},{13,15},{15,13},{16,18},{18,... | collective-permute-start | bytes 786440 | tf_op jit(solution)/shard_map/sum_exp/ppermute | solution.py:563
  35.0 13.7 %collective-permute-start.10 = (bf16[80,1024]{1,0:T(8,128)(2,1)S(1)}, bf16[80,1024]{1,0:T(8,128)(2,1)S(1)}, u32[]{:S(2)}, u32[]{:S(2)}) collective-permute-start(bf16[80,1024]{1,0:T(8,128)(2,1)S(1)} %get-tuple-element.91), channel_id=1, source_target_pairs={{0,8},{2,10},{4,12},{6,14},{9,1},{11,3},{13,5},{15,7},{16,24},{18,... | collective-permute-start | bytes 491528 | tf_op jit(solution)/shard_map/dispatch/ppermute | solution.py:563
  37.2 8.5 %collective-permute-start.9 = (bf16[128,1024]{1,0:T(8,128)(2,1)S(1)}, bf16[128,1024]{1,0:T(8,128)(2,1)S(1)}, u32[]{:S(2)}, u32[]{:S(2)}) collective-permute-start(bf16[128,1024]{1,0:T(8,128)(2,1)S(1)} %get-tuple-element.88.refs_0_), channel_id=1, source_target_pairs={{0,2},{2,0},{4,6},{6,4},{9,11},{11,9},{13,15},{15,13},{16,18},{18,... | collective-permute-start | bytes 786440 | tf_op jit(solution)/shard_map/sum_exp/ppermute | solution.py:563
  40.6 15.1 %collective-permute-start.11 = (bf16[80,1024]{1,0:T(8,128)(2,1)S(1)}, bf16[80,1024]{1,0:T(8,128)(2,1)S(1)}, u32[]{:S(2)}, u32[]{:S(2)}) collective-permute-start(bf16[80,1024]{1,0:T(8,128)(2,1)S(1)} %get-tuple-element.92), channel_id=1, source_target_pairs={{0,12},{2,14},{4,8},{6,10},{9,5},{11,7},{13,1},{15,3},{16,28},{18,... | collective-permute-start | bytes 491528 | tf_op jit(solution)/shard_map/dispatch/ppermute | solution.py:563
  41.9 13.8 %collective-permute-start.12 = (bf16[80,1024]{1,0:T(8,128)(2,1)S(1)}, bf16[80,1024]{1,0:T(8,128)(2,1)S(1)}, u32[]{:S(2)}, u32[]{:S(2)}) collective-permute-start(bf16[80,1024]{1,0:T(8,128)(2,1)S(1)} %get-tuple-element.93), channel_id=1, source_target_pairs={{0,4},{2,6},{4,0},{6,2},{9,13},{11,15},{13,9},{15,11},{16,20},{18,... | collective-permute-start | bytes 491528 | tf_op jit(solution)/shard_map/dispatch/ppermute | solution.py:563
  46.1 9.6 %collective-permute-start.13 = (bf16[80,1024]{1,0:T(8,128)(2,1)S(1)}, bf16[80,1024]{1,0:T(8,128)(2,1)S(1)}, u32[]{:S(2)}, u32[]{:S(2)}) collective-permute-start(bf16[80,1024]{1,0:T(8,128)(2,1)S(1)} %get-tuple-element.95), channel_id=1, source_target_pairs={{0,8},{2,10},{4,12},{6,14},{9,1},{11,3},{13,5},{15,7},{16,24},{18,... | collective-permute-start | bytes 491528 | tf_op jit(solution)/shard_map/dispatch/ppermute | solution.py:563
  47.4 8.3 %collective-permute-start.14 = (bf16[80,1024]{1,0:T(8,128)(2,1)S(1)}, bf16[80,1024]{1,0:T(8,128)(2,1)S(1)}, u32[]{:S(2)}, u32[]{:S(2)}) collective-permute-start(bf16[80,1024]{1,0:T(8,128)(2,1)S(1)} %get-tuple-element.96), channel_id=1, source_target_pairs={{0,12},{2,14},{4,8},{6,10},{9,5},{11,7},{13,1},{15,3},{16,28},{18,... | collective-permute-start | bytes 491528 | tf_op jit(solution)/shard_map/dispatch/ppermute | solution.py:563
  48.8 7.2 %collective-permute-start.15 = (bf16[80,1024]{1,0:T(8,128)(2,1)S(1)}, bf16[80,1024]{1,0:T(8,128)(2,1)S(1)}, u32[]{:S(2)}, u32[]{:S(2)}) collective-permute-start(bf16[80,1024]{1,0:T(8,128)(2,1)S(1)} %get-tuple-element.97), channel_id=1, source_target_pairs={{0,4},{2,6},{4,0},{6,2},{9,13},{11,15},{13,9},{15,11},{16,20},{18,... | collective-permute-start | bytes 491528 | tf_op jit(solution)/shard_map/dispatch/ppermute | solution.py:563
  60.1 4.0 %collective-permute-start.17 = (bf16[160,4224]{1,0:T(8,128)(2,1)S(1)}, bf16[160,4224]{1,0:T(8,128)(2,1)S(1)}, u32[]{:S(2)}, u32[]{:S(2)}) collective-permute-start(bf16[160,4224]{1,0:T(8,128)(2,1)S(1)} %get-tuple-element.105.refs_0_), channel_id=1, source_target_pairs={{0,1},{1,0},{2,3},{3,2},{4,5},{5,4},{6,7},{7,6},{8,9},{9,8},{10,11... | collective-permute-start | bytes 4055048 | tf_op jit(solution)/shard_map/gate_up/ppermute | solution.py:572
  63.6 4.0 %collective-permute-start.16 = (bf16[160,4096]{1,0:T(8,128)(2,1)S(1)}, bf16[160,4096]{1,0:T(8,128)(2,1)S(1)}, u32[]{:S(2)}, u32[]{:S(2)}) collective-permute-start(bf16[160,4096]{1,0:T(8,128)(2,1)S(1)} %get-tuple-element.104.refs_0_), channel_id=1, source_target_pairs={{0,1},{1,0},{2,3},{3,2},{4,5},{5,4},{6,7},{7,6},{8,9},{9,8},{10,11... | collective-permute-start | bytes 3932168 | tf_op jit(solution)/shard_map/gate_up/ppermute | solution.py:572
  67.6 20.8 %copy-start = (f32[64,2]{0,1:T(2,128)S(1)}, f32[64,2]{0,1:T(2,128)}, u32[]{:S(2)}) copy-start(f32[64,2]{0,1:T(2,128)} %param.26) | copy-start | bytes 1540
  68.9 9.7 %collective-permute-start.21 = (bf16[160,1024]{1,0:T(8,128)(2,1)S(1)}, bf16[160,1024]{1,0:T(8,128)(2,1)S(1)}, u32[]{:S(2)}, u32[]{:S(2)}) collective-permute-start(bf16[160,1024]{1,0:T(8,128)(2,1)S(1)} %get-tuple-element.118), channel_id=1, source_target_pairs={{0,2},{2,0},{1,3},{3,1},{4,6},{6,4},{5,7},{7,5},{8,10},{10,8},{9,1... | collective-permute-start | bytes 983048 | tf_op jit(solution)/shard_map/sum_experts/ppermute | solution.py:693
  71.1 11.7 %collective-permute-start.18 = (bf16[64,1024]{1,0:T(8,128)(2,1)S(1)}, bf16[64,1024]{1,0:T(8,128)(2,1)S(1)}, u32[]{:S(2)}, u32[]{:S(2)}) collective-permute-start(bf16[64,1024]{1,0:T(8,128)(2,1)S(1)} %get-tuple-element.113), channel_id=1, source_target_pairs={{0,8},{6,14},{9,1},{15,7},{16,24},{22,30},{25,17},{31,23}} | collective-permute-start | bytes 393224 | tf_op jit(solution)/shard_map/stream_home/ppermute | solution.py:563
  76.0 6.8 %collective-permute-start.19 = (bf16[64,1024]{1,0:T(8,128)(2,1)S(1)}, bf16[64,1024]{1,0:T(8,128)(2,1)S(1)}, u32[]{:S(2)}, u32[]{:S(2)}) collective-permute-start(bf16[64,1024]{1,0:T(8,128)(2,1)S(1)} %get-tuple-element.115), channel_id=1, source_target_pairs={{0,12},{6,10},{9,5},{15,3},{16,28},{22,26},{25,21},{31,19}} | collective-permute-start | bytes 393224 | tf_op jit(solution)/shard_map/stream_home/ppermute | solution.py:563
  77.3 5.5 %collective-permute-start.20 = (bf16[64,1024]{1,0:T(8,128)(2,1)S(1)}, bf16[64,1024]{1,0:T(8,128)(2,1)S(1)}, u32[]{:S(2)}, u32[]{:S(2)}) collective-permute-start(bf16[64,1024]{1,0:T(8,128)(2,1)S(1)} %get-tuple-element.117), channel_id=1, source_target_pairs={{0,4},{6,2},{9,13},{15,11},{16,20},{22,18},{25,29},{31,27}} | collective-permute-start | bytes 393224 | tf_op jit(solution)/shard_map/stream_home/ppermute | solution.py:563
  78.8 8.1 %collective-permute-start.22 = (bf16[40,1024]{1,0:T(8,128)(2,1)S(1)}, bf16[40,1024]{1,0:T(8,128)(2,1)S(1)}, u32[]{:S(2)}, u32[]{:S(2)}) collective-permute-start(bf16[40,1024]{1,0:T(8,128)(2,1)S(1)} %get-tuple-element.120), channel_id=1, source_target_pairs={{0,8},{1,9},{2,10},{3,11},{4,12},{5,13},{6,14},{7,15},{8,0},{9,1},... | collective-permute-start | bytes 245768 | tf_op jit(solution)/shard_map/reply/ppermute | solution.py:563
  81.8 6.4 %collective-permute-start.23 = (bf16[40,1024]{1,0:T(8,128)(2,1)S(1)}, bf16[40,1024]{1,0:T(8,128)(2,1)S(1)}, u32[]{:S(2)}, u32[]{:S(2)}) collective-permute-start(bf16[40,1024]{1,0:T(8,128)(2,1)S(1)} %get-tuple-element.121), channel_id=1, source_target_pairs={{0,12},{1,13},{2,14},{3,15},{4,8},{5,9},{6,10},{7,11},{8,4},{9,5},... | collective-permute-start | bytes 245768 | tf_op jit(solution)/shard_map/reply/ppermute | solution.py:563
  82.8 5.6 %collective-permute-start.24 = (bf16[40,1024]{1,0:T(8,128)(2,1)S(1)}, bf16[40,1024]{1,0:T(8,128)(2,1)S(1)}, u32[]{:S(2)}, u32[]{:S(2)}) collective-permute-start(bf16[40,1024]{1,0:T(8,128)(2,1)S(1)} %get-tuple-element.122), channel_id=1, source_target_pairs={{0,4},{1,5},{2,6},{3,7},{4,0},{5,1},{6,2},{7,3},{8,12},{9,13},{10,... | collective-permute-start | bytes 245768 | tf_op jit(solution)/shard_map/reply/ppermute | solution.py:563
